TPU v7x, 32 devices: a whole 2x2x4 slice. The times are simulated.
32 devices in a mesh: read: 32 (over z, y, x, core), pos: 1.
Axes of the slice: x: 2, y: 2, z: 4, core: 2. Of those that a mesh axis runs over, the one named last changes fastest.
Arguments:
- features: bfloat16 [128, 32, 768], P('read', 'pos'), may hold values from -6 to 6
- grad_out: bfloat16 [128, 32, 768], P('read', 'pos'), may hold values from -16 to 16
- weights: bfloat16 [4, 768, 768], replicated, may hold values from -0.21875 to 0.21875
- read_start: int32 [128], replicated, may hold values from 0 to 15
- read_end: int32 [128], replicated, may hold values from 17 to 32
Outputs:
- grad_input: bfloat16 [128, 32, 768], P('read', 'pos')
- weight_grads: float32 [768, 3072], P(('read', 'pos'))
Inputs may be any that keep to these rules, and one draw needn't show every extreme that they name: read_end is above read_start for every read.
All inputs are finite; a program needn't handle non-finite values.
Results may differ from a plain program's by a relative error of at most 0.0086.
Values may be sent and summed in bfloat16 or wider, within the bound.
No kernel may reach another device: no remote copies, remote signals or barrier semaphores. Data moves between devices by JAX's collectives and lax.ppermute only.
A program may use at most 128 MiB of HBM per device.

v0:
```python
import math

import jax
import jax.numpy as jnp
from jax import lax
from jax.sharding import PartitionSpec as P

HEADS = 12
HEAD_DIM = 64


def coverage(starts, ends, first_col, col_count):
    columns = first_col + jnp.arange(col_count, dtype=jnp.int32)
    inside = (columns[None, :] >= starts[:, None]) & (columns[None, :] < ends[:, None])
    return inside.astype(jnp.float32)


def dot_back(left, right):
    return lax.dot_general(
        left, right, (((1,), (1,)), ((), ())), preferred_element_type=jnp.float32
    )


def project(source, upstream, covered, weights):
    width = source.shape[-1]
    values32 = source.reshape(-1, width).astype(jnp.float32)
    inverse = lax.rsqrt(jnp.mean(values32 * values32, -1, keepdims=True) + 1e-05)
    normed = values32 * inverse
    normed_b = normed.astype(jnp.bfloat16)
    query = (jnp.dot(normed_b, weights[0], preferred_element_type=jnp.float32) * covered).astype(
        jnp.bfloat16
    )
    keys = (jnp.dot(normed_b, weights[1], preferred_element_type=jnp.float32) * covered).astype(
        jnp.bfloat16
    )
    values = (jnp.dot(normed_b, weights[2], preferred_element_type=jnp.float32) * covered).astype(
        jnp.bfloat16
    )
    grad_flat = upstream.reshape(-1, width)
    back_out = dot_back(grad_flat, weights[3]).astype(jnp.bfloat16)
    return (normed, inverse, normed_b, grad_flat, query, keys, values, back_out)


def attend(query, keys, values, back_out, covered, scale):
    reads, narrow, width = query.shape
    shape4 = (reads, narrow, HEADS, HEAD_DIM)
    query4 = query.reshape(shape4)
    keys4 = keys.reshape(shape4)
    values4 = values.reshape(shape4)
    back4 = back_out.reshape(shape4)
    partial_logits = jnp.einsum("rchd,schd->hrs", query4, keys4, preferred_element_type=jnp.float32)
    logits = lax.psum(partial_logits, ("read", "pos")) * scale
    expon = jnp.exp(logits)
    probs = expon / jnp.sum(expon, -1, keepdims=True)
    probs_b = probs.astype(jnp.bfloat16)
    slopes = lax.psum(
        jnp.einsum("rchd,schd->hrs", back4, values4, preferred_element_type=jnp.float32),
        ("read", "pos"),
    )
    mixed = (scale * probs * (slopes - jnp.sum(probs * slopes, -1, keepdims=True))).astype(
        jnp.bfloat16
    )
    output = jnp.einsum(
        "hrs,schd->rchd", probs_b, values4, preferred_element_type=jnp.float32
    ).astype(jnp.bfloat16)
    keep4 = covered[:, :, None, None]
    grad_query = (
        jnp.einsum("hrs,schd->rchd", mixed, keys4, preferred_element_type=jnp.float32) * keep4
    ).astype(jnp.bfloat16)
    grad_keys = (
        jnp.einsum("hrs,rchd->schd", mixed, query4, preferred_element_type=jnp.float32) * keep4
    ).astype(jnp.bfloat16)
    grad_values = (
        jnp.einsum("hrs,rchd->schd", probs_b, back4, preferred_element_type=jnp.float32) * keep4
    ).astype(jnp.bfloat16)
    shape3 = (reads, narrow, width)
    return (
        output.reshape(shape3),
        grad_query.reshape(shape3),
        grad_keys.reshape(shape3),
        grad_values.reshape(shape3),
    )


def input_grad(grad_query, grad_keys, grad_values, weights, normed, inverse):
    grad_norm = (
        dot_back(grad_query, weights[0])
        + dot_back(grad_keys, weights[1])
        + dot_back(grad_values, weights[2])
    )
    result = inverse * (grad_norm - normed * jnp.mean(grad_norm * normed, -1, keepdims=True))
    return result.astype(jnp.bfloat16)


def shards(features, grad_out, weights, read_start, read_end):
    rows, col_dev, width = features.shape
    read_count = lax.axis_size("read")
    pos_count = lax.axis_size("pos")
    read_at = lax.axis_index("read")
    pos_at = lax.axis_index("pos")
    scale = 1.0 / math.sqrt(HEAD_DIM * col_dev * pos_count)
    narrow = col_dev // read_count
    total_reads = rows * read_count
    column_first = pos_at * col_dev + read_at * narrow
    column_cover = coverage(read_start, read_end, column_first, narrow)
    source, upstream = (
        lax.all_to_all(features, "read", split_axis=1, concat_axis=0, tiled=True),
        lax.all_to_all(grad_out, "read", split_axis=1, concat_axis=0, tiled=True),
    )
    normed, inverse, normed_b, grad_flat, query, keys, values, back_out = project(
        source, upstream, column_cover, weights
    )
    column_shape = (total_reads, narrow, width)
    output, grad_query, grad_keys, grad_values = attend(
        query.reshape(column_shape),
        keys.reshape(column_shape),
        values.reshape(column_shape),
        back_out.reshape(column_shape),
        column_cover,
        scale,
    )
    output_flat = output.reshape(-1, width)
    query_flat = grad_query.reshape(-1, width)
    keys_flat = grad_keys.reshape(-1, width)
    values_flat = grad_values.reshape(-1, width)
    column_grad = input_grad(query_flat, keys_flat, values_flat, weights, normed, inverse).reshape(
        column_shape
    )
    grad_input = lax.all_to_all(column_grad, "read", split_axis=0, concat_axis=1, tiled=True)
    right_side = jnp.concatenate([query_flat, keys_flat, values_flat], axis=1)
    inner_part = lax.dot_general(
        normed_b, right_side, (((0,), (0,)), ((), ())), preferred_element_type=jnp.float32
    )
    outer_part = lax.dot_general(
        output_flat, grad_flat, (((0,), (0,)), ((), ())), preferred_element_type=jnp.float32
    )
    weight_grads = lax.psum_scatter(
        jnp.concatenate([inner_part, outer_part], axis=1),
        ("read", "pos"),
        scatter_dimension=0,
        tiled=True,
    )
    return (grad_input, weight_grads)


def solution(mesh):
    in_specs = (P("read", "pos", None), P("read", "pos", None), P(), P(), P())
    out_specs = (P("read", "pos", None), P(("read", "pos"), None))
    return jax.shard_map(shards, mesh=mesh, in_specs=in_specs, out_specs=out_specs, check_vma=False)
```

profile of v0, /device:TPU:0, one launch (start us, length us, event | category | flops | bytes accessed | tf_op | source)
XLA Modules:
  0.0 332.3 jit_solution(14721531443585229019)
XLA Ops:
  7.2 1.8 copy.66
  8.9 7.3 %all-to-all-start = ((bf16[4,32,768]{2,0,1:T(4,128)(2,1)}), bf16[4,32,768]{2,0,1:T(4,128)(2,1)S(1)}, u32[]{:S(2)}, u32[]{:S(2)}) async-start(bf16[4,32,768]{2,0,1:T(4,128)(2,1)} %copy.66), calls=%async_computation | async-start | bytes 393216 | tf_op jit(solution)/shard_map/all_to_all | solution.py:107
  16.2 1.8 copy.73
  18.0 0.7 and_convert_fusion
  18.7 6.4 %all-to-all-done = bf16[4,32,768]{2,0,1:T(4,128)(2,1)S(1)} async-done(((bf16[4,32,768]{2,0,1:T(4,128)(2,1)}), bf16[4,32,768]{2,0,1:T(4,128)(2,1)S(1)}, u32[]{:S(2)}, u32[]{:S(2)}) %all-to-all-start) | async-done | bytes 196640 | tf_op jit(solution)/shard_map/all_to_all | solution.py:107
  25.1 2.7 all-to-all-start.1
  27.9 0.1 bitcast_reduce_fusion
  28.0 0.1 multiply_convert_fusion.2
  28.1 0.2 copy.70
  28.4 1.6 fusion.22
  30.0 1.6 fusion.16
  31.6 0.2 copy.75
  31.7 0.2 copy.71
  31.9 1.6 fusion.19
  33.5 0.2 copy.72
  33.7 3.1 all-to-all-done.1
  36.8 1.8 fusion.13
  38.6 0.2 copy.74
  38.8 1.2 fusion.50
  40.0 1.2 fusion.49
  41.3 0.1 copy.69
  41.4 0.1 rsqrt.13
  41.5 0.3 copy.76
  41.8 0.1 reshape.113
  41.9 129.9 %all-reduce.3.cloned.1.call-done = (f32[12,128,128]{2,1,0:T(8,128)}, f32[12,128,128]{2,1,0:T(8,128)}) async-done(((f32[12,128,128]{2,1,0:T(8,128)}, f32[12,128,128]{2,1,0:T(8,128)}), (f32[12,128,128]{2,1,0:T(8,128)}, f32[12,128,128]{2,1,0:T(8,128)})) %all-reduce.3.cloned.1.call-update) | async-done | bytes 1572880 | tf_op jit(solution)/shard_map/psum | solution.py:56
  171.8 1.5 fusion.35
  173.3 1.6 fusion.25
  174.9 1.6 convolution_convert_fusion
  176.5 0.5 multiply_reduce_fusion
  177.1 0.5 multiply_convert_fusion
  177.5 0.2 fusion.26
  177.8 0.4 fusion.27
  178.2 0.5 fusion.51
  178.6 4.0 %fusion.36 = f32[768,2304]{1,0:T(8,128)} fusion(bf16[128,768]{0,1:T(8,128)(2,1)S(1)} %bitcast.124, bf16[128,768]{0,1:T(8,128)(2,1)S(1)} %bitcast.114, bf16[128,768]{0,1:T(8,128)(2,1)S(1)} %bitcast.116, f32[128,768]{1,0:T(8,128)S(1)} %reshape.113, f32[128]{0:T(128)S(1)} %rsqrt.13), kind=kOutput, calls=%fused_computation.41 | convolution fusion | flops 454950912 | bytes 8061440 | tf_op jit(solution)/shard_map/dot_general | solution.py:131
  182.6 8.1 %pad_maximum_fusion = f32[768,3072]{1,0:T(8,128)} fusion(f32[768,768]{1,0:T(8,128)S(1)} %fusion.51, f32[768,2304]{1,0:T(8,128)} %fusion.36), kind=kLoop, calls=%fused_computation | loop fusion | flops 2359296 | bytes 18874368 | tf_op jit(solution)/shard_map/concatenate | solution.py:138
  190.7 1.8 fusion.7
  192.5 1.8 convolution_add_fusion.1
  194.3 2.0 multiply_reduce_fusion.1
  196.4 0.1 fusion.42
  196.5 0.5 broadcast.71
  197.1 0.7 reduce.2
  197.8 0.1 reshape.117
  197.9 12.1 %all_to_all.42 = bf16[32,2,1536]{2,1,0:T(2,128)(2,1)S(1)} all-to-all(bf16[32,2,1536]{2,1,0:T(2,128)(2,1)S(1)} %reshape.117), channel_id=1, replica_groups=mesh['read'=32,'pos'=1] {'read'}, dimensions={0} | all-to-all | bytes 393216 | tf_op jit(solution)/shard_map/all_to_all | solution.py:129
  210.0 0.1 reshape.118
  210.1 1.2 reduce.1
  211.3 0.1 all_to_all.36
  211.3 0.7 copy.79
  212.0 113.4 %reduce-scatter.2.cloned.1.call-done = f32[24,3072]{1,0:T(8,128)} async-done(((f32[768,3072]{1,0:T(8,128)}), f32[24,3072]{1,0:T(8,128)}) %reduce-scatter.2.cloned.1.call-update) | async-done | bytes 294928 | tf_op jit(solution)/shard_map/reduce_scatter | solution.py:137
  (13 shorter events, 0.3 us)
Async XLA Ops:
  8.9 16.2 %all-to-all-start = ((bf16[4,32,768]{2,0,1:T(4,128)(2,1)}), bf16[4,32,768]{2,0,1:T(4,128)(2,1)S(1)}, u32[]{:S(2)}, u32[]{:S(2)}) async-start(bf16[4,32,768]{2,0,1:T(4,128)(2,1)} %copy.66), calls=%async_computation | async-start | bytes 393216 | tf_op jit(solution)/shard_map/all_to_all | solution.py:107
  25.1 11.6 %all-to-all-start.1 = ((bf16[4,32,768]{2,0,1:T(4,128)(2,1)}), bf16[4,32,768]{2,0,1:T(4,128)(2,1)S(1)}, u32[]{:S(2)}, u32[]{:S(2)}) async-start(bf16[4,32,768]{2,0,1:T(4,128)(2,1)} %copy.73), calls=%async_computation.1 | async-start | bytes 393216 | tf_op jit(solution)/shard_map/all_to_all | solution.py:108
  27.8 144.0 %all-reduce.3.cloned.1.call-start = ((), (), s32[]{:S(2)}) async-start(), calls=%async_computation.5 | async-start | bytes 3145728 | tf_op jit(solution)/shard_map/psum | solution.py:56
  41.2 284.2 %reduce-scatter.2.cloned.1.call-start = ((), (), s32[]{:S(2)}) async-start(), calls=%async_computation.4 | async-start | bytes 9732096 | tf_op jit(solution)/shard_map/reduce_scatter | solution.py:137
  171.8 4.7 %copy-start = (f32[12,128,128]{2,1,0:T(8,128)S(1)}, f32[12,128,128]{2,1,0:T(8,128)}, u32[]{:S(2)}) copy-start(f32[12,128,128]{2,1,0:T(8,128)} %get-tuple-element.9) | copy-start | bytes 2359300
  171.8 4.7 %copy-start.1 = (f32[12,128,128]{2,1,0:T(8,128)S(1)}, f32[12,128,128]{2,1,0:T(8,128)}, u32[]{:S(2)}) copy-start(f32[12,128,128]{2,1,0:T(8,128)} %get-tuple-element.8) | copy-start | bytes 2359300
Sparse Core Ops, SparseCore 0:
  41.3 130.4 all-reduce.2
  190.8 134.5 reduce-scatter.1
where the time goes:
time: 333 us; the launch traced here: 332 us
  waiting for transfers between devices  253 us (76%)
  matrix products  22.9 us (7%)
  between operations  14.3 us (4%)
  other arithmetic  13.5 us (4%)
  blocking collectives  12.1 us (4%)
  starting transfers between devices  10.1 us (3%)
  local copies, waits for them, and re-layouts  6.56 us (2%)
    psum x1, waiting for transfers between devices, attend(): lax.psum(jnp.einsum('rchd,schd->hrs', back4, values4, preferred_element_t...  130 us
    reduce_scatter x1, waiting for transfers between devices, shards(): lax.psum_scatter(jnp.concatenate([inner_part, outer_part], axis=1), ('rea...  113 us
    all_to_all x1, blocking collectives, shards(): lax.all_to_all(column_grad, 'read', split_axis=0, concat_axis=1, tiled=True)  12.1 us
    concatenate x1, other arithmetic, shards(): jnp.concatenate([inner_part, outer_part], axis=1)  8.06 us
    dot_general x4, matrix products, dot_back(): lax.dot_general(left, right, (((1,), (1,)), ((), ())), preferred_element_...  7.46 us
    all_to_all x1, starting transfers between devices, shards(): lax.all_to_all(features, 'read', split_axis=1, concat_axis=0, tiled=True)  7.3 us
  transfers between devices with their start and end apart: 4, of which 4 were waited for; matrix products, arithmetic and copies ran while one was open for 5% of the time, Pallas kernels for 0%

commit v1 on v0

v1 whole, which is shorter than its diff:
```python
import math

import jax
import jax.numpy as jnp
from jax import lax
from jax.sharding import PartitionSpec as P

HEADS = 12
HEAD_DIM = 64
CORES = 2
KINDS = 4


def coverage(starts, ends, columns):
    inside = (columns[:, None] >= starts[None, :]) & (columns[:, None] < ends[None, :])
    return inside.astype(jnp.float32)


def dot_back(left, right):
    return lax.dot_general(
        left, right, (((1,), (1,)), ((), ())), preferred_element_type=jnp.float32
    )


def dot_cells(left, right):
    return lax.dot_general(
        left, right, (((0,), (0,)), ((), ())), preferred_element_type=jnp.float32
    )


def exchange(array, groups):
    return lax.all_to_all(
        array, "read", split_axis=0, concat_axis=0, tiled=True, axis_index_groups=groups
    )


def shards(features, grad_out, weights, read_start, read_end):
    rows, col_dev, width = features.shape
    count = lax.axis_size("read")
    pos_count = lax.axis_size("pos")
    me = lax.axis_index("read")
    pos_at = lax.axis_index("pos")
    scale = 1.0 / math.sqrt(HEAD_DIM * col_dev * pos_count)
    reads = rows * count
    chips = count // CORES
    part_heads = HEADS // CORES
    half = width // CORES
    core = me % CORES
    kind = (me // CORES) % KINDS
    tied_rows = reads // chips

    same_core = [list(range(c, count, CORES)) for c in range(CORES)]
    plane = [
        [base + c + CORES * j for j in range(KINDS)]
        for base in range(0, count, CORES * KINDS)
        for c in range(CORES)
    ]
    partner = [(i, i ^ 1) for i in range(count)]

    send = jnp.stack([features, grad_out]).transpose(2, 0, 1, 3).reshape(-1, width)
    own = exchange(send, None)
    other = lax.ppermute(own, "read", partner)
    both = jnp.stack([own, other]).reshape(2, count, 2, rows, width)
    source = both[:, :, 0].reshape(2 * reads, width)
    upstream = both[:, :, 1].reshape(2 * reads, width)
    columns = pos_at * col_dev + jnp.stack([me, me ^ 1])
    covered = coverage(read_start, read_end, columns).reshape(-1, 1)

    heads_in = lax.dynamic_slice_in_dim(weights[:3], core * half, half, 2)
    heads_out = lax.dynamic_slice_in_dim(weights[3], core * half, half, 0)
    source32 = source.astype(jnp.float32)
    inverse = lax.rsqrt(jnp.mean(source32 * source32, -1, keepdims=True) + 1e-05)
    normed = source32 * inverse
    normed_b = normed.astype(jnp.bfloat16)
    query, keys, values = (
        (jnp.dot(normed_b, heads_in[i], preferred_element_type=jnp.float32) * covered).astype(
            jnp.bfloat16
        )
        for i in range(3)
    )
    back_out = dot_back(upstream, heads_out).astype(jnp.bfloat16)

    shape4 = (2, reads, part_heads, HEAD_DIM)
    query4, keys4, values4, back4 = (
        a.reshape(shape4) for a in (query, keys, values, back_out)
    )
    partial = jnp.stack(
        [
            jnp.einsum("crhd,cshd->hrs", query4, keys4, preferred_element_type=jnp.float32),
            jnp.einsum("crhd,cshd->hrs", back4, values4, preferred_element_type=jnp.float32),
        ],
        1,
    ).astype(jnp.bfloat16)
    partial = partial.reshape(part_heads, 2, chips, tied_rows, reads).transpose(2, 0, 1, 3, 4)
    parts = exchange(partial, same_core).astype(jnp.float32)
    tied = lax.psum(jnp.sum(parts, 0), "pos")
    logits = tied[:, 0] * scale
    slopes = tied[:, 1]
    expon = jnp.exp(logits)
    probs = expon / jnp.sum(expon, -1, keepdims=True)
    mixed = scale * probs * (slopes - jnp.sum(probs * slopes, -1, keepdims=True))
    pair = jnp.stack([probs, mixed], 1).astype(jnp.bfloat16)
    copies = jnp.broadcast_to(pair[None], (chips,) + pair.shape)
    pairs = exchange(copies, same_core).transpose(1, 2, 0, 3, 4)
    pairs = pairs.reshape(part_heads, 2, reads, reads)
    probs_b, mixed = pairs[:, 0], pairs[:, 1]

    keep4 = covered.reshape(2, reads, 1, 1)

    def spread(form, left, right, keep=None):
        result = jnp.einsum(form, left, right, preferred_element_type=jnp.float32)
        if keep is not None:
            result = result * keep
        return result.astype(jnp.bfloat16).reshape(2 * reads, half)

    output = spread("hrs,cshd->crhd", probs_b, values4)
    grad_query = spread("hrs,cshd->crhd", mixed, keys4, keep4)
    grad_keys = spread("hrs,crhd->cshd", mixed, query4, keep4)
    grad_values = spread("hrs,crhd->cshd", probs_b, back4, keep4)

    grad_norm = (
        dot_back(grad_query, heads_in[0])
        + dot_back(grad_keys, heads_in[1])
        + dot_back(grad_values, heads_in[2])
    )
    grad_norm = grad_norm[:reads] + lax.ppermute(grad_norm[reads:], "read", partner)
    grad_in = inverse[:reads] * (
        grad_norm - normed[:reads] * jnp.mean(grad_norm * normed[:reads], -1, keepdims=True)
    )
    grad_in = exchange(grad_in.astype(jnp.bfloat16), None)
    grad_input = grad_in.reshape(col_dev, rows, width).transpose(1, 0, 2)

    left = jnp.stack([normed_b[:reads]] * 3 + [upstream[:reads]])
    left = exchange(left, plane)
    left = jnp.stack([left, lax.ppermute(left, "read", partner)], 1).reshape(-1, width)
    right = exchange(jnp.stack([grad_query, grad_keys, grad_values, output]), plane)
    right = right.reshape(-1, half)
    right_other = lax.ppermute(right, "read", partner)
    right_other = right_other.reshape(KINDS, 2, reads, half)[:, ::-1].reshape(-1, half)
    outputs = jnp.concatenate(
        [
            jnp.where(core == 0, right, right_other),
            jnp.where(core == 0, right_other, right),
        ],
        1,
    )
    last = kind == KINDS - 1
    product = dot_cells(
        jnp.where(last, outputs, left),
        jnp.where(last, lax.dynamic_slice_in_dim(left, core * half, half, 1), right),
    ).astype(jnp.bfloat16)
    pieces = exchange(product.reshape(count, width // count, half), None)
    pieces = pieces.reshape(-1, KINDS, CORES, width // count, half).astype(jnp.float32)
    sums = jnp.sum(pieces, 0).transpose(2, 0, 1, 3).reshape(width // count, KINDS * width)
    weight_grads = lax.psum_scatter(sums, "pos", scatter_dimension=0, tiled=True)
    return (grad_input, weight_grads)


def solution(mesh):
    in_specs = (P("read", "pos", None), P("read", "pos", None), P(), P(), P())
    out_specs = (P("read", "pos", None), P(("read", "pos"), None))
    return jax.shard_map(shards, mesh=mesh, in_specs=in_specs, out_specs=out_specs, check_vma=False)
```

time: 333 us -> 194 us (0.58)
  waiting for transfers between devices: 253 us -> 47.6 us
  local copies, waits for them, and re-layouts: 6.56 us -> 61.7 us
  starting transfers between devices: 10.1 us -> 26 us
  between operations: 14.3 us -> 1.04 us
  blocking collectives: 12.1 us -> 20.4 us
    psum x1 -> x0, waiting for transfers between devices: 130 us -> none  [attend(): lax.psum(jnp.einsum('rchd,schd->hrs', back4, values4, preferred_element_t...]
    reduce_scatter x1 -> x0, waiting for transfers between devices: 113 us -> none  [shards(): lax.psum_scatter(jnp.concatenate([inner_part, outer_part], axis=1), ('rea...]
    all_to_all x2 -> x6, waiting for transfers between devices: 9.5 us -> 47.6 us  [exchange(): lax.all_to_all(array, 'read', split_axis=0, concat_axis=0, tiled=True, ax...]
    convert_element_type x8 -> x12, local copies, waits for them, and re-layouts: 1.25 us -> 18.3 us  [the longest x3 5.23 us: shards(): (jnp.dot(normed_b, heads_in[i], preferred_element_type=jnp.float32) * cov...]
    all_to_all x2 -> x6, starting transfers between devices: 10 us -> 25.8 us  [exchange(): lax.all_to_all(array, 'read', split_axis=0, concat_axis=0, tiled=True, ax...]
    another operation x0 -> x10, local copies, waits for them, and re-layouts: none -> 13.5 us  [the longest x4 6.92 us: shards(): jnp.stack([grad_query, grad_keys, grad_values, output])]
    another operation x0 -> x7, other arithmetic: none -> 8.61 us  [the longest x1 2.21 us: shards(): jnp.stack([grad_query, grad_keys, grad_values, output])]
    slice x0 -> x8, local copies, waits for them, and re-layouts: none -> 8.6 us  [the longest x1 2.41 us: shards(): heads_out = lax.dynamic_slice_in_dim(weights[3], core * half, half, 0)]
  transfers between devices with their start and end apart: 4 -> 10, of which waited for: 4 -> 5; matrix products, arithmetic and copies ran while one was open for 5% -> 27% of each run, Pallas kernels for 0% -> 0%
where the time goes in v1:
time: 194 us; the launch traced here: 192 us
  local copies, waits for them, and re-layouts  61.7 us (32%)
  waiting for transfers between devices  47.6 us (25%)
  starting transfers between devices  26 us (13%)
  matrix products  22 us (11%)
  blocking collectives  20.4 us (11%)
  other arithmetic  13.8 us (7%)
    all_to_all x6, waiting for transfers between devices, exchange(): lax.all_to_all(array, 'read', split_axis=0, concat_axis=0, tiled=True, ax...  47.6 us
    all_to_all x6, starting transfers between devices, exchange(): lax.all_to_all(array, 'read', split_axis=0, concat_axis=0, tiled=True, ax...  25.8 us
    all_to_all x1, blocking collectives, exchange(): lax.all_to_all(array, 'read', split_axis=0, concat_axis=0, tiled=True, ax...  20.4 us
    another operation x4, local copies, waits for them, and re-layouts, shards(): jnp.stack([grad_query, grad_keys, grad_values, output])  6.92 us
    reshape x4, local copies, waits for them, and re-layouts, shards(): a.reshape(shape4)  6.62 us
    dot_general x4, matrix products, dot_back(): lax.dot_general(left, right, (((1,), (1,)), ((), ())), preferred_element_...  6.6 us
    dot_general x3, matrix products, shards(): jnp.dot(normed_b, heads_in[i], preferred_element_type=jnp.float32) * covered  6.13 us
    convert_element_type x3, local copies, waits for them, and re-layouts, shards(): (jnp.dot(normed_b, heads_in[i], preferred_element_type=jnp.float32) * cov...  5.23 us
  transfers between devices with their start and end apart: 10, of which 5 were waited for; matrix products, arithmetic and copies ran while one was open for 27% of the time, Pallas kernels for 0%

profile of v1, /device:TPU:0, one launch (start us, length us, event | category | flops | bytes accessed | tf_op | source)
XLA Modules:
  0.0 192.5 jit_solution(15633588490640355188)
XLA Ops:
  1.9 20.4 %all_to_all.46 = bf16[32,8,768]{2,1,0:T(8,128)(2,1)} all-to-all(bf16[32,8,768]{2,1,0:T(8,128)(2,1)S(1)} %copy.144), channel_id=1, replica_groups=mesh['read'=32,'pos'=1] {'read'}, dimensions={0} | all-to-all | bytes 786432 | tf_op jit(solution)/shard_map/all_to_all | solution.py:32
  22.3 2.2 %slice.61 = bf16[3,768,768]{2,1,0:T(8,128)(2,1)S(1)} slice(bf16[4,768,768]{2,1,0:T(8,128)(2,1)} %param.7), slice={[0:3], [0:768], [0:768]} | slice | bytes 7077888 | tf_op jit(solution)/shard_map/slice | solution.py:69
  24.6 2.4 %slice.65 = bf16[1,768,768]{2,1,0:T(8,128)(2,1)} slice(bf16[4,768,768]{2,1,0:T(8,128)(2,1)} %param.7), slice={[3:4], [0:768], [0:768]} | slice | bytes 2359296 | tf_op jit(solution)/shard_map/slice | solution.py:70
  27.1 1.8 copy.106
  28.9 1.9 stack.68
  31.9 2.1 %pad_maximum_fusion.3 = (bf16[2,32,1,4,768]{4,1,3,2,0:T(8,128)(2,1)}, f32[2,32,1,4,768]{4,1,3,2,0:T(8,128)}) fusion(bf16[1,32,2,4,768]{4,1,3,2,0:T(8,128)(2,1)S(1)} %copy.107, bf16[1,32,2,4,768]{4,1,3,2,0:T(8,128)(2,1)} %bitcast.149), kind=kLoop, calls=%fused_computation.55 | loop fusion | flops 589824 | bytes 1966080 | tf_op jit(solution)/shard_map/stack | solution.py:63
  35.5 1.8 convert_element_type.98
  37.3 2.0 %fusion.6 = bf16[256,384]{1,0:T(8,128)(2,1)} fusion(bf16[256,768]{1,0:T(8,128)(2,1)} %convert_element_type.98, bf16[3,768,768]{2,1,0:T(8,128)(2,1)S(1)} %slice.61, s32[]{:T(128)S(6)} %select_n.47, f32[256]{0:T(256)S(1)} %fusion.60), kind=kOutput, calls=%fused_computation.19 | convolution fusion | flops 151191552 | bytes 1180676 | tf_op jit(solution)/shard_map/dot_general | solution.py:76
  39.3 2.0 %fusion.7 = bf16[256,384]{1,0:T(8,128)(2,1)} fusion(bf16[256,768]{1,0:T(8,128)(2,1)} %convert_element_type.98, bf16[3,768,768]{2,1,0:T(8,128)(2,1)S(1)} %slice.61, s32[]{:T(128)S(6)} %add.55, s32[]{:T(128)S(6)} %select_n.47, f32[256]{0:T(256)S(1)} %fusion.60), kind=kOutput, calls=%fused_computation.20 | convolution fusion | flops 151191552 | bytes 1180680 | tf_op jit(solution)/shard_map/dot_general | solution.py:76
  41.4 1.7 copy.116
  43.1 1.7 reshape.256
  44.8 2.1 %copy.114 = bf16[2,32,1,4,768]{4,3,1,0,2:T(4,128)(2,1)} copy(bf16[2,32,1,4,768]{4,1,3,2,0:T(8,128)(2,1)} %get-tuple-element.8) | data formatting | bytes 786432 | tf_op jit(solution)/shard_map/slice | solution.py:65
  46.9 1.8 reshape_squeeze.4
  48.7 2.2 %convolution_convert_fusion.1 = bf16[256,384]{1,0:T(8,128)(2,1)} fusion(bf16[256,768]{1,0:T(8,128)(2,1)} %reshape_squeeze.4, bf16[1,768,768]{2,1,0:T(8,128)(2,1)} %slice.65, s32[]{:T(128)S(6)} %select_n.47), kind=kOutput, calls=%fused_computation.27 | convolution fusion | flops 151093248 | bytes 1179652 | tf_op jit(solution)/shard_map/dot_general | solution.py:20
  51.0 1.8 copy.115
  52.7 1.7 reshape.255
  54.4 2.1 %fusion.5 = bf16[256,384]{1,0:T(8,128)(2,1)} fusion(bf16[256,768]{1,0:T(8,128)(2,1)} %convert_element_type.98, bf16[3,768,768]{2,1,0:T(8,128)(2,1)S(1)} %slice.61, s32[]{:T(128)S(6)} %add.54, s32[]{:T(128)S(6)} %select_n.47, f32[256]{0:T(256)S(1)} %fusion.60), kind=kOutput, calls=%fused_computation.18 | convolution fusion | flops 151191552 | bytes 1180680 | tf_op jit(solution)/shard_map/dot_general | solution.py:76
  56.4 1.7 copy.110
  58.1 1.7 reshape.253
  59.8 1.8 copy.111
  61.6 1.7 reshape.254
  66.6 4.2 %all-to-all-start.1 = ((bf16[16,6,2,8,128]{4,3,1,2,0:T(8,128)(2,1)}), bf16[16,6,2,8,128]{4,3,1,2,0:T(8,128)(2,1)}, u32[]{:S(2)}, u32[]{:S(2)}) async-start(bf16[16,6,2,8,128]{4,3,1,2,0:T(8,128)(2,1)} %copy_bitcast_fusion), calls=%async_computation.1 | async-start | bytes 786432 | tf_op jit(solution)/shard_map/all_to_all | solution.py:32
  72.6 1.7 stack.79
  75.0 2.5 %copy.128 = f32[2,32,1,4,768]{4,3,1,0,2:T(4,128)} copy(f32[2,32,1,4,768]{4,1,3,2,0:T(8,128)} %get-tuple-element.9) | data formatting | bytes 1572864 | tf_op jit(solution)/shard_map/convert_element_type | solution.py:71
  77.5 2.3 %reshape.268 = f32[256,768]{1,0:T(8,128)} reshape(f32[2,32,1,4,768]{4,3,1,0,2:T(4,128)} %copy.128) | data formatting | bytes 1572864 | tf_op jit(solution)/shard_map/convert_element_type | solution.py:71
  80.7 1.3 broadcast_multiply_fusion
  83.9 4.2 %all-to-all-start.5 = ((bf16[4,128,768]{2,1,0:T(8,128)(2,1)}), bf16[4,128,768]{2,1,0:T(8,128)(2,1)}, u32[]{:S(2)}, u32[]{:S(2)}) async-start(bf16[4,128,768]{2,1,0:T(8,128)(2,1)} %pad_maximum_fusion.2), calls=%async_computation.5 | async-start | bytes 1572864 | tf_op jit(solution)/shard_map/all_to_all | solution.py:32
  90.1 9.8 %all-to-all-done.5 = bf16[4,128,768]{2,1,0:T(8,128)(2,1)} async-done(((bf16[4,128,768]{2,1,0:T(8,128)(2,1)}), bf16[4,128,768]{2,1,0:T(8,128)(2,1)}, u32[]{:S(2)}, u32[]{:S(2)}) %all-to-all-start.5) | async-done | bytes 786464 | tf_op jit(solution)/shard_map/all_to_all | solution.py:32
  99.9 1.5 broadcast_in_dim.2
  101.5 5.7 %all-to-all-start.2 = ((bf16[16,6,2,8,128]{4,3,1,2,0:T(8,128)(2,1)}), bf16[16,6,2,8,128]{4,3,1,2,0:T(8,128)(2,1)}, u32[]{:S(2)}, u32[]{:S(2)}) async-start(bf16[16,6,2,8,128]{4,3,1,2,0:T(8,128)(2,1)} %broadcast_in_dim.2), calls=%async_computation.2 | async-start | bytes 786432 | tf_op jit(solution)/shard_map/all_to_all | solution.py:32
  107.8 11.6 %all-to-all-done.2 = bf16[16,6,2,8,128]{4,3,1,2,0:T(8,128)(2,1)} async-done(((bf16[16,6,2,8,128]{4,3,1,2,0:T(8,128)(2,1)}), bf16[16,6,2,8,128]{4,3,1,2,0:T(8,128)(2,1)}, u32[]{:S(2)}, u32[]{:S(2)}) %all-to-all-start.2) | async-done | bytes 393248 | tf_op jit(solution)/shard_map/all_to_all | solution.py:32
  121.8 1.8 fusion.15
  126.3 1.7 stack_reshape.12
  128.0 2.3 %fusion.24 = f32[256,768]{1,0:T(8,128)} fusion(bf16[3,768,768]{2,1,0:T(8,128)(2,1)S(1)} %slice.61, s32[]{:T(128)S(6)} %select_n.47, bf16[48,8,2,128]{3,2,1,0:T(2,128)(2,1)} %bitcast.158), kind=kOutput, calls=%fused_computation.51 | convolution fusion | flops 150994944 | bytes 1572868 | tf_op jit(solution)/shard_map/dot_general | solution.py:20
  132.9 1.7 stack_reshape.15
  134.7 1.7 stack_reshape.14
  136.4 1.7 stack_reshape.13
  138.1 2.2 %pad_maximum_fusion.1 = bf16[4,256,384]{1,2,0:T(8,128)(2,1)} fusion(bf16[1,256,384]{1,2,0:T(8,128)(2,1)} %stack_reshape.15, bf16[1,256,384]{1,2,0:T(8,128)(2,1)} %stack_reshape.14, bf16[1,256,384]{1,2,0:T(8,128)(2,1)} %stack_reshape.13, bf16[1,256,384]{1,2,0:T(8,128)(2,1)} %stack_reshape.12), kind=kLoop, calls=%fused_computation.36 | loop fusion | flops 1179648 | bytes 1572864 | tf_op jit(solution)/shard_map/stack | solution.py:136
  140.3 4.2 %all-to-all-start.4 = ((bf16[4,256,384]{1,2,0:T(8,128)(2,1)}), bf16[4,256,384]{1,2,0:T(8,128)(2,1)}, u32[]{:S(2)}, u32[]{:S(2)}) async-start(bf16[4,256,384]{1,2,0:T(8,128)(2,1)} %pad_maximum_fusion.1), calls=%async_computation.4 | async-start | bytes 1572864 | tf_op jit(solution)/shard_map/all_to_all | solution.py:32
  144.5 1.7 convolution_add_fusion.1
  147.9 4.7 %all-to-all-done.4 = bf16[4,256,384]{1,2,0:T(8,128)(2,1)} async-done(((bf16[4,256,384]{1,2,0:T(8,128)(2,1)}), bf16[4,256,384]{1,2,0:T(8,128)(2,1)}, u32[]{:S(2)}, u32[]{:S(2)}) %all-to-all-start.4) | async-done | bytes 786464 | tf_op jit(solution)/shard_map/all_to_all | solution.py:32
  152.6 1.5 copy.135
  154.2 1.5 pad_maximum_fusion
  158.1 4.8 %all-to-all-start.3 = ((bf16[32,4,768]{2,1,0:T(4,128)(2,1)}), bf16[32,4,768]{2,1,0:T(4,128)(2,1)S(1)}, u32[]{:S(2)}, u32[]{:S(2)}) async-start(bf16[32,4,768]{2,1,0:T(4,128)(2,1)} %all_to_all.34), calls=%async_computation.3 | async-start | bytes 393216 | tf_op jit(solution)/shard_map/all_to_all | solution.py:32
  164.5 1.9 fusion.4
  166.4 5.4 %all-to-all-done.3 = bf16[32,4,768]{2,1,0:T(4,128)(2,1)S(1)} async-done(((bf16[32,4,768]{2,1,0:T(4,128)(2,1)}), bf16[32,4,768]{2,1,0:T(4,128)(2,1)S(1)}, u32[]{:S(2)}, u32[]{:S(2)}) %all-to-all-start.3) | async-done | bytes 196640 | tf_op jit(solution)/shard_map/all_to_all | solution.py:32
  171.8 2.7 %all-to-all-start.6 = ((bf16[32,24,384]{2,1,0:T(8,128)(2,1)}), bf16[32,24,384]{2,1,0:T(8,128)(2,1)S(1)}, u32[]{:S(2)}, u32[]{:S(2)}) async-start(bf16[32,24,384]{2,1,0:T(8,128)(2,1)} %bitcast.45), calls=%async_computation.6 | async-start | bytes 1179648 | tf_op jit(solution)/shard_map/all_to_all | solution.py:32
  175.2 16.0 %all-to-all-done.6 = bf16[32,24,384]{2,1,0:T(8,128)(2,1)S(1)} async-done(((bf16[32,24,384]{2,1,0:T(8,128)(2,1)}), bf16[32,24,384]{2,1,0:T(8,128)(2,1)S(1)}, u32[]{:S(2)}, u32[]{:S(2)}) %all-to-all-start.6) | async-done | bytes 589856 | tf_op jit(solution)/shard_map/all_to_all | solution.py:32
  (91 shorter events, 30.3 us)
Async XLA Ops:
  22.3 6.6 %collective-permute-start = (bf16[256,768]{1,0:T(8,128)(2,1)}, bf16[256,768]{1,0:T(8,128)(2,1)}, u32[]{:S(2)}, u32[]{:S(2)}) collective-permute-start(bf16[256,768]{1,0:T(8,128)(2,1)} %bitcast.5), channel_id=1, source_target_pairs={{0,1},{1,0},{2,3},{3,2},{4,5},{5,4},{6,7},{7,6},{8,9},{9,8},{10,11... | collective-permute-start | bytes 1179656 | tf_op jit(solution)/shard_map/ppermute | solution.py:62
  24.5 2.5 %copy-start.12 = (s32[128]{0:T(128)S(1)}, s32[128]{0:T(128)}, u32[]{:S(2)}) copy-start(s32[128]{0:T(128)} %param.9) | copy-start | bytes 1540
  24.6 2.5 %copy-start.13 = (s32[128]{0:T(128)S(1)}, s32[128]{0:T(128)}, u32[]{:S(2)}) copy-start(s32[128]{0:T(128)} %param.8) | copy-start | bytes 1540
  27.1 7.0 %copy-start.14 = (s32[2]{0:T(128)}, s32[2]{0:T(128)S(1)}, u32[]{:S(2)}) copy-start(s32[2]{0:T(128)S(1)} %add_bitcast_fusion) | copy-start | bytes 28
  30.8 3.3 %copy-start = (bf16[32,8,768]{2,0,1:T(8,128)(2,1)S(1)}, bf16[32,8,768]{2,0,1:T(8,128)(2,1)}, u32[]{:S(2)}) copy-start(bf16[32,8,768]{2,0,1:T(8,128)(2,1)} %copy.106) | copy-start | bytes 1179652
  66.6 17.3 %all-to-all-start.1 = ((bf16[16,6,2,8,128]{4,3,1,2,0:T(8,128)(2,1)}), bf16[16,6,2,8,128]{4,3,1,2,0:T(8,128)(2,1)}, u32[]{:S(2)}, u32[]{:S(2)}) async-start(bf16[16,6,2,8,128]{4,3,1,2,0:T(8,128)(2,1)} %copy_bitcast_fusion), calls=%async_computation.1 | async-start | bytes 786432 | tf_op jit(solution)/shard_map/all_to_all | solution.py:32
  80.7 2.2 %copy-start.7 = (bf16[1,128,768]{2,1,0:T(8,128)(2,1)S(1)}, bf16[1,128,768]{2,1,0:T(8,128)(2,1)}, u32[]{:S(2)}) copy-start(bf16[1,128,768]{2,1,0:T(8,128)(2,1)} %stack.79) | copy-start | bytes 589828
  82.0 0.9 copy-start.3
  83.9 23.3 %copy-start.15 = (s32[2]{0:T(128)S(1)}, s32[2]{0:T(128)}, u32[]{:S(2)}) copy-start(s32[2]{0:T(128)} %copy-done.14) | copy-start | bytes 28
  83.9 16.0 %all-to-all-start.5 = ((bf16[4,128,768]{2,1,0:T(8,128)(2,1)}), bf16[4,128,768]{2,1,0:T(8,128)(2,1)}, u32[]{:S(2)}, u32[]{:S(2)}) async-start(bf16[4,128,768]{2,1,0:T(8,128)(2,1)} %pad_maximum_fusion.2), calls=%async_computation.5 | async-start | bytes 1572864 | tf_op jit(solution)/shard_map/all_to_all | solution.py:32
  101.5 18.0 %all-to-all-start.2 = ((bf16[16,6,2,8,128]{4,3,1,2,0:T(8,128)(2,1)}), bf16[16,6,2,8,128]{4,3,1,2,0:T(8,128)(2,1)}, u32[]{:S(2)}, u32[]{:S(2)}) async-start(bf16[16,6,2,8,128]{4,3,1,2,0:T(8,128)(2,1)} %broadcast_in_dim.2), calls=%async_computation.2 | async-start | bytes 786432 | tf_op jit(solution)/shard_map/all_to_all | solution.py:32
  107.8 15.8 %copy-start.16 = (f32[2,128]{1,0:T(2,128)S(1)}, f32[2,128]{1,0:T(2,128)}, u32[]{:S(2)}) copy-start(f32[2,128]{1,0:T(2,128)} %and_convert_fusion) | copy-start | bytes 3076
  107.8 46.4 %collective-permute-start.3 = (bf16[4,128,768]{2,1,0:T(8,128)(2,1)}, bf16[4,128,768]{2,1,0:T(8,128)(2,1)}, u32[]{:S(2)}, u32[]{:S(2)}) collective-permute-start(bf16[4,128,768]{2,1,0:T(8,128)(2,1)} %all-to-all-done.5), channel_id=1, source_target_pairs={{0,1},{1,0},{2,3},{3,2},{4,5},{5,4},{6,7},{7,6},{8,9},{9,8},{10,11... | collective-permute-start | bytes 2359304 | tf_op jit(solution)/shard_map/ppermute | solution.py:135
  119.4 4.2 %copy-start.8 = (bf16[2,128,6,64]{1,0,3,2:T(2,128)(2,1)S(1)}, bf16[2,128,6,64]{1,0,3,2:T(2,128)(2,1)}, u32[]{:S(2)}) copy-start(bf16[2,128,6,64]{1,0,3,2:T(2,128)(2,1)} %reshape.255) | copy-start | bytes 589828
  119.4 5.0 %copy-start.6 = (bf16[2,128,6,64]{1,0,3,2:T(2,128)(2,1)S(1)}, bf16[2,128,6,64]{1,0,3,2:T(2,128)(2,1)}, u32[]{:S(2)}) copy-start(bf16[2,128,6,64]{1,0,3,2:T(2,128)(2,1)} %reshape.256) | copy-start | bytes 589828
  128.0 2.3 %copy-start.10 = (bf16[2,128,6,64]{1,3,0,2:T(8,128)(2,1)S(1)}, bf16[2,128,6,64]{1,3,0,2:T(8,128)(2,1)}, u32[]{:S(2)}) copy-start(bf16[2,128,6,64]{1,3,0,2:T(8,128)(2,1)} %fusion.15) | copy-start | bytes 589828
  128.0 3.2 %copy-start.11 = (bf16[2,128,6,64]{1,3,0,2:T(8,128)(2,1)S(1)}, bf16[2,128,6,64]{1,3,0,2:T(8,128)(2,1)}, u32[]{:S(2)}) copy-start(bf16[2,128,6,64]{1,3,0,2:T(8,128)(2,1)} %fusion.14) | copy-start | bytes 589828
  128.0 4.0 %copy-start.9 = (bf16[2,128,6,64]{1,3,0,2:T(8,128)(2,1)S(1)}, bf16[2,128,6,64]{1,3,0,2:T(8,128)(2,1)}, u32[]{:S(2)}) copy-start(bf16[2,128,6,64]{1,3,0,2:T(8,128)(2,1)} %fusion.13) | copy-start | bytes 589828
  140.3 12.3 %all-to-all-start.4 = ((bf16[4,256,384]{1,2,0:T(8,128)(2,1)}), bf16[4,256,384]{1,2,0:T(8,128)(2,1)}, u32[]{:S(2)}, u32[]{:S(2)}) async-start(bf16[4,256,384]{1,2,0:T(8,128)(2,1)} %pad_maximum_fusion.1), calls=%async_computation.4 | async-start | bytes 1572864 | tf_op jit(solution)/shard_map/all_to_all | solution.py:32
  144.5 1.7 copy-start.5
  146.6 0.9 copy-start.1
  147.6 8.3 %collective-permute-start.1 = (f32[128,768]{1,0:T(8,128)S(1)}, f32[128,768]{1,0:T(8,128)S(1)}, u32[]{:S(2)}, u32[]{:S(2)}) collective-permute-start(f32[128,768]{1,0:T(8,128)S(1)} %slice.84), channel_id=1, source_target_pairs={{0,1},{1,0},{2,3},{3,2},{4,5},{5,4},{6,7},{7,6},{8,9},{9,8},{10,11... | collective-permute-start | bytes 1179656 | tf_op jit(solution)/shard_map/ppermute | solution.py:126
  154.1 8.8 %collective-permute-start.2 = (bf16[1024,384]{1,0:T(8,128)(2,1)S(1)}, bf16[1024,384]{1,0:T(8,128)(2,1)}, u32[]{:S(2)}, u32[]{:S(2)}) collective-permute-start(bf16[1024,384]{1,0:T(8,128)(2,1)S(1)} %bitcast.153), channel_id=1, source_target_pairs={{0,1},{1,0},{2,3},{3,2},{4,5},{5,4},{6,7},{7,6},{8,9},{9,8},{10,11... | collective-permute-start | bytes 2359304 | tf_op jit(solution)/shard_map/ppermute | solution.py:138
  155.7 1.1 copy-start.2
  155.7 1.4 copy-start.4
  158.1 13.7 %all-to-all-start.3 = ((bf16[32,4,768]{2,1,0:T(4,128)(2,1)}), bf16[32,4,768]{2,1,0:T(4,128)(2,1)S(1)}, u32[]{:S(2)}, u32[]{:S(2)}) async-start(bf16[32,4,768]{2,1,0:T(4,128)(2,1)} %all_to_all.34), calls=%async_computation.3 | async-start | bytes 393216 | tf_op jit(solution)/shard_map/all_to_all | solution.py:32
  171.8 19.5 %all-to-all-start.6 = ((bf16[32,24,384]{2,1,0:T(8,128)(2,1)}), bf16[32,24,384]{2,1,0:T(8,128)(2,1)S(1)}, u32[]{:S(2)}, u32[]{:S(2)}) async-start(bf16[32,24,384]{2,1,0:T(8,128)(2,1)} %bitcast.45), calls=%async_computation.6 | async-start | bytes 1179648 | tf_op jit(solution)/shard_map/all_to_all | solution.py:32

commit v2 on v1

v2 whole, which is shorter than its diff:
```python
import functools
import math

import jax
import jax.numpy as jnp
from jax import lax
from jax.experimental import pallas as pl
from jax.experimental.pallas import tpu as pltpu
from jax.sharding import PartitionSpec as P

HEADS = 12
HEAD_DIM = 64
CORES = 2
KINDS = 4
LANES = 128
VMEM_LIMIT = 48 * 1024 * 1024

BF16 = jnp.bfloat16
F32 = jnp.float32


def dot(left, right, contract=(1, 0)):
    return lax.dot_general(
        left, right, (((contract[0],), (contract[1],)), ((), ())), preferred_element_type=F32
    )


def row_mask(start, end, column):
    return ((start <= column) & (column < end)).astype(F32)


def first_heads(rows, lanes):
    at = lax.broadcasted_iota(jnp.int32, (rows, lanes), 1)
    return lax.rem(at, LANES) < HEAD_DIM


def slab(array, at):
    reads = array.shape[0] // 2
    lanes = slice(at * LANES, (at + 1) * LANES)
    return jnp.concatenate([array[:reads, lanes], array[reads:, lanes]], axis=1)


def project_kernel(
    scalars, own, other, heads_in, heads_out, start, end, proj, tied, left_own, left_other, *, rows
):
    cells = own.shape[0] // 2
    at = lax.broadcasted_iota(jnp.int32, (cells, 2 * cells), 0)
    spot = lax.broadcasted_iota(jnp.int32, (cells, 2 * cells), 1)
    place = lax.div(at, rows) * (2 * rows) + lax.rem(at, rows)
    pick_source = (spot == place).astype(F32).astype(BF16)
    pick_upstream = (spot == place + rows).astype(F32).astype(BF16)
    mine, theirs = own[...], other[...]
    source = jnp.concatenate([dot(pick_source, mine), dot(pick_source, theirs)], axis=0)
    upstream32 = jnp.concatenate([dot(pick_upstream, mine), dot(pick_upstream, theirs)], axis=0)
    upstream = upstream32.astype(BF16)
    inverse = lax.rsqrt(jnp.mean(source * source, -1, keepdims=True) + 1e-05)
    normed = (source * inverse).astype(BF16)
    covered = jnp.concatenate(
        [
            row_mask(start[...], end[...], scalars[2]),
            row_mask(start[...], end[...], scalars[3]),
        ],
        axis=0,
    )
    query = (dot(normed, heads_in[0]) * covered).astype(BF16)
    keys = (dot(normed, heads_in[1]) * covered).astype(BF16)
    values = (dot(normed, heads_in[2]) * covered).astype(BF16)
    back_out = dot(upstream, heads_out[0], (1, 1)).astype(BF16)
    proj[0] = query
    proj[1] = keys
    proj[2] = values
    proj[3] = back_out

    normed32 = normed.astype(F32)
    for step in range(KINDS):
        last = jnp.bitwise_xor(scalars[1], step) == KINDS - 1
        left_own[step] = jnp.where(last, upstream32[:cells], normed32[:cells]).astype(BF16)
    last = scalars[1] == KINDS - 1
    left_other[...] = jnp.where(last, upstream32[cells:], normed32[cells:]).astype(BF16)

    low = first_heads(cells, 2 * LANES)
    chips = tied.shape[0]
    part = cells // chips
    for pair in range(query.shape[1] // LANES):
        queries, backs = slab(query, pair), slab(back_out, pair)
        key, value = slab(keys, pair), slab(values, pair)
        for odd in range(2):
            keep = jnp.logical_not(low) if odd else low
            logits = dot(jnp.where(keep, queries, 0), key, (1, 1))
            slopes = dot(jnp.where(keep, backs, 0), value, (1, 1))
            both = jnp.concatenate(
                [logits.reshape(chips, part, cells), slopes.reshape(chips, part, cells)], axis=1
            )
            spot = (2 * pair + odd) * 2 * part
            tied[:, spot : spot + 2 * part, :] = both.astype(BF16)


def soften_kernel(parts, copies, *, scale, part):
    total = jnp.sum(parts[...].astype(F32), axis=0)
    blocks = total.reshape(-1, 2 * part, total.shape[-1])
    logits = blocks[:, :part] * scale
    slopes = blocks[:, part:]
    expon = jnp.exp(logits)
    probs = expon / jnp.sum(expon, -1, keepdims=True)
    mixed = scale * probs * (slopes - jnp.sum(probs * slopes, -1, keepdims=True))
    result = jnp.concatenate([probs, mixed], axis=1).reshape(total.shape).astype(BF16)
    for chip in range(copies.shape[0]):
        copies[chip] = result


def attend_kernel(scalars, pairs, proj, start, end, grads):
    cells = proj.shape[1] // 2
    chips = pairs.shape[0]
    part = cells // chips
    covered = jnp.concatenate(
        [
            jnp.broadcast_to(row_mask(start[...], end[...], scalars[2]), (cells, LANES)),
            jnp.broadcast_to(row_mask(start[...], end[...], scalars[3]), (cells, LANES)),
        ],
        axis=1,
    )
    low = first_heads(cells, 2 * LANES)

    def store(kind, pair, first, second, masked):
        result = jnp.where(low, first, second)
        if masked:
            result = result * covered
        result = result.astype(BF16)
        lanes = slice(pair * LANES, (pair + 1) * LANES)
        grads[kind, :cells, lanes] = result[:, :LANES]
        grads[kind, cells:, lanes] = result[:, LANES:]

    for pair in range(proj.shape[2] // LANES):
        probs, mixed = [], []
        for odd in range(2):
            spot = (2 * pair + odd) * 2 * part
            both = pairs[:, spot : spot + 2 * part, :].astype(F32)
            probs.append(both[:, :part].reshape(cells, cells))
            mixed.append(both[:, part:].reshape(cells, cells))
        probs_t = [a.T.astype(BF16) for a in probs]
        mixed_t = [a.T.astype(BF16) for a in mixed]
        probs = [a.astype(BF16) for a in probs]
        mixed = [a.astype(BF16) for a in mixed]
        query, key, value, back = (slab(proj[kind], pair) for kind in range(KINDS))
        store(0, pair, dot(mixed[0], key), dot(mixed[1], key), True)
        store(1, pair, dot(mixed_t[0], query), dot(mixed_t[1], query), True)
        store(2, pair, dot(probs_t[0], back), dot(probs_t[1], back), True)
        store(3, pair, dot(probs[0], value), dot(probs[1], value), False)


def back_kernel(scalars, grads, heads_in, own, other):
    cells = own.shape[0]
    total = dot(grads[0], heads_in[0], (1, 1))
    total = total + dot(grads[1], heads_in[1], (1, 1))
    total = total + dot(grads[2], heads_in[2], (1, 1))
    own[...] = total[:cells]
    other[...] = total[cells:]


def weight_kernel(scalars, *refs):
    lefts_own, lefts_other = refs[:KINDS], refs[KINDS : 2 * KINDS]
    right, right_other, product = refs[2 * KINDS :]
    cells = right.shape[1] // 2
    half = right.shape[2]
    core, kind = scalars[0], scalars[1]

    @pl.when(kind < KINDS - 1)
    def _():
        total = None
        for step in range(KINDS):
            grads = right[jnp.bitwise_xor(kind, step)]
            term = dot(lefts_own[step][...], grads[:cells], (0, 0))
            term = term + dot(lefts_other[step][...], grads[cells:], (0, 0))
            total = term if total is None else total + term
        product[...] = total.astype(BF16)

    for side in range(CORES):

        @pl.when((kind == KINDS - 1) & (core == side))
        def _():
            lanes = slice(side * half, (side + 1) * half)
            mine, theirs = None, None
            for step in range(KINDS):
                chip = jnp.bitwise_xor(kind, step)
                ups = [lefts_own[step][:, lanes], lefts_other[step][:, lanes]]
                term = dot(right[chip, :cells], ups[0], (0, 0))
                term = term + dot(right[chip, cells:], ups[1], (0, 0))
                mine = term if mine is None else mine + term
                term = dot(right_other[chip, cells:], ups[0], (0, 0))
                term = term + dot(right_other[chip, :cells], ups[1], (0, 0))
                theirs = term if theirs is None else theirs + term
            product[side * half : (side + 1) * half, :] = mine.astype(BF16)
            product[(1 - side) * half : (2 - side) * half, :] = theirs.astype(BF16)


def exchange(array, groups):
    return lax.all_to_all(
        array, "read", split_axis=0, concat_axis=0, tiled=True, axis_index_groups=groups
    )


def whole(shape):
    return pl.BlockSpec(shape, lambda i, s: (0,) * len(shape))


def run(kernel, scalars, args, specs, outs):
    return pl.pallas_call(
        kernel,
        grid_spec=pltpu.PrefetchScalarGridSpec(
            num_scalar_prefetch=1,
            grid=(1,),
            in_specs=[spec or whole(arg.shape) for arg, spec in zip(args, specs)],
            out_specs=[whole(out.shape) for out in outs],
        ),
        out_shape=outs,
        compiler_params=pltpu.CompilerParams(vmem_limit_bytes=VMEM_LIMIT),
    )(scalars, *args)


def shards(features, grad_out, weights, read_start, read_end):
    rows, col_dev, width = features.shape
    count = lax.axis_size("read")
    pos_count = lax.axis_size("pos")
    me = lax.axis_index("read")
    pos_at = lax.axis_index("pos")
    scale = 1.0 / math.sqrt(HEAD_DIM * col_dev * pos_count)
    reads = rows * count
    chips = count // CORES
    half = width // CORES
    core = lax.rem(me, CORES)
    kind = lax.rem(me // CORES, KINDS)
    part = reads // chips
    tied_rows = (HEADS // CORES) * 2 * part
    first = pos_at * col_dev
    scalars = jnp.stack([core, kind, first + me, first + jnp.bitwise_xor(me, 1)]).astype(jnp.int32)
    start = read_start.reshape(reads, 1)
    end = read_end.reshape(reads, 1)

    same_core = [list(range(c, count, CORES)) for c in range(CORES)]
    plane = [
        [base + c + CORES * j for j in range(KINDS)]
        for base in range(0, count, CORES * KINDS)
        for c in range(CORES)
    ]

    def swap(array, bits):
        return lax.ppermute(array, "read", [(i, i ^ bits) for i in range(count)])

    shape = jax.ShapeDtypeStruct
    heads_in = pl.BlockSpec((3, width, half), lambda i, s: (0, 0, s[0]))
    heads_out = pl.BlockSpec((1, half, width), lambda i, s: (3, s[0], 0))

    send = jnp.stack([features, grad_out]).transpose(2, 0, 1, 3).reshape(-1, width)
    own = exchange(send, None)
    other = swap(own, 1)
    proj, tied, left_own, left_other = run(
        functools.partial(project_kernel, rows=rows),
        scalars,
        (own, other, weights, weights, start, end),
        (None, None, heads_in, heads_out, None, None),
        (
            shape((KINDS, 2 * reads, half), BF16),
            shape((chips, tied_rows, reads), BF16),
            shape((KINDS, reads, width), BF16),
            shape((reads, width), BF16),
        ),
    )

    parts = exchange(tied, same_core)
    lefts_own = [left_own[0]] + [swap(left_own[k], CORES * k) for k in range(1, KINDS)]
    lefts_other = [left_other] + [swap(a, 1) for a in lefts_own[1:]]
    if pos_count > 1:
        parts = lax.psum(jnp.sum(parts.astype(F32), 0, keepdims=True), "pos")
    copies = pl.pallas_call(
        functools.partial(soften_kernel, scale=scale, part=part),
        out_shape=shape((chips, tied_rows, reads), BF16),
        compiler_params=pltpu.CompilerParams(vmem_limit_bytes=VMEM_LIMIT),
    )(parts)
    pairs = exchange(copies, same_core)

    (grads,) = run(
        attend_kernel,
        scalars,
        (pairs, proj, start, end),
        (None,) * 4,
        (shape((KINDS, 2 * reads, half), BF16),),
    )
    right = exchange(grads, plane)

    grad_own, grad_other = run(
        back_kernel,
        scalars,
        (grads, weights),
        (None, heads_in),
        (shape((reads, width), F32), shape((reads, width), F32)),
    )
    source = own.reshape(count, 2, rows, width)[:, 0].reshape(reads, width).astype(F32)
    inverse = lax.rsqrt(jnp.mean(source * source, -1, keepdims=True) + 1e-05)
    normed = source * inverse
    grad_norm = grad_own + swap(grad_other, 1)
    grad_in = inverse * (grad_norm - normed * jnp.mean(grad_norm * normed, -1, keepdims=True))
    grad_in = exchange(grad_in.astype(BF16), None)
    grad_input = grad_in.reshape(col_dev, rows, width).transpose(1, 0, 2)

    right_other = swap(right, 1)
    (product,) = run(
        weight_kernel,
        scalars,
        (*lefts_own, *lefts_other, right, right_other),
        (None,) * (2 * KINDS + 2),
        (shape((width, half), BF16),),
    )
    pieces = exchange(product.reshape(count, width // count, half), None)
    pieces = pieces.reshape(-1, KINDS, CORES, width // count, half).astype(F32)
    sums = jnp.sum(pieces, 0).transpose(2, 0, 1, 3).reshape(width // count, KINDS * width)
    weight_grads = lax.psum_scatter(sums, "pos", scatter_dimension=0, tiled=True)
    return (grad_input, weight_grads)


def solution(mesh):
    in_specs = (P("read", "pos", None), P("read", "pos", None), P(), P(), P())
    out_specs = (P("read", "pos", None), P(("read", "pos"), None))
    return jax.shard_map(shards, mesh=mesh, in_specs=in_specs, out_specs=out_specs, check_vma=False)
```

time: 194 us -> 116 us (0.60)
  local copies, waits for them, and re-layouts: 61.7 us -> 5.76 us
  matrix products: 22 us -> 0 us
  blocking collectives: 20.4 us -> 36.9 us
  Pallas kernels: 0 us -> 12.6 us
  other arithmetic: 13.8 us -> 2.72 us
  waiting for transfers between devices: 47.6 us -> 38.2 us
  starting transfers between devices: 26 us -> 18.5 us
    dot_general x14 -> x0, matrix products: 22 us -> none  [the longest x4 6.6 us: dot_back(): lax.dot_general(left, right, (((1,), (1,)), ((), ())), preferred_element_...]
    convert_element_type x12 -> x2, local copies, waits for them, and re-layouts: 18.3 us -> 0.39 us  [shards(): own.reshape(count, 2, rows, width)[:, 0].reshape(reads, width).astype(F32)]
    all_to_all x1 -> x2, blocking collectives: 20.4 us -> 36.9 us  [exchange(): lax.all_to_all(array, 'read', split_axis=0, concat_axis=0, tiled=True, ax...]
    another operation x10 -> x0, local copies, waits for them, and re-layouts: 13.5 us -> none  [the longest x4 6.92 us: shards(): jnp.stack([grad_query, grad_keys, grad_values, output])]
    pallas_call x0 -> x5, Pallas kernels: none -> 12.6 us  [the longest x4 11.7 us: run(): pl.pallas_call(kernel, grid_spec=pltpu.PrefetchScalarGridSpec(num_scalar_...]
    all_to_all x6 -> x4, starting transfers between devices: 25.8 us -> 14.3 us  [exchange(): lax.all_to_all(array, 'read', split_axis=0, concat_axis=0, tiled=True, ax...]
    all_to_all x6 -> x4, waiting for transfers between devices: 47.6 us -> 36.2 us  [exchange(): lax.all_to_all(array, 'read', split_axis=0, concat_axis=0, tiled=True, ax...]
    slice x8 -> x0, local copies, waits for them, and re-layouts: 8.6 us -> none  [the longest x1 2.41 us: shards(): heads_out = lax.dynamic_slice_in_dim(weights[3], core * half, half, 0)]
  transfers between devices with their start and end apart: 10 -> 13, of which waited for: 5 -> 9; matrix products, arithmetic and copies ran while one was open for 27% -> 5% of each run, Pallas kernels for 0% -> 2%
where the time goes in v2:
time: 116 us; the launch traced here: 115 us
  waiting for transfers between devices  38.2 us (33%)
  blocking collectives  36.9 us (32%)
  starting transfers between devices  18.5 us (16%)
  Pallas kernels  12.6 us (11%)
  local copies, waits for them, and re-layouts  5.76 us (5%)
  other arithmetic  2.72 us (2%)
    all_to_all x2, blocking collectives, exchange(): lax.all_to_all(array, 'read', split_axis=0, concat_axis=0, tiled=True, ax...  36.9 us
    all_to_all x4, waiting for transfers between devices, exchange(): lax.all_to_all(array, 'read', split_axis=0, concat_axis=0, tiled=True, ax...  36.2 us
    all_to_all x4, starting transfers between devices, exchange(): lax.all_to_all(array, 'read', split_axis=0, concat_axis=0, tiled=True, ax...  14.3 us
    pallas_call x4, Pallas kernels, run(): pl.pallas_call(kernel, grid_spec=pltpu.PrefetchScalarGridSpec(num_scalar_...  11.7 us
    ppermute x9, starting transfers between devices, swap(): return lax.ppermute(array, 'read', [(i, i ^ bits) for i in range(count)])  4.17 us
  transfers between devices with their start and end apart: 13, of which 9 were waited for; matrix products, arithmetic and copies ran while one was open for 5% of the time, Pallas kernels for 2%

profile of v2, /device:TPU:0, one launch (start us, length us, event | category | flops | bytes accessed | tf_op | source)
XLA Modules:
  0.0 115.4 jit_solution(8701574384543840964)
XLA Ops:
  0.6 1.1 pad_maximum_fusion
  1.7 0.2 copy.39
  1.9 20.3 %all_to_all.40 = bf16[32,8,768]{2,1,0:T(8,128)(2,1)S(1)} all-to-all(bf16[32,8,768]{2,1,0:T(8,128)(2,1)S(1)} %copy.39), channel_id=1, replica_groups=mesh['read'=32,'pos'=1] {'read'}, dimensions={0} | all-to-all | bytes 786432 | tf_op jit(solution)/shard_map/all_to_all | solution.py:197
  22.2 0.0 collective-permute-start
  22.2 0.8 copy.32.start
  23.0 0.8 copy.33.end
  23.7 0.1 pad_add_fusion.scalars
  23.8 0.1 collective-permute-done.other
  23.9 3.8 %shard_map.68 = (bf16[4,256,384]{2,1,0:T(8,128)(2,1)S(1)}, bf16[16,96,128]{2,1,0:T(8,128)(2,1)S(1)}, bf16[4,128,768]{2,1,0:T(8,128)(2,1)S(1)}, bf16[128,768]{1,0:T(8,128)(2,1)S(1)}) custom-call(s32[4]{0:T(128)S(1)} %pad_add_fusion.scalars, bf16[256,768]{1,0:T(8,128)(2,1)S(1)} %bitcast.29, bf16[256,768]{1,0:T(8,128)(2,1)S(1)} %collective-permute-done.other, ...), custom_call_target="tpu_custom_call" | custom-call | tf_op jit(solution)/shard_map/pallas_call | solution.py:207
  27.7 16.6 %all_to_all.41.parts = bf16[16,96,128]{2,1,0:T(8,128)(2,1)S(1)} all-to-all(bf16[16,96,128]{2,1,0:T(8,128)(2,1)S(1)} %get-tuple-element.8), channel_id=1, replica_groups={{0,2,4,6,8,10,12,14,16,18,20,22,24,26,28,30},{1,3,5,7,9,11,13,15,17,19,..., dimensions={0} | all-to-all | bytes 786432 | tf_op jit(solution)/shard_map/all_to_all | solution.py:197
  44.3 1.0 shard_map.69
  45.3 3.6 %all-to-all-start.2 = ((bf16[16,96,128]{2,1,0:T(8,128)(2,1)}), bf16[16,96,128]{2,1,0:T(8,128)(2,1)S(1)}, u32[]{:S(2)}, u32[]{:S(2)}) async-start(bf16[16,96,128]{2,1,0:T(8,128)(2,1)} %shard_map.69), calls=%async_computation.2 | async-start | bytes 786432 | tf_op jit(solution)/shard_map/all_to_all | solution.py:197
  48.9 0.1 copy.30
  49.0 0.1 multiply_reduce_fusion.1
  49.2 11.8 %all-to-all-done.2.pairs = bf16[16,96,128]{2,1,0:T(8,128)(2,1)S(1)} async-done(((bf16[16,96,128]{2,1,0:T(8,128)(2,1)}), bf16[16,96,128]{2,1,0:T(8,128)(2,1)S(1)}, u32[]{:S(2)}, u32[]{:S(2)}) %all-to-all-start.2) | async-done | bytes 393248 | tf_op jit(solution)/shard_map/all_to_all | solution.py:197
  61.0 2.0 %shard_map.70.grads = bf16[4,256,384]{2,1,0:T(8,128)(2,1)} custom-call(s32[4]{0:T(128)S(1)} %pad_add_fusion.scalars, bf16[16,96,128]{2,1,0:T(8,128)(2,1)S(1)} %all-to-all-done.2.pairs, bf16[4,256,384]{2,1,0:T(8,128)(2,1)S(1)} %get-tuple-element.9.proj, s32[128,1]{1,0:T(8,128)S(1)} %copy.32.start, s32[128,1]{1,0:T(8,128)S(1)} %copy.33.end), custom_call_target="tpu_custom_call" | custom-call | tf_op jit(solution)/shard_map/pallas_call | solution.py:207
  63.0 3.0 %shard_map.71 = (f32[128,768]{1,0:T(8,128)S(1)}, f32[128,768]{1,0:T(8,128)S(1)}) custom-call(s32[4]{0:T(128)S(1)} %pad_add_fusion.scalars, bf16[4,256,384]{2,1,0:T(8,128)(2,1)} %shard_map.70.grads, bf16[4,768,768]{2,1,0:T(8,128)(2,1)} %heads_in.3), custom_call_target="tpu_custom_call" | custom-call | tf_op jit(solution)/shard_map/pallas_call | solution.py:207
  66.1 3.5 %all-to-all-start.4 = ((bf16[4,256,384]{2,1,0:T(8,128)(2,1)}), bf16[4,256,384]{2,1,0:T(8,128)(2,1)S(1)}, u32[]{:S(2)}, u32[]{:S(2)}) async-start(bf16[4,256,384]{2,1,0:T(8,128)(2,1)} %shard_map.70.grads), calls=%async_computation.4 | async-start | bytes 1572864 | tf_op jit(solution)/shard_map/all_to_all | solution.py:197
  69.6 0.1 collective-permute-start.1
  69.7 0.3 copy.36
  69.9 0.1 reshape.61
  70.1 0.1 copy.31
  70.2 0.1 rsqrt.12
  70.3 0.8 slice_bitcast_fusion
  71.1 1.9 %collective-permute-start.2 = (bf16[128,768]{1,0:T(8,128)(2,1)}, bf16[128,768]{1,0:T(8,128)(2,1)S(1)}, u32[]{:S(2)}, u32[]{:S(2)}) collective-permute-start(bf16[128,768]{1,0:T(8,128)(2,1)} %get-tuple-element.22), channel_id=1, source_target_pairs={{0,2},{1,3},{2,0},{3,1},{4,6},{5,7},{6,4},{7,5},{8,10},{9,11},{10,... | collective-permute-start | bytes 589832 | tf_op jit(solution)/shard_map/ppermute | solution.py:247
  73.0 1.5 %collective-permute-start.3 = (bf16[128,768]{1,0:T(8,128)(2,1)}, bf16[128,768]{1,0:T(8,128)(2,1)S(1)}, u32[]{:S(2)}, u32[]{:S(2)}) collective-permute-start(bf16[128,768]{1,0:T(8,128)(2,1)} %get-tuple-element.21), channel_id=1, source_target_pairs={{0,4},{1,5},{2,6},{3,7},{4,0},{5,1},{6,2},{7,3},{8,12},{9,13},{10,... | collective-permute-start | bytes 589832 | tf_op jit(solution)/shard_map/ppermute | solution.py:247
  74.5 0.1 collective-permute-start.4
  74.6 0.0 collective-permute-done.1
  74.6 1.2 %multiply_reduce_fusion = (f32[128]{0:T(128)S(1)}, f32[128,768]{1,0:T(8,128)S(1)}) fusion(f32[128,768]{1,0:T(8,128)S(1)} %reshape.61, f32[128]{0:T(128)S(1)} %rsqrt.12, f32[128,768]{1,0:T(8,128)S(1)} %get-tuple-element.10, f32[128,768]{1,0:T(8,128)} %collective-permute-done.1), kind=kLoop, calls=%fused_computation.3 | loop fusion | flops 393088 | bytes 1573888 | tf_op jit(solution)/shard_map/reduce_sum | solution.py:301
  75.8 4.7 %all-to-all-done.4.refs_8_ = bf16[4,256,384]{2,1,0:T(8,128)(2,1)S(1)} async-done(((bf16[4,256,384]{2,1,0:T(8,128)(2,1)}), bf16[4,256,384]{2,1,0:T(8,128)(2,1)S(1)}, u32[]{:S(2)}, u32[]{:S(2)}) %all-to-all-start.4) | async-done | bytes 786464 | tf_op jit(solution)/shard_map/all_to_all | solution.py:197
  80.5 0.0 collective-permute-start.8
  80.5 0.1 multiply_convert_fusion
  80.7 0.7 all_to_all.30
  81.4 4.5 %all-to-all-start.3 = ((bf16[32,4,768]{2,1,0:T(4,128)(2,1)}), bf16[32,4,768]{2,1,0:T(4,128)(2,1)S(1)}, u32[]{:S(2)}, u32[]{:S(2)}) async-start(bf16[32,4,768]{2,1,0:T(4,128)(2,1)} %all_to_all.30), calls=%async_computation.3 | async-start | bytes 393216 | tf_op jit(solution)/shard_map/all_to_all | solution.py:197
  85.9 0.3 collective-permute-start.5
  86.2 0.3 collective-permute-start.6
  86.5 0.4 collective-permute-done.4.refs_3_
  86.9 0.5 collective-permute-done.5.refs_5_
  87.4 0.3 collective-permute-done.6.refs_6_
  87.7 0.7 collective-permute-done.7.refs_7_
  88.3 2.8 %shard_map.72 = bf16[768,384]{1,0:T(8,128)(2,1)} custom-call(s32[4]{0:T(128)S(1)} %pad_add_fusion.scalars, bf16[128,768]{1,0:T(8,128)(2,1)S(1)} %get-tuple-element.23.refs_0_, bf16[128,768]{1,0:T(8,128)(2,1)S(1)} %collective-permute-done.2.refs_1_, bf16[128,768]{1,0:T(8,128)(2,1)S(1)} %collective-permute-done.3.refs_2_, ...), custom_call_target="tpu_custom_call" | custom-call | tf_op jit(solution)/shard_map/pallas_call | solution.py:207
  91.1 3.6 %all-to-all-done.3 = bf16[32,4,768]{2,1,0:T(4,128)(2,1)S(1)} async-done(((bf16[32,4,768]{2,1,0:T(4,128)(2,1)}), bf16[32,4,768]{2,1,0:T(4,128)(2,1)S(1)}, u32[]{:S(2)}, u32[]{:S(2)}) %all-to-all-start.3) | async-done | bytes 196640 | tf_op jit(solution)/shard_map/all_to_all | solution.py:197
  94.8 2.7 %all-to-all-start.5 = ((bf16[32,24,384]{2,1,0:T(8,128)(2,1)}), bf16[32,24,384]{2,1,0:T(8,128)(2,1)S(1)}, u32[]{:S(2)}, u32[]{:S(2)}) async-start(bf16[32,24,384]{2,1,0:T(8,128)(2,1)} %bitcast.17), calls=%async_computation.5 | async-start | bytes 1179648 | tf_op jit(solution)/shard_map/all_to_all | solution.py:197
  97.5 0.7 copy.38
  98.2 16.0 %all-to-all-done.5 = bf16[32,24,384]{2,1,0:T(8,128)(2,1)S(1)} async-done(((bf16[32,24,384]{2,1,0:T(8,128)(2,1)}), bf16[32,24,384]{2,1,0:T(8,128)(2,1)S(1)}, u32[]{:S(2)}, u32[]{:S(2)}) %all-to-all-start.5) | async-done | bytes 589856 | tf_op jit(solution)/shard_map/all_to_all | solution.py:197
  114.2 0.1 convert_reduce_fusion
  114.3 0.2 copy.37
  114.5 1.0 reshape.60
  (7 shorter events, 0.0 us)
Async XLA Ops:
  22.2 1.7 %collective-permute-start = (bf16[256,768]{1,0:T(8,128)(2,1)S(1)}, bf16[256,768]{1,0:T(8,128)(2,1)S(1)}, u32[]{:S(2)}, u32[]{:S(2)}) collective-permute-start(bf16[256,768]{1,0:T(8,128)(2,1)S(1)} %bitcast.28), channel_id=1, source_target_pairs={{0,1},{1,0},{2,3},{3,2},{4,5},{5,4},{6,7},{7,6},{8,9},{9,8},{10,11... | collective-permute-start | bytes 1179656 | tf_op jit(solution)/shard_map/ppermute | solution.py:247
  45.3 15.7 %all-to-all-start.2 = ((bf16[16,96,128]{2,1,0:T(8,128)(2,1)}), bf16[16,96,128]{2,1,0:T(8,128)(2,1)S(1)}, u32[]{:S(2)}, u32[]{:S(2)}) async-start(bf16[16,96,128]{2,1,0:T(8,128)(2,1)} %shard_map.69), calls=%async_computation.2 | async-start | bytes 786432 | tf_op jit(solution)/shard_map/all_to_all | solution.py:197
  66.1 14.5 %all-to-all-start.4 = ((bf16[4,256,384]{2,1,0:T(8,128)(2,1)}), bf16[4,256,384]{2,1,0:T(8,128)(2,1)S(1)}, u32[]{:S(2)}, u32[]{:S(2)}) async-start(bf16[4,256,384]{2,1,0:T(8,128)(2,1)} %shard_map.70.grads), calls=%async_computation.4 | async-start | bytes 1572864 | tf_op jit(solution)/shard_map/all_to_all | solution.py:197
  69.6 5.0 %collective-permute-start.1 = (f32[128,768]{1,0:T(8,128)S(1)}, f32[128,768]{1,0:T(8,128)}, u32[]{:S(2)}, u32[]{:S(2)}) collective-permute-start(f32[128,768]{1,0:T(8,128)S(1)} %get-tuple-element.11), channel_id=1, source_target_pairs={{0,1},{1,0},{2,3},{3,2},{4,5},{5,4},{6,7},{7,6},{8,9},{9,8},{10,11... | collective-permute-start | bytes 1179656 | tf_op jit(solution)/shard_map/ppermute | solution.py:247
  71.1 14.8 %collective-permute-start.2 = (bf16[128,768]{1,0:T(8,128)(2,1)}, bf16[128,768]{1,0:T(8,128)(2,1)S(1)}, u32[]{:S(2)}, u32[]{:S(2)}) collective-permute-start(bf16[128,768]{1,0:T(8,128)(2,1)} %get-tuple-element.22), channel_id=1, source_target_pairs={{0,2},{1,3},{2,0},{3,1},{4,6},{5,7},{6,4},{7,5},{8,10},{9,11},{10,... | collective-permute-start | bytes 589832 | tf_op jit(solution)/shard_map/ppermute | solution.py:247
  73.0 13.2 %collective-permute-start.3 = (bf16[128,768]{1,0:T(8,128)(2,1)}, bf16[128,768]{1,0:T(8,128)(2,1)S(1)}, u32[]{:S(2)}, u32[]{:S(2)}) collective-permute-start(bf16[128,768]{1,0:T(8,128)(2,1)} %get-tuple-element.21), channel_id=1, source_target_pairs={{0,4},{1,5},{2,6},{3,7},{4,0},{5,1},{6,2},{7,3},{8,12},{9,13},{10,... | collective-permute-start | bytes 589832 | tf_op jit(solution)/shard_map/ppermute | solution.py:247
  74.5 12.4 %collective-permute-start.4 = (bf16[128,768]{1,0:T(8,128)(2,1)}, bf16[128,768]{1,0:T(8,128)(2,1)S(1)}, u32[]{:S(2)}, u32[]{:S(2)}) collective-permute-start(bf16[128,768]{1,0:T(8,128)(2,1)} %get-tuple-element.20), channel_id=1, source_target_pairs={{0,6},{1,7},{2,4},{3,5},{4,2},{5,3},{6,0},{7,1},{8,14},{9,15},{10,... | collective-permute-start | bytes 589832 | tf_op jit(solution)/shard_map/ppermute | solution.py:247
  80.5 7.8 %collective-permute-start.8 = (bf16[4,256,384]{2,1,0:T(8,128)(2,1)S(1)}, bf16[4,256,384]{2,1,0:T(8,128)(2,1)S(1)}, u32[]{:S(2)}, u32[]{:S(2)}) collective-permute-start(bf16[4,256,384]{2,1,0:T(8,128)(2,1)S(1)} %all-to-all-done.4.refs_8_), channel_id=1, source_target_pairs={{0,1},{1,0},{2,3},{3,2},{4,5},{5,4},{6,7},{7,6},{8,9},{9,8},{10,11... | collective-permute-start | bytes 2359304 | tf_op jit(solution)/shard_map/ppermute | solution.py:247
  81.4 13.4 %all-to-all-start.3 = ((bf16[32,4,768]{2,1,0:T(4,128)(2,1)}), bf16[32,4,768]{2,1,0:T(4,128)(2,1)S(1)}, u32[]{:S(2)}, u32[]{:S(2)}) async-start(bf16[32,4,768]{2,1,0:T(4,128)(2,1)} %all_to_all.30), calls=%async_computation.3 | async-start | bytes 393216 | tf_op jit(solution)/shard_map/all_to_all | solution.py:197
  85.9 1.5 %collective-permute-start.5 = (bf16[128,768]{1,0:T(8,128)(2,1)S(1)}, bf16[128,768]{1,0:T(8,128)(2,1)S(1)}, u32[]{:S(2)}, u32[]{:S(2)}) collective-permute-start(bf16[128,768]{1,0:T(8,128)(2,1)S(1)} %collective-permute-done.2.refs_1_), channel_id=1, source_target_pairs={{0,1},{1,0},{2,3},{3,2},{4,5},{5,4},{6,7},{7,6},{8,9},{9,8},{10,11... | collective-permute-start | bytes 589832 | tf_op jit(solution)/shard_map/ppermute | solution.py:247
  86.2 1.5 %collective-permute-start.6 = (bf16[128,768]{1,0:T(8,128)(2,1)S(1)}, bf16[128,768]{1,0:T(8,128)(2,1)S(1)}, u32[]{:S(2)}, u32[]{:S(2)}) collective-permute-start(bf16[128,768]{1,0:T(8,128)(2,1)S(1)} %collective-permute-done.3.refs_2_), channel_id=1, source_target_pairs={{0,1},{1,0},{2,3},{3,2},{4,5},{5,4},{6,7},{7,6},{8,9},{9,8},{10,11... | collective-permute-start | bytes 589832 | tf_op jit(solution)/shard_map/ppermute | solution.py:247
  86.9 1.4 %collective-permute-start.7 = (bf16[128,768]{1,0:T(8,128)(2,1)S(1)}, bf16[128,768]{1,0:T(8,128)(2,1)S(1)}, u32[]{:S(2)}, u32[]{:S(2)}) collective-permute-start(bf16[128,768]{1,0:T(8,128)(2,1)S(1)} %collective-permute-done.4.refs_3_), channel_id=1, source_target_pairs={{0,1},{1,0},{2,3},{3,2},{4,5},{5,4},{6,7},{7,6},{8,9},{9,8},{10,11... | collective-permute-start | bytes 589832 | tf_op jit(solution)/shard_map/ppermute | solution.py:247
  94.8 19.5 %all-to-all-start.5 = ((bf16[32,24,384]{2,1,0:T(8,128)(2,1)}), bf16[32,24,384]{2,1,0:T(8,128)(2,1)S(1)}, u32[]{:S(2)}, u32[]{:S(2)}) async-start(bf16[32,24,384]{2,1,0:T(8,128)(2,1)} %bitcast.17), calls=%async_computation.5 | async-start | bytes 1179648 | tf_op jit(solution)/shard_map/all_to_all | solution.py:197

commit v3 on v2

v3 whole, which is shorter than its diff:
```python
import functools
import math

import jax
import jax.numpy as jnp
from jax import lax
from jax.experimental import pallas as pl
from jax.experimental.pallas import tpu as pltpu
from jax.sharding import PartitionSpec as P

HEADS = 12
HEAD_DIM = 64
CORES = 2
KINDS = 4
LANES = 128
VMEM_LIMIT = 48 * 1024 * 1024

BF16 = jnp.bfloat16
F32 = jnp.float32


def dot(left, right, contract=(1, 0)):
    return lax.dot_general(
        left, right, (((contract[0],), (contract[1],)), ((), ())), preferred_element_type=F32
    )


def upright(lanes):
    size = lanes.shape[1]
    rows = lax.broadcasted_iota(jnp.int32, (size, size), 0)
    cols = lax.broadcasted_iota(jnp.int32, (size, size), 1)
    spread = jnp.broadcast_to(lanes.astype(F32), (size, size))
    return jnp.sum(jnp.where(rows == cols, spread, 0.0), -1, keepdims=True)


def row_mask(start, end, column):
    column = column.astype(F32)
    return ((start <= column) & (column < end)).astype(F32)


def first_heads(rows, lanes):
    at = lax.broadcasted_iota(jnp.int32, (rows, lanes), 1)
    return lax.rem(at, LANES) < HEAD_DIM


def slab(array, at):
    reads = array.shape[0] // 2
    lanes = slice(at * LANES, (at + 1) * LANES)
    return jnp.concatenate([array[:reads, lanes], array[reads:, lanes]], axis=1)


def indicator(rows, cols, place):
    at = lax.broadcasted_iota(jnp.int32, (rows, cols), 0)
    spot = lax.broadcasted_iota(jnp.int32, (rows, cols), 1)
    return place(at, spot).astype(F32).astype(BF16)


def project_kernel(
    scalars, own, other, heads_in, heads_out, start, end, proj, tied, normed_own, inverse_own,
    left_other, *pieces, rows
):
    ops, lefts = pieces[:KINDS], pieces[KINDS:]
    cells = own.shape[0] // 2

    def pick(shift):
        return indicator(
            cells,
            2 * cells,
            lambda at, spot: spot == lax.div(at, rows) * (2 * rows) + lax.rem(at, rows) + shift,
        )

    mine, theirs = own[...], other[...]
    source = jnp.concatenate([dot(pick(0), mine), dot(pick(0), theirs)], axis=0)
    upstream = jnp.concatenate([dot(pick(rows), mine), dot(pick(rows), theirs)], axis=0)
    upstream = upstream.astype(BF16)
    inverse = lax.rsqrt(jnp.mean(source * source, -1, keepdims=True) + 1e-05)
    normed32 = source * inverse
    normed = normed32.astype(BF16)
    normed_own[...] = normed32[:cells]
    inverse_own[...] = jnp.broadcast_to(inverse[:cells], inverse_own.shape)
    first, last = upright(start[...]), upright(end[...])
    covered = jnp.concatenate(
        [row_mask(first, last, scalars[2]), row_mask(first, last, scalars[3])], axis=0
    )
    query = (dot(normed, heads_in[0]) * covered).astype(BF16)
    keys = (dot(normed, heads_in[1]) * covered).astype(BF16)
    values = (dot(normed, heads_in[2]) * covered).astype(BF16)
    back_out = dot(upstream, heads_out[0], (1, 1)).astype(BF16)
    proj[0] = query
    proj[1] = keys
    proj[2] = values
    proj[3] = back_out

    for kind in range(KINDS):

        @pl.when(scalars[1] == kind)
        def _():
            needs = (keys, query, back_out, values)
            for step in range(KINDS):
                ops[step][...] = needs[kind ^ step]
                side = upstream if kind ^ step == KINDS - 1 else normed
                lefts[step][...] = side[:cells]
                if step == 0:
                    left_other[...] = side[cells:]

    low = first_heads(cells, 2 * LANES)
    chips = tied.shape[0]
    part = cells // chips
    for pair in range(query.shape[1] // LANES):
        queries, backs = slab(query, pair), slab(back_out, pair)
        key, value = slab(keys, pair), slab(values, pair)
        for odd in range(2):
            keep = jnp.logical_not(low) if odd else low
            logits = dot(jnp.where(keep, queries, 0), key, (1, 1))
            slopes = dot(jnp.where(keep, backs, 0), value, (1, 1))
            both = jnp.concatenate(
                [logits.reshape(chips, part, cells), slopes.reshape(chips, part, cells)], axis=1
            )
            spot = (2 * pair + odd) * 2 * part
            tied[:, spot : spot + 2 * part, :] = both.astype(BF16)


def soften_kernel(parts, copies, *, scale, part):
    total = jnp.sum(parts[...].astype(F32), axis=0)
    blocks = total.reshape(-1, 2 * part, total.shape[-1])
    logits = blocks[:, :part] * scale
    slopes = blocks[:, part:]
    expon = jnp.exp(logits)
    probs = expon / jnp.sum(expon, -1, keepdims=True)
    mixed = scale * probs * (slopes - jnp.sum(probs * slopes, -1, keepdims=True))
    result = jnp.concatenate([probs, mixed], axis=1).reshape(total.shape).astype(BF16)
    for chip in range(copies.shape[0]):
        copies[chip] = result


def head_maps(pairs, head, cells):
    part = cells // pairs.shape[0]
    both = pairs[:, head * 2 * part : (head + 1) * 2 * part, :].astype(F32)
    return both[:, :part].reshape(cells, cells), both[:, part:].reshape(cells, cells)


def back_kernel(scalars, pairs, proj, heads_in, start, end, own, other, grads):
    cells = proj.shape[1] // 2
    first, last = upright(start[...]), upright(end[...])
    covered = jnp.concatenate(
        [
            jnp.broadcast_to(row_mask(first, last, scalars[2]), (cells, LANES)),
            jnp.broadcast_to(row_mask(first, last, scalars[3]), (cells, LANES)),
        ],
        axis=1,
    )
    low = first_heads(cells, 2 * LANES)
    for pair in range(proj.shape[2] // LANES):
        lanes = slice(pair * LANES, (pair + 1) * LANES)

        def store(kind, one, two):
            result = (jnp.where(low, one, two) * covered).astype(BF16)
            grads[kind, :cells, lanes] = result[:, :LANES]
            grads[kind, cells:, lanes] = result[:, LANES:]

        maps = [head_maps(pairs, 2 * pair + odd, cells) for odd in range(2)]
        probs_t = [a.T.astype(BF16) for a, _ in maps]
        mixed_t = [b.T.astype(BF16) for _, b in maps]
        mixed = [b.astype(BF16) for _, b in maps]
        query, key, back = slab(proj[0], pair), slab(proj[1], pair), slab(proj[3], pair)
        store(0, dot(mixed[0], key), dot(mixed[1], key))
        store(1, dot(mixed_t[0], query), dot(mixed_t[1], query))
        store(2, dot(probs_t[0], back), dot(probs_t[1], back))

    total = dot(grads[0], heads_in[0], (1, 1))
    total = total + dot(grads[1], heads_in[1], (1, 1))
    total = total + dot(grads[2], heads_in[2], (1, 1))
    own[...] = total[:cells]
    other[...] = total[cells:]


def weight_kernel(scalars, pairs, pairs_other, start, end, *refs):
    ops, ops_other, lefts, lefts_other = (
        refs[at * KINDS : (at + 1) * KINDS] for at in range(4)
    )
    product, right, right_other = refs[4 * KINDS :]
    cells, width = lefts[0].shape
    half = ops[0].shape[1]
    core, kind = scalars[0], scalars[1]
    low = first_heads(cells, 2 * KINDS * LANES)
    use_probs = kind >= 2
    use_flip = (kind == 1) | (kind == 2)

    def gradient(source, operands, covered, out, swapped):
        for pair in range(half // LANES):
            cat = jnp.concatenate([slab(operand[...], pair) for operand in operands], axis=1)
            sides = []
            for odd in range(2):
                probs, mixed = head_maps(source, 2 * pair + odd, cells)
                if swapped:
                    chosen = probs
                else:
                    chosen = jnp.where(use_probs, probs, mixed)
                    chosen = jnp.where(use_flip, chosen.T, chosen)
                sides.append(dot(chosen.astype(BF16), cat))
            result = jnp.where(low, sides[0], sides[1])
            if covered is not None:
                result = result * covered
            result = result.astype(BF16)
            lanes = slice(pair * LANES, (pair + 1) * LANES)
            for at in range(2 * KINDS):
                to = at ^ 1 if swapped else at
                out[to * cells : (to + 1) * cells, lanes] = result[
                    :, at * LANES : (at + 1) * LANES
                ]

    first, last = upright(start[...]), upright(end[...])
    masks = []
    for step in range(KINDS):
        for side in range(2):
            mask = row_mask(first, last, scalars[4 + 2 * step + side])
            masks.append(jnp.broadcast_to(mask, (cells, LANES)))
    covered = jnp.concatenate(masks, axis=1)
    covered = jnp.where(kind == KINDS - 1, 1.0, covered)
    gradient(pairs, ops, covered, right, False)

    @pl.when(kind < KINDS - 1)
    def _():
        left = jnp.concatenate(
            [ref[...] for pair in zip(lefts, lefts_other) for ref in pair], axis=0
        )
        product[...] = dot(left, right[...], (0, 0)).astype(BF16)

    @pl.when(kind == KINDS - 1)
    def _():
        gradient(pairs_other, ops_other, None, right_other, True)
        for side in range(CORES):

            @pl.when(core == side)
            def _():
                lanes = slice(side * half, (side + 1) * half)
                ups = jnp.concatenate(
                    [ref[:, lanes] for pair in zip(lefts, lefts_other) for ref in pair], axis=0
                )
                mine = dot(right[...], ups, (0, 0)).astype(BF16)
                theirs = dot(right_other[...], ups, (0, 0)).astype(BF16)
                product[side * half : (side + 1) * half, :] = mine
                product[(1 - side) * half : (2 - side) * half, :] = theirs


def pack_kernel(grad_own, grad_recv, normed, inverse, product, payload, *, rows):
    cells, width = normed.shape
    tiles = width // LANES
    half = product.shape[1]
    group = rows * tiles
    grad_norm = grad_own[...] + grad_recv[...]
    mean = jnp.mean(grad_norm * normed[...], -1, keepdims=True)
    result = (grad_norm - normed[...] * mean) * inverse[:, :1]
    result = result.astype(BF16)
    stack = jnp.concatenate(
        [result[:, t * LANES : (t + 1) * LANES] for t in range(tiles)], axis=0
    )

    def place(at, spot):
        tile, cell = lax.div(spot, cells), lax.rem(spot, cells)
        return at == lax.div(cell, rows) * group + tile * rows + lax.rem(cell, rows)

    payload[:, :half] = product[...]
    payload[:, half:] = dot(indicator(width, tiles * cells, place), stack).astype(BF16)


def finish_kernel(arrived, grad_input, sums):
    count, chunk, wide = arrived.shape
    rows, cols, width = grad_input.shape
    half = wide - LANES
    group = KINDS * CORES
    for kind in range(KINDS):
        for core in range(CORES):
            total = None
            for base in range(0, count, group):
                term = arrived[base + kind * CORES + core, :, :half].astype(F32)
                total = term if total is None else total + term
            spot = kind * width + core * half
            sums[:, spot : spot + half] = total
    flat = arrived[:, :, half:].astype(F32).reshape(count * chunk, LANES).astype(BF16)
    cells = rows * cols

    def place(at, spot):
        tile, cell = lax.div(at, cells), lax.rem(at, cells)
        return spot == lax.rem(cell, cols) * chunk + tile * rows + lax.div(cell, cols)

    tiles = width // LANES
    moved = dot(indicator(tiles * cells, count * chunk, place), flat).astype(BF16)
    for tile in range(tiles):
        for row in range(rows):
            spot = tile * cells + row * cols
            grad_input[row, :, tile * LANES : (tile + 1) * LANES] = moved[spot : spot + cols]


def exchange(array, groups):
    return lax.all_to_all(
        array, "read", split_axis=0, concat_axis=0, tiled=True, axis_index_groups=groups
    )


def whole(shape):
    return pl.BlockSpec(shape, lambda i, s: (0,) * len(shape))


def call(kernel, scalars, args, outs, specs=None, scratch=()):
    specs = specs or {}
    return pl.pallas_call(
        kernel,
        grid_spec=pltpu.PrefetchScalarGridSpec(
            num_scalar_prefetch=1,
            grid=(1,),
            in_specs=[specs.get(at) or whole(arg.shape) for at, arg in enumerate(args)],
            out_specs=[whole(out.shape) for out in outs],
            scratch_shapes=scratch,
        ),
        out_shape=outs,
        compiler_params=pltpu.CompilerParams(vmem_limit_bytes=VMEM_LIMIT),
    )(scalars, *args)


def simple(kernel, args, outs):
    return pl.pallas_call(
        kernel,
        out_shape=outs,
        compiler_params=pltpu.CompilerParams(vmem_limit_bytes=VMEM_LIMIT),
    )(*args)


def shards(features, grad_out, weights, read_start, read_end):
    rows, col_dev, width = features.shape
    count = lax.axis_size("read")
    pos_count = lax.axis_size("pos")
    me = lax.axis_index("read")
    pos_at = lax.axis_index("pos")
    scale = 1.0 / math.sqrt(HEAD_DIM * col_dev * pos_count)
    reads = rows * count
    chips = count // CORES
    half = width // CORES
    part = reads // chips
    tied_rows = (HEADS // CORES) * 2 * part
    chunk = width // count
    first = pos_at * col_dev
    core = jnp.bitwise_and(me, CORES - 1)
    kind = jnp.bitwise_and(jnp.right_shift(me, 1), KINDS - 1)
    columns = [first + jnp.bitwise_xor(me, at) for at in range(CORES * KINDS)]
    scalars = jnp.stack([core, kind, columns[0], columns[1], *columns]).astype(jnp.int32)
    start = read_start.reshape(1, reads)
    end = read_end.reshape(1, reads)

    same_core = [list(range(c, count, CORES)) for c in range(CORES)]

    def swap(array, bits):
        return lax.ppermute(array, "read", [(i, i ^ bits) for i in range(count)])

    shape = jax.ShapeDtypeStruct
    heads_in = pl.BlockSpec((3, width, half), lambda i, s: (0, 0, s[0]))
    heads_out = pl.BlockSpec((1, half, width), lambda i, s: (3, s[0], 0))

    send = jnp.stack([features, grad_out]).transpose(2, 0, 1, 3).reshape(-1, width)
    own = exchange(send, None)
    other = swap(own, 1)
    proj, tied, normed, inverse, left_other, *pieces = call(
        functools.partial(project_kernel, rows=rows),
        scalars,
        (own, other, weights, weights, start, end),
        (
            shape((KINDS, 2 * reads, half), BF16),
            shape((chips, tied_rows, reads), BF16),
            shape((reads, width), F32),
            shape((reads, LANES), F32),
            shape((reads, width), BF16),
            *[shape((2 * reads, half), BF16)] * KINDS,
            *[shape((reads, width), BF16)] * KINDS,
        ),
        {2: heads_in, 3: heads_out},
    )
    ops, lefts = pieces[:KINDS], pieces[KINDS:]

    parts = exchange(tied, same_core)
    moved = [swap(ops[k], CORES * k) for k in range(1, KINDS)]
    parts, *moved = lax.optimization_barrier((parts, *moved))
    ops = [ops[0], *moved]
    if pos_count > 1:
        parts = lax.psum(jnp.sum(parts.astype(F32), 0, keepdims=True), "pos")
    copies = simple(
        functools.partial(soften_kernel, scale=scale, part=part),
        (parts,),
        shape((chips, tied_rows, reads), BF16),
    )
    pairs = exchange(copies, same_core)
    lefts = [lefts[0]] + [swap(lefts[k], CORES * k) for k in range(1, KINDS)]
    lefts_other = [left_other] + [swap(a, 1) for a in lefts[1:]]
    ops_other = [swap(a, 1) for a in ops]
    pairs_other = swap(pairs, 1)

    grad_own, grad_other = call(
        back_kernel,
        scalars,
        (pairs, proj, weights, start, end),
        (shape((reads, width), F32), shape((reads, width), F32)),
        {2: heads_in},
        [pltpu.VMEM((3, 2 * reads, half), BF16)],
    )
    grad_recv = swap(grad_other, 1)

    cells = 2 * KINDS * reads
    (product,) = call(
        weight_kernel,
        scalars,
        (pairs, pairs_other, start, end, *ops, *ops_other, *lefts, *lefts_other),
        (shape((width, half), BF16),),
        None,
        [pltpu.VMEM((cells, half), BF16), pltpu.VMEM((cells, half), BF16)],
    )
    payload = simple(
        functools.partial(pack_kernel, rows=rows),
        (grad_own, grad_recv, normed, inverse, product),
        shape((width, half + LANES), BF16),
    )
    arrived = exchange(payload.reshape(count, chunk, half + LANES), None)
    grad_input, sums = simple(
        finish_kernel,
        (arrived,),
        (shape((rows, col_dev, width), BF16), shape((chunk, KINDS * width), F32)),
    )
    weight_grads = lax.psum_scatter(sums, "pos", scatter_dimension=0, tiled=True)
    return (grad_input, weight_grads)


def solution(mesh):
    in_specs = (P("read", "pos", None), P("read", "pos", None), P(), P(), P())
    out_specs = (P("read", "pos", None), P(("read", "pos"), None))
    return jax.shard_map(shards, mesh=mesh, in_specs=in_specs, out_specs=out_specs, check_vma=False)
```

time: 116 us -> 111 us (0.957)
  waiting for transfers between devices: 38.2 us -> 27.9 us
  blocking collectives: 36.9 us -> 45.4 us
  local copies, waits for them, and re-layouts: 5.76 us -> 3.59 us
  Pallas kernels: 12.6 us -> 14.4 us
  other arithmetic: 2.72 us -> 1.06 us
  starting transfers between devices: 18.5 us -> 17.2 us
    all_to_all x4 -> x2, waiting for transfers between devices: 36.2 us -> 0.01 us  [exchange(): lax.all_to_all(array, 'read', split_axis=0, concat_axis=0, tiled=True, ax...]
    ppermute x9 -> x16, waiting for transfers between devices: 1.99 us -> 27.9 us  [swap(): return lax.ppermute(array, 'read', [(i, i ^ bits) for i in range(count)])]
    all_to_all x2, blocking collectives: 36.9 us -> 45.4 us  [exchange(): lax.all_to_all(array, 'read', split_axis=0, concat_axis=0, tiled=True, ax...]
    all_to_all x4 -> x2, starting transfers between devices: 14.3 us -> 8.44 us  [exchange(): lax.all_to_all(array, 'read', split_axis=0, concat_axis=0, tiled=True, ax...]
    ppermute x9 -> x16, starting transfers between devices: 4.17 us -> 8.71 us  [swap(): return lax.ppermute(array, 'read', [(i, i ^ bits) for i in range(count)])]
    unnamed x1 -> x16, local copies, waits for them, and re-layouts: 0.7 us -> 3.28 us
    reshape x3 -> x0, local copies, waits for them, and re-layouts: 2.47 us -> none  [the longest x1 0.95 us: shards(): jnp.sum(pieces, 0).transpose(2, 0, 1, 3)]
    pallas_call x5 -> x6, Pallas kernels: 12.6 us -> 14.4 us  [the longest x3 11.5 us: call(): pl.pallas_call(kernel, grid_spec=pltpu.PrefetchScalarGridSpec(num_scalar_...]
  transfers between devices with their start and end apart: 13 -> 18, of which waited for: 9 -> 10; matrix products, arithmetic and copies ran while one was open for 5% -> 0% of each run, Pallas kernels for 2% -> 6%
where the time goes in v3:
time: 111 us; the launch traced here: 110 us
  blocking collectives  45.4 us (41%)
  waiting for transfers between devices  27.9 us (25%)
  starting transfers between devices  17.2 us (15%)
  Pallas kernels  14.4 us (13%)
  local copies, waits for them, and re-layouts  3.59 us (3%)
    all_to_all x2, blocking collectives, exchange(): lax.all_to_all(array, 'read', split_axis=0, concat_axis=0, tiled=True, ax...  45.4 us
    ppermute x16, waiting for transfers between devices, swap(): return lax.ppermute(array, 'read', [(i, i ^ bits) for i in range(count)])  27.9 us
    pallas_call x3, Pallas kernels, call(): pl.pallas_call(kernel, grid_spec=pltpu.PrefetchScalarGridSpec(num_scalar_...  11.5 us
    ppermute x16, starting transfers between devices, swap(): return lax.ppermute(array, 'read', [(i, i ^ bits) for i in range(count)])  8.71 us
    all_to_all x2, starting transfers between devices, exchange(): lax.all_to_all(array, 'read', split_axis=0, concat_axis=0, tiled=True, ax...  8.44 us
    unnamed x16, local copies, waits for them, and re-layouts  3.28 us
    pallas_call x3, Pallas kernels, simple(): pl.pallas_call(kernel, out_shape=outs, compiler_params=pltpu.CompilerPara...  2.95 us
  transfers between devices with their start and end apart: 18, of which 10 were waited for; matrix products, arithmetic and copies ran while one was open for 0% of the time, Pallas kernels for 6%

profile of v3, /device:TPU:0, one launch (start us, length us, event | category | flops | bytes accessed | tf_op | source)
XLA Modules:
  0.0 110.2 jit_solution(8412697855497662271)
XLA Ops:
  0.6 1.1 pad_maximum_fusion
  1.7 0.2 copy.7
  1.9 20.3 %all_to_all.26 = bf16[32,8,768]{2,1,0:T(8,128)(2,1)S(1)} all-to-all(bf16[32,8,768]{2,1,0:T(8,128)(2,1)S(1)} %copy.7), channel_id=1, replica_groups=mesh['read'=32,'pos'=1] {'read'}, dimensions={0} | all-to-all | bytes 786432 | tf_op jit(solution)/shard_map/all_to_all | solution.py:296
  22.2 0.0 collective-permute-start
  22.2 0.1 stack.54.scalars
  22.3 1.6 %collective-permute-done.other = bf16[256,768]{1,0:T(8,128)(2,1)S(1)} collective-permute-done((bf16[256,768]{1,0:T(8,128)(2,1)S(1)}, bf16[256,768]{1,0:T(8,128)(2,1)S(1)}, u32[]{:S(2)}, u32[]{:S(2)}) %collective-permute-start) | collective-permute-done | bytes 393248 | tf_op jit(solution)/shard_map/ppermute | solution.py:353
  23.9 0.7 copy-done.2
  24.6 0.7 copy-done.4
  25.2 4.7 %shard_map.68 = (bf16[4,256,384]{2,1,0:T(8,128)(2,1)S(1)}, bf16[16,96,128]{2,1,0:T(8,128)(2,1)}, f32[128,768]{1,0:T(8,128)S(1)}, f32[128,128]{1,0:T(8,128)S(1)},...) custom-call(s32[12]{0:T(128)S(1)} %stack.54.scalars, ...), custom_call_target="tpu_custom_call" | custom-call | tf_op jit(solution)/shard_map/pallas_call | solution.py:307
  30.0 0.6 copy-done
  30.6 0.7 copy-done.6
  31.3 0.7 copy-done.7
  32.0 3.7 %all-to-all-start.1 = ((bf16[16,96,128]{2,1,0:T(8,128)(2,1)}), bf16[16,96,128]{2,1,0:T(8,128)(2,1)S(1)}, u32[]{:S(2)}, u32[]{:S(2)}) async-start(bf16[16,96,128]{2,1,0:T(8,128)(2,1)} %get-tuple-element.21), calls=%async_computation.1 | async-start | bytes 786432 | tf_op jit(solution)/shard_map/all_to_all | solution.py:296
  35.6 1.9 %collective-permute-start.1 = (bf16[256,384]{1,0:T(8,128)(2,1)}, bf16[256,384]{1,0:T(8,128)(2,1)S(1)}, u32[]{:S(2)}, u32[]{:S(2)}) collective-permute-start(bf16[256,384]{1,0:T(8,128)(2,1)} %get-tuple-element.22), channel_id=1, source_target_pairs={{0,2},{1,3},{2,0},{3,1},{4,6},{5,7},{6,4},{7,5},{8,10},{9,11},{10,... | collective-permute-start | bytes 589832 | tf_op jit(solution)/shard_map/ppermute | solution.py:353
  37.5 1.5 %collective-permute-start.2 = (bf16[256,384]{1,0:T(8,128)(2,1)S(1)}, bf16[256,384]{1,0:T(8,128)(2,1)S(1)}, u32[]{:S(2)}, u32[]{:S(2)}) collective-permute-start(bf16[256,384]{1,0:T(8,128)(2,1)S(1)} %get-tuple-element.23), channel_id=1, source_target_pairs={{0,4},{1,5},{2,6},{3,7},{4,0},{5,1},{6,2},{7,3},{8,12},{9,13},{10,... | collective-permute-start | bytes 589832 | tf_op jit(solution)/shard_map/ppermute | solution.py:353
  39.0 0.2 collective-permute-start.3
  39.2 8.0 %collective-permute-done.1.refs_1_ = bf16[256,384]{1,0:T(8,128)(2,1)S(1)} collective-permute-done((bf16[256,384]{1,0:T(8,128)(2,1)}, bf16[256,384]{1,0:T(8,128)(2,1)S(1)}, u32[]{:S(2)}, u32[]{:S(2)}) %collective-permute-start.1) | collective-permute-done | bytes 196640 | tf_op jit(solution)/shard_map/ppermute | solution.py:353
  47.2 0.9 collective-permute-done.2.refs_2_
  48.1 3.7 %collective-permute-done.3.refs_3_ = bf16[256,384]{1,0:T(8,128)(2,1)S(1)} collective-permute-done((bf16[256,384]{1,0:T(8,128)(2,1)S(1)}, bf16[256,384]{1,0:T(8,128)(2,1)S(1)}, u32[]{:S(2)}, u32[]{:S(2)}) %collective-permute-start.3) | collective-permute-done | bytes 196640 | tf_op jit(solution)/shard_map/ppermute | solution.py:353
  51.8 1.0 shard_map.69
  52.7 4.8 %all-to-all-start.2 = ((bf16[16,96,128]{2,1,0:T(8,128)(2,1)}), bf16[16,96,128]{2,1,0:T(8,128)(2,1)S(1)}, u32[]{:S(2)}, u32[]{:S(2)}) async-start(bf16[16,96,128]{2,1,0:T(8,128)(2,1)} %shard_map.69), calls=%async_computation.2 | async-start | bytes 786432 | tf_op jit(solution)/shard_map/all_to_all | solution.py:296
  57.5 1.9 %collective-permute-start.10 = (bf16[128,768]{1,0:T(8,128)(2,1)}, bf16[128,768]{1,0:T(8,128)(2,1)S(1)}, u32[]{:S(2)}, u32[]{:S(2)}) collective-permute-start(bf16[128,768]{1,0:T(8,128)(2,1)} %get-tuple-element.36), channel_id=1, source_target_pairs={{0,2},{1,3},{2,0},{3,1},{4,6},{5,7},{6,4},{7,5},{8,10},{9,11},{10,... | collective-permute-start | bytes 589832 | tf_op jit(solution)/shard_map/ppermute | solution.py:353
  59.5 1.5 %collective-permute-start.11 = (bf16[128,768]{1,0:T(8,128)(2,1)}, bf16[128,768]{1,0:T(8,128)(2,1)S(1)}, u32[]{:S(2)}, u32[]{:S(2)}) collective-permute-start(bf16[128,768]{1,0:T(8,128)(2,1)} %copy-done.7), channel_id=1, source_target_pairs={{0,4},{1,5},{2,6},{3,7},{4,0},{5,1},{6,2},{7,3},{8,12},{9,13},{10,... | collective-permute-start | bytes 589832 | tf_op jit(solution)/shard_map/ppermute | solution.py:353
  60.9 0.2 collective-permute-start.12
  61.1 0.0 collective-permute-start.6
  61.1 8.5 %collective-permute-done.10.refs_9_ = bf16[128,768]{1,0:T(8,128)(2,1)S(1)} collective-permute-done((bf16[128,768]{1,0:T(8,128)(2,1)}, bf16[128,768]{1,0:T(8,128)(2,1)S(1)}, u32[]{:S(2)}, u32[]{:S(2)}) %collective-permute-start.10) | collective-permute-done | bytes 196640 | tf_op jit(solution)/shard_map/ppermute | solution.py:353
  69.6 0.0 collective-permute-start.13
  69.6 0.6 collective-permute-done.11.refs_10_
  70.2 0.0 collective-permute-start.14
  70.2 3.0 %collective-permute-done.12.refs_11_ = bf16[128,768]{1,0:T(8,128)(2,1)} collective-permute-done((bf16[128,768]{1,0:T(8,128)(2,1)}, bf16[128,768]{1,0:T(8,128)(2,1)}, u32[]{:S(2)}, u32[]{:S(2)}) %collective-permute-start.12) | collective-permute-done | bytes 196640 | tf_op jit(solution)/shard_map/ppermute | solution.py:353
  73.2 0.0 collective-permute-start.15
  73.2 0.0 all-to-all-done.2.pairs
  73.2 0.5 collective-permute-start.5
  73.7 3.2 %shard_map.70 = (f32[128,768]{1,0:T(8,128)S(1)}, f32[128,768]{1,0:T(8,128)S(1)}) custom-call(s32[12]{0:T(128)S(1)} %stack.54.scalars, bf16[16,96,128]{2,1,0:T(8,128)(2,1)S(1)} %all-to-all-done.2.pairs, bf16[4,256,384]{2,1,0:T(8,128)(2,1)S(1)} %get-tuple-element.26.proj, bf16[4,768,768]{2,1,0:T(8,128)(2,1)} %heads_in.3, s32[1,128]{1,0:T(1,128)S(1)} %bitcast.23, ...), custom_call_target="tpu_custom_call" | custom-call | tf_op jit(solution)/shard_map/pallas_call | solution.py:307
  77.0 0.1 collective-permute-start.4
  77.1 0.0 collective-permute-done.13.refs_13_
  77.1 0.5 collective-permute-start.7
  77.6 0.0 collective-permute-done.14.refs_14_
  77.6 0.1 collective-permute-start.8
  77.7 0.4 collective-permute-start.9
  78.1 1.0 collective-permute-done.7.refs_5_
  79.0 0.3 collective-permute-done.8.refs_6_
  79.3 0.3 collective-permute-done.9.refs_7_
  79.6 3.5 %shard_map.71.product = bf16[768,384]{1,0:T(8,128)(2,1)S(1)} custom-call(s32[12]{0:T(128)S(1)} %stack.54.scalars, bf16[16,96,128]{2,1,0:T(8,128)(2,1)S(1)} %all-to-all-done.2.pairs, bf16[16,96,128]{2,1,0:T(8,128)(2,1)S(1)} %collective-permute-done.5.pairs_other, s32[1,128]{1,0:T(1,128)S(1)} %bitcast.24, s32[1,128]{1,0:T(1,128)S(1)} %bitcast.27, ...), custom_call_target="tpu_custom_call" | custom-call | tf_op jit(solution)/shard_map/pallas_call | solution.py:307
  83.1 0.0 collective-permute-done.4.grad_recv
  83.1 0.7 shard_map.72
  83.9 25.1 %all_to_all.27.arrived = bf16[32,24,512]{2,1,0:T(8,128)(2,1)S(1)} all-to-all(bf16[32,24,512]{2,1,0:T(8,128)(2,1)S(1)} %bitcast.19), channel_id=1, replica_groups=mesh['read'=32,'pos'=1] {'read'}, dimensions={0} | all-to-all | bytes 1572864 | tf_op jit(solution)/shard_map/all_to_all | solution.py:296
  109.0 1.3 %shard_map.73 = (bf16[4,32,768]{2,1,0:T(8,128)(2,1)}, f32[24,3072]{1,0:T(8,128)}) custom-call(bf16[32,24,512]{2,1,0:T(8,128)(2,1)S(1)} %all_to_all.27.arrived), custom_call_target="tpu_custom_call" | custom-call | tf_op jit(solution)/shard_map/pallas_call | solution.py:322
  (15 shorter events, 0.0 us)
Async XLA Ops:
  22.2 1.7 %collective-permute-start = (bf16[256,768]{1,0:T(8,128)(2,1)S(1)}, bf16[256,768]{1,0:T(8,128)(2,1)S(1)}, u32[]{:S(2)}, u32[]{:S(2)}) collective-permute-start(bf16[256,768]{1,0:T(8,128)(2,1)S(1)} %bitcast.20), channel_id=1, source_target_pairs={{0,1},{1,0},{2,3},{3,2},{4,5},{5,4},{6,7},{7,6},{8,9},{9,8},{10,11... | collective-permute-start | bytes 1179656 | tf_op jit(solution)/shard_map/ppermute | solution.py:353
  23.9 0.7 copy-start.2
  24.6 0.7 copy-start.4
  25.2 48.5 %copy-start.3 = (s32[128]{0:T(128)S(1)}, s32[128]{0:T(128)}, u32[]{:S(2)}) copy-start(s32[128]{0:T(128)} %param.8) | copy-start | bytes 1540
  25.2 48.5 %copy-start.5 = (s32[128]{0:T(128)S(1)}, s32[128]{0:T(128)}, u32[]{:S(2)}) copy-start(s32[128]{0:T(128)} %param.9) | copy-start | bytes 1540
  30.0 0.6 copy-start
  30.6 0.7 copy-start.6
  31.3 0.7 copy-start.7
  32.0 19.8 %all-to-all-start.1 = ((bf16[16,96,128]{2,1,0:T(8,128)(2,1)}), bf16[16,96,128]{2,1,0:T(8,128)(2,1)S(1)}, u32[]{:S(2)}, u32[]{:S(2)}) async-start(bf16[16,96,128]{2,1,0:T(8,128)(2,1)} %get-tuple-element.21), calls=%async_computation.1 | async-start | bytes 786432 | tf_op jit(solution)/shard_map/all_to_all | solution.py:296
  35.6 11.6 %collective-permute-start.1 = (bf16[256,384]{1,0:T(8,128)(2,1)}, bf16[256,384]{1,0:T(8,128)(2,1)S(1)}, u32[]{:S(2)}, u32[]{:S(2)}) collective-permute-start(bf16[256,384]{1,0:T(8,128)(2,1)} %get-tuple-element.22), channel_id=1, source_target_pairs={{0,2},{1,3},{2,0},{3,1},{4,6},{5,7},{6,4},{7,5},{8,10},{9,11},{10,... | collective-permute-start | bytes 589832 | tf_op jit(solution)/shard_map/ppermute | solution.py:353
  37.5 10.6 %collective-permute-start.2 = (bf16[256,384]{1,0:T(8,128)(2,1)S(1)}, bf16[256,384]{1,0:T(8,128)(2,1)S(1)}, u32[]{:S(2)}, u32[]{:S(2)}) collective-permute-start(bf16[256,384]{1,0:T(8,128)(2,1)S(1)} %get-tuple-element.23), channel_id=1, source_target_pairs={{0,4},{1,5},{2,6},{3,7},{4,0},{5,1},{6,2},{7,3},{8,12},{9,13},{10,... | collective-permute-start | bytes 589832 | tf_op jit(solution)/shard_map/ppermute | solution.py:353
  39.0 12.8 %collective-permute-start.3 = (bf16[256,384]{1,0:T(8,128)(2,1)S(1)}, bf16[256,384]{1,0:T(8,128)(2,1)S(1)}, u32[]{:S(2)}, u32[]{:S(2)}) collective-permute-start(bf16[256,384]{1,0:T(8,128)(2,1)S(1)} %get-tuple-element.24), channel_id=1, source_target_pairs={{0,6},{1,7},{2,4},{3,5},{4,2},{5,3},{6,0},{7,1},{8,14},{9,15},{10,... | collective-permute-start | bytes 589832 | tf_op jit(solution)/shard_map/ppermute | solution.py:353
  52.7 20.5 %all-to-all-start.2 = ((bf16[16,96,128]{2,1,0:T(8,128)(2,1)}), bf16[16,96,128]{2,1,0:T(8,128)(2,1)S(1)}, u32[]{:S(2)}, u32[]{:S(2)}) async-start(bf16[16,96,128]{2,1,0:T(8,128)(2,1)} %shard_map.69), calls=%async_computation.2 | async-start | bytes 786432 | tf_op jit(solution)/shard_map/all_to_all | solution.py:296
  57.5 12.0 %collective-permute-start.10 = (bf16[128,768]{1,0:T(8,128)(2,1)}, bf16[128,768]{1,0:T(8,128)(2,1)S(1)}, u32[]{:S(2)}, u32[]{:S(2)}) collective-permute-start(bf16[128,768]{1,0:T(8,128)(2,1)} %get-tuple-element.36), channel_id=1, source_target_pairs={{0,2},{1,3},{2,0},{3,1},{4,6},{5,7},{6,4},{7,5},{8,10},{9,11},{10,... | collective-permute-start | bytes 589832 | tf_op jit(solution)/shard_map/ppermute | solution.py:353
  59.5 10.7 %collective-permute-start.11 = (bf16[128,768]{1,0:T(8,128)(2,1)}, bf16[128,768]{1,0:T(8,128)(2,1)S(1)}, u32[]{:S(2)}, u32[]{:S(2)}) collective-permute-start(bf16[128,768]{1,0:T(8,128)(2,1)} %copy-done.7), channel_id=1, source_target_pairs={{0,4},{1,5},{2,6},{3,7},{4,0},{5,1},{6,2},{7,3},{8,12},{9,13},{10,... | collective-permute-start | bytes 589832 | tf_op jit(solution)/shard_map/ppermute | solution.py:353
  60.9 12.3 %collective-permute-start.12 = (bf16[128,768]{1,0:T(8,128)(2,1)}, bf16[128,768]{1,0:T(8,128)(2,1)}, u32[]{:S(2)}, u32[]{:S(2)}) collective-permute-start(bf16[128,768]{1,0:T(8,128)(2,1)} %copy-done.6), channel_id=1, source_target_pairs={{0,6},{1,7},{2,4},{3,5},{4,2},{5,3},{6,0},{7,1},{8,14},{9,15},{10,... | collective-permute-start | bytes 589832 | tf_op jit(solution)/shard_map/ppermute | solution.py:353
  61.1 15.9 %collective-permute-start.6 = (bf16[256,384]{1,0:T(8,128)(2,1)S(1)}, bf16[256,384]{1,0:T(8,128)(2,1)}, u32[]{:S(2)}, u32[]{:S(2)}) collective-permute-start(bf16[256,384]{1,0:T(8,128)(2,1)S(1)} %get-tuple-element.31.refs_0_), channel_id=1, source_target_pairs={{0,1},{1,0},{2,3},{3,2},{4,5},{5,4},{6,7},{7,6},{8,9},{9,8},{10,11... | collective-permute-start | bytes 589832 | tf_op jit(solution)/shard_map/ppermute | solution.py:353
  69.6 7.5 %collective-permute-start.13 = (bf16[128,768]{1,0:T(8,128)(2,1)S(1)}, bf16[128,768]{1,0:T(8,128)(2,1)}, u32[]{:S(2)}, u32[]{:S(2)}) collective-permute-start(bf16[128,768]{1,0:T(8,128)(2,1)S(1)} %collective-permute-done.10.refs_9_), channel_id=1, source_target_pairs={{0,1},{1,0},{2,3},{3,2},{4,5},{5,4},{6,7},{7,6},{8,9},{9,8},{10,11... | collective-permute-start | bytes 589832 | tf_op jit(solution)/shard_map/ppermute | solution.py:353
  70.2 7.4 %collective-permute-start.14 = (bf16[128,768]{1,0:T(8,128)(2,1)S(1)}, bf16[128,768]{1,0:T(8,128)(2,1)}, u32[]{:S(2)}, u32[]{:S(2)}) collective-permute-start(bf16[128,768]{1,0:T(8,128)(2,1)S(1)} %collective-permute-done.11.refs_10_), channel_id=1, source_target_pairs={{0,1},{1,0},{2,3},{3,2},{4,5},{5,4},{6,7},{7,6},{8,9},{9,8},{10,11... | collective-permute-start | bytes 589832 | tf_op jit(solution)/shard_map/ppermute | solution.py:353
  73.2 4.5 %collective-permute-start.15 = (bf16[128,768]{1,0:T(8,128)(2,1)}, bf16[128,768]{1,0:T(8,128)(2,1)}, u32[]{:S(2)}, u32[]{:S(2)}) collective-permute-start(bf16[128,768]{1,0:T(8,128)(2,1)} %collective-permute-done.12.refs_11_), channel_id=1, source_target_pairs={{0,1},{1,0},{2,3},{3,2},{4,5},{5,4},{6,7},{7,6},{8,9},{9,8},{10,11... | collective-permute-start | bytes 589832 | tf_op jit(solution)/shard_map/ppermute | solution.py:353
  73.2 6.4 %collective-permute-start.5 = (bf16[16,96,128]{2,1,0:T(8,128)(2,1)S(1)}, bf16[16,96,128]{2,1,0:T(8,128)(2,1)S(1)}, u32[]{:S(2)}, u32[]{:S(2)}) collective-permute-start(bf16[16,96,128]{2,1,0:T(8,128)(2,1)S(1)} %all-to-all-done.2.pairs), channel_id=1, source_target_pairs={{0,1},{1,0},{2,3},{3,2},{4,5},{5,4},{6,7},{7,6},{8,9},{9,8},{10,11... | collective-permute-start | bytes 1179656 | tf_op jit(solution)/shard_map/ppermute | solution.py:353
  73.7 9.4 %copy-start.1 = (f32[128,128]{1,0:T(8,128)S(1)}, f32[128,128]{1,0:T(8,128)}, u32[]{:S(2)}) copy-start(f32[128,128]{1,0:T(8,128)} %copy-done) | copy-start | bytes 196612
  77.0 6.1 %collective-permute-start.4 = (f32[128,768]{1,0:T(8,128)S(1)}, f32[128,768]{1,0:T(8,128)S(1)}, u32[]{:S(2)}, u32[]{:S(2)}) collective-permute-start(f32[128,768]{1,0:T(8,128)S(1)} %get-tuple-element.28), channel_id=1, source_target_pairs={{0,1},{1,0},{2,3},{3,2},{4,5},{5,4},{6,7},{7,6},{8,9},{9,8},{10,11... | collective-permute-start | bytes 1179656 | tf_op jit(solution)/shard_map/ppermute | solution.py:353
  77.1 2.0 %collective-permute-start.7 = (bf16[256,384]{1,0:T(8,128)(2,1)S(1)}, bf16[256,384]{1,0:T(8,128)(2,1)S(1)}, u32[]{:S(2)}, u32[]{:S(2)}) collective-permute-start(bf16[256,384]{1,0:T(8,128)(2,1)S(1)} %collective-permute-done.1.refs_1_), channel_id=1, source_target_pairs={{0,1},{1,0},{2,3},{3,2},{4,5},{5,4},{6,7},{7,6},{8,9},{9,8},{10,11... | collective-permute-start | bytes 589832 | tf_op jit(solution)/shard_map/ppermute | solution.py:353
  77.6 1.8 %collective-permute-start.8 = (bf16[256,384]{1,0:T(8,128)(2,1)S(1)}, bf16[256,384]{1,0:T(8,128)(2,1)S(1)}, u32[]{:S(2)}, u32[]{:S(2)}) collective-permute-start(bf16[256,384]{1,0:T(8,128)(2,1)S(1)} %collective-permute-done.2.refs_2_), channel_id=1, source_target_pairs={{0,1},{1,0},{2,3},{3,2},{4,5},{5,4},{6,7},{7,6},{8,9},{9,8},{10,11... | collective-permute-start | bytes 589832 | tf_op jit(solution)/shard_map/ppermute | solution.py:353
  77.7 2.0 %collective-permute-start.9 = (bf16[256,384]{1,0:T(8,128)(2,1)S(1)}, bf16[256,384]{1,0:T(8,128)(2,1)S(1)}, u32[]{:S(2)}, u32[]{:S(2)}) collective-permute-start(bf16[256,384]{1,0:T(8,128)(2,1)S(1)} %collective-permute-done.3.refs_3_), channel_id=1, source_target_pairs={{0,1},{1,0},{2,3},{3,2},{4,5},{5,4},{6,7},{7,6},{8,9},{9,8},{10,11... | collective-permute-start | bytes 589832 | tf_op jit(solution)/shard_map/ppermute | solution.py:353

commit v4 on v3

--- a/solution.py
+++ b/solution.py
@@ -13,7 +13,7 @@
 CORES = 2
 KINDS = 4
 LANES = 128
-VMEM_LIMIT = 48 * 1024 * 1024
+MIB = 1024 * 1024
 
 BF16 = jnp.bfloat16
 F32 = jnp.float32
@@ -55,12 +55,40 @@
     return place(at, spot).astype(F32).astype(BF16)
 
 
+def position():
+    me = lax.axis_index("read")
+    core = jnp.bitwise_and(me, CORES - 1)
+    kind = jnp.bitwise_and(jnp.right_shift(me, 1), KINDS - 1)
+    return me, core, kind
+
+
+def head_lanes(core, half):
+    return pl.ds(pl.multiple_of(core * half, LANES), half)
+
+
 def project_kernel(
-    scalars, own, other, heads_in, heads_out, start, end, proj, tied, normed_own, inverse_own,
-    left_other, *pieces, rows
+    own, other, weights, start, end, proj, tied, normed_own, inverse_own, bounds, left_other,
+    *rest, rows, col_dev
 ):
-    ops, lefts = pieces[:KINDS], pieces[KINDS:]
+    ops, lefts = rest[:KINDS], rest[KINDS : 2 * KINDS]
+    heads_in, heads_out, start_here, end_here, sems = rest[2 * KINDS :]
     cells = own.shape[0] // 2
+    width = own.shape[1]
+    half = width // CORES
+    me, core, mine_kind = position()
+    first_col = lax.axis_index("pos") * col_dev
+    copies = [
+        pltpu.make_async_copy(
+            weights.at[pl.ds(0, 3), :, head_lanes(core, half)], heads_in, sems.at[0]
+        ),
+        pltpu.make_async_copy(
+            weights.at[3, head_lanes(core, half), :], heads_out, sems.at[1]
+        ),
+        pltpu.make_async_copy(start, start_here, sems.at[2]),
+        pltpu.make_async_copy(end, end_here, sems.at[3]),
+    ]
+    for copy in copies:
+        copy.start()
 
     def pick(shift):
         return indicator(
@@ -69,31 +97,41 @@
             lambda at, spot: spot == lax.div(at, rows) * (2 * rows) + lax.rem(at, rows) + shift,
         )
 
-    mine, theirs = own[...], other[...]
-    source = jnp.concatenate([dot(pick(0), mine), dot(pick(0), theirs)], axis=0)
-    upstream = jnp.concatenate([dot(pick(rows), mine), dot(pick(rows), theirs)], axis=0)
-    upstream = upstream.astype(BF16)
+    arrived = jnp.concatenate([own[...], other[...]], axis=1)
+    source = dot(pick(0), arrived)
+    source = jnp.concatenate([source[:, :width], source[:, width:]], axis=0)
+    upstream = dot(pick(rows), arrived).astype(BF16)
+    upstream = jnp.concatenate([upstream[:, :width], upstream[:, width:]], axis=0)
     inverse = lax.rsqrt(jnp.mean(source * source, -1, keepdims=True) + 1e-05)
     normed32 = source * inverse
     normed = normed32.astype(BF16)
     normed_own[...] = normed32[:cells]
     inverse_own[...] = jnp.broadcast_to(inverse[:cells], inverse_own.shape)
-    first, last = upright(start[...]), upright(end[...])
+    copies[2].wait()
+    copies[3].wait()
+    first, last = upright(start_here[...]), upright(end_here[...])
+    lane = lax.broadcasted_iota(jnp.int32, bounds.shape, 1)
+    bounds[...] = jnp.where(lane == 0, first, last)
     covered = jnp.concatenate(
-        [row_mask(first, last, scalars[2]), row_mask(first, last, scalars[3])], axis=0
-    )
+        [
+            row_mask(first, last, first_col + me),
+            row_mask(first, last, first_col + jnp.bitwise_xor(me, 1)),
+        ],
+        axis=0,
+    )
+    copies[0].wait()
     query = (dot(normed, heads_in[0]) * covered).astype(BF16)
     keys = (dot(normed, heads_in[1]) * covered).astype(BF16)
     values = (dot(normed, heads_in[2]) * covered).astype(BF16)
-    back_out = dot(upstream, heads_out[0], (1, 1)).astype(BF16)
+    copies[1].wait()
+    back_out = dot(upstream, heads_out[...], (1, 1)).astype(BF16)
     proj[0] = query
     proj[1] = keys
-    proj[2] = values
-    proj[3] = back_out
+    proj[2] = back_out
 
     for kind in range(KINDS):
 
-        @pl.when(scalars[1] == kind)
+        @pl.when(mine_kind == kind)
         def _():
             needs = (keys, query, back_out, values)
             for step in range(KINDS):
@@ -106,15 +144,21 @@
     low = first_heads(cells, 2 * LANES)
     chips = tied.shape[0]
     part = cells // chips
-    for pair in range(query.shape[1] // LANES):
-        queries, backs = slab(query, pair), slab(back_out, pair)
-        key, value = slab(keys, pair), slab(values, pair)
+
+    def both_heads(array):
+        return jnp.concatenate([jnp.where(low, array, 0), jnp.where(low, 0, array)], axis=0)
+
+    for pair in range(half // LANES):
+        logits = dot(both_heads(slab(query, pair)), slab(keys, pair), (1, 1))
+        slopes = dot(both_heads(slab(back_out, pair)), slab(values, pair), (1, 1))
         for odd in range(2):
-            keep = jnp.logical_not(low) if odd else low
-            logits = dot(jnp.where(keep, queries, 0), key, (1, 1))
-            slopes = dot(jnp.where(keep, backs, 0), value, (1, 1))
+            here = slice(odd * cells, (odd + 1) * cells)
             both = jnp.concatenate(
-                [logits.reshape(chips, part, cells), slopes.reshape(chips, part, cells)], axis=1
+                [
+                    logits[here].reshape(chips, part, cells),
+                    slopes[here].reshape(chips, part, cells),
+                ],
+                axis=1,
             )
             spot = (2 * pair + odd) * 2 * part
             tied[:, spot : spot + 2 * part, :] = both.astype(BF16)
@@ -139,34 +183,39 @@
     return both[:, :part].reshape(cells, cells), both[:, part:].reshape(cells, cells)
 
 
-def back_kernel(scalars, pairs, proj, heads_in, start, end, own, other, grads):
+def back_kernel(pairs, proj, bounds, weights, own, other, grads, heads_in, sem, *, col_dev):
     cells = proj.shape[1] // 2
-    first, last = upright(start[...]), upright(end[...])
-    covered = jnp.concatenate(
-        [
-            jnp.broadcast_to(row_mask(first, last, scalars[2]), (cells, LANES)),
-            jnp.broadcast_to(row_mask(first, last, scalars[3]), (cells, LANES)),
-        ],
-        axis=1,
-    )
+    half = proj.shape[2]
+    me, core, _ = position()
+    first_col = lax.axis_index("pos") * col_dev
+    copy = pltpu.make_async_copy(
+        weights.at[pl.ds(0, 3), :, head_lanes(core, half)], heads_in, sem
+    )
+    copy.start()
+    first, last = bounds[:, 0:1], bounds[:, 1:2]
+    masks = [
+        jnp.broadcast_to(
+            row_mask(first, last, first_col + jnp.bitwise_xor(me, side)), (cells, LANES)
+        )
+        for side in range(2)
+    ]
+    covered = jnp.concatenate(masks, axis=1)
     low = first_heads(cells, 2 * LANES)
-    for pair in range(proj.shape[2] // LANES):
+    for pair in range(half // LANES):
         lanes = slice(pair * LANES, (pair + 1) * LANES)
 
-        def store(kind, one, two):
-            result = (jnp.where(low, one, two) * covered).astype(BF16)
+        def store(kind, maps, operand):
+            result = dot(jnp.concatenate(maps, axis=0), operand)
+            result = (jnp.where(low, result[:cells], result[cells:]) * covered).astype(BF16)
             grads[kind, :cells, lanes] = result[:, :LANES]
             grads[kind, cells:, lanes] = result[:, LANES:]
 
         maps = [head_maps(pairs, 2 * pair + odd, cells) for odd in range(2)]
-        probs_t = [a.T.astype(BF16) for a, _ in maps]
-        mixed_t = [b.T.astype(BF16) for _, b in maps]
-        mixed = [b.astype(BF16) for _, b in maps]
-        query, key, back = slab(proj[0], pair), slab(proj[1], pair), slab(proj[3], pair)
-        store(0, dot(mixed[0], key), dot(mixed[1], key))
-        store(1, dot(mixed_t[0], query), dot(mixed_t[1], query))
-        store(2, dot(probs_t[0], back), dot(probs_t[1], back))
-
+        store(0, [b.astype(BF16) for _, b in maps], slab(proj[1], pair))
+        store(1, [b.T.astype(BF16) for _, b in maps], slab(proj[0], pair))
+        store(2, [a.T.astype(BF16) for a, _ in maps], slab(proj[2], pair))
+
+    copy.wait()
     total = dot(grads[0], heads_in[0], (1, 1))
     total = total + dot(grads[1], heads_in[1], (1, 1))
     total = total + dot(grads[2], heads_in[2], (1, 1))
@@ -174,14 +223,15 @@
     other[...] = total[cells:]
 
 
-def weight_kernel(scalars, pairs, pairs_other, start, end, *refs):
+def weight_kernel(pairs, pairs_other, bounds, *refs, col_dev):
     ops, ops_other, lefts, lefts_other = (
         refs[at * KINDS : (at + 1) * KINDS] for at in range(4)
     )
     product, right, right_other = refs[4 * KINDS :]
     cells, width = lefts[0].shape
     half = ops[0].shape[1]
-    core, kind = scalars[0], scalars[1]
+    me, core, kind = position()
+    first_col = lax.axis_index("pos") * col_dev
     low = first_heads(cells, 2 * KINDS * LANES)
     use_probs = kind >= 2
     use_flip = (kind == 1) | (kind == 2)
@@ -189,7 +239,7 @@
     def gradient(source, operands, covered, out, swapped):
         for pair in range(half // LANES):
             cat = jnp.concatenate([slab(operand[...], pair) for operand in operands], axis=1)
-            sides = []
+            maps = []
             for odd in range(2):
                 probs, mixed = head_maps(source, 2 * pair + odd, cells)
                 if swapped:
@@ -197,8 +247,9 @@
                 else:
                     chosen = jnp.where(use_probs, probs, mixed)
                     chosen = jnp.where(use_flip, chosen.T, chosen)
-                sides.append(dot(chosen.astype(BF16), cat))
-            result = jnp.where(low, sides[0], sides[1])
+                maps.append(chosen.astype(BF16))
+            result = dot(jnp.concatenate(maps, axis=0), cat)
+            result = jnp.where(low, result[:cells], result[cells:])
             if covered is not None:
                 result = result * covered
             result = result.astype(BF16)
@@ -209,12 +260,11 @@
                     :, at * LANES : (at + 1) * LANES
                 ]
 
-    first, last = upright(start[...]), upright(end[...])
+    first, last = bounds[:, 0:1], bounds[:, 1:2]
     masks = []
-    for step in range(KINDS):
-        for side in range(2):
-            mask = row_mask(first, last, scalars[4 + 2 * step + side])
-            masks.append(jnp.broadcast_to(mask, (cells, LANES)))
+    for at in range(2 * KINDS):
+        mask = row_mask(first, last, first_col + jnp.bitwise_xor(me, at))
+        masks.append(jnp.broadcast_to(mask, (cells, LANES)))
     covered = jnp.concatenate(masks, axis=1)
     covered = jnp.where(kind == KINDS - 1, 1.0, covered)
     gradient(pairs, ops, covered, right, False)
@@ -298,31 +348,19 @@
     )
 
 
-def whole(shape):
-    return pl.BlockSpec(shape, lambda i, s: (0,) * len(shape))
-
-
-def call(kernel, scalars, args, outs, specs=None, scratch=()):
-    specs = specs or {}
+def call(kernel, args, outs, mib, far=(), scratch=()):
+    args = [
+        pltpu.with_memory_space_constraint(arg, pltpu.HBM) if at in far else arg
+        for at, arg in enumerate(args)
+    ]
+    near, away = (pl.BlockSpec(memory_space=space) for space in (pltpu.VMEM, pltpu.HBM))
     return pl.pallas_call(
         kernel,
-        grid_spec=pltpu.PrefetchScalarGridSpec(
-            num_scalar_prefetch=1,
-            grid=(1,),
-            in_specs=[specs.get(at) or whole(arg.shape) for at, arg in enumerate(args)],
-            out_specs=[whole(out.shape) for out in outs],
-            scratch_shapes=scratch,
-        ),
+        in_specs=[away if at in far else near for at in range(len(args))],
+        out_specs=jax.tree.map(lambda _: near, outs),
         out_shape=outs,
-        compiler_params=pltpu.CompilerParams(vmem_limit_bytes=VMEM_LIMIT),
-    )(scalars, *args)
-
-
-def simple(kernel, args, outs):
-    return pl.pallas_call(
-        kernel,
-        out_shape=outs,
-        compiler_params=pltpu.CompilerParams(vmem_limit_bytes=VMEM_LIMIT),
+        scratch_shapes=scratch,
+        compiler_params=pltpu.CompilerParams(vmem_limit_bytes=mib * MIB),
     )(*args)
 
 
@@ -330,8 +368,6 @@
     rows, col_dev, width = features.shape
     count = lax.axis_size("read")
     pos_count = lax.axis_size("pos")
-    me = lax.axis_index("read")
-    pos_at = lax.axis_index("pos")
     scale = 1.0 / math.sqrt(HEAD_DIM * col_dev * pos_count)
     reads = rows * count
     chips = count // CORES
@@ -339,11 +375,6 @@
     part = reads // chips
     tied_rows = (HEADS // CORES) * 2 * part
     chunk = width // count
-    first = pos_at * col_dev
-    core = jnp.bitwise_and(me, CORES - 1)
-    kind = jnp.bitwise_and(jnp.right_shift(me, 1), KINDS - 1)
-    columns = [first + jnp.bitwise_xor(me, at) for at in range(CORES * KINDS)]
-    scalars = jnp.stack([core, kind, columns[0], columns[1], *columns]).astype(jnp.int32)
     start = read_start.reshape(1, reads)
     end = read_end.reshape(1, reads)
 
@@ -353,75 +384,88 @@
         return lax.ppermute(array, "read", [(i, i ^ bits) for i in range(count)])
 
     shape = jax.ShapeDtypeStruct
-    heads_in = pl.BlockSpec((3, width, half), lambda i, s: (0, 0, s[0]))
-    heads_out = pl.BlockSpec((1, half, width), lambda i, s: (3, s[0], 0))
-
     send = jnp.stack([features, grad_out]).transpose(2, 0, 1, 3).reshape(-1, width)
     own = exchange(send, None)
     other = swap(own, 1)
-    proj, tied, normed, inverse, left_other, *pieces = call(
-        functools.partial(project_kernel, rows=rows),
-        scalars,
-        (own, other, weights, weights, start, end),
+    proj, tied, normed, inverse, bounds, left_other, *pieces = call(
+        functools.partial(project_kernel, rows=rows, col_dev=col_dev),
+        (own, other, weights, start, end),
         (
-            shape((KINDS, 2 * reads, half), BF16),
+            shape((KINDS - 1, 2 * reads, half), BF16),
             shape((chips, tied_rows, reads), BF16),
             shape((reads, width), F32),
+            shape((reads, LANES), F32),
             shape((reads, LANES), F32),
             shape((reads, width), BF16),
             *[shape((2 * reads, half), BF16)] * KINDS,
             *[shape((reads, width), BF16)] * KINDS,
         ),
-        {2: heads_in, 3: heads_out},
+        20,
+        (2, 3, 4),
+        [
+            pltpu.VMEM((3, width, half), BF16),
+            pltpu.VMEM((half, width), BF16),
+            pltpu.VMEM((1, reads), jnp.int32),
+            pltpu.VMEM((1, reads), jnp.int32),
+            pltpu.SemaphoreType.DMA((4,)),
+        ],
     )
     ops, lefts = pieces[:KINDS], pieces[KINDS:]
 
     parts = exchange(tied, same_core)
     moved = [swap(ops[k], CORES * k) for k in range(1, KINDS)]
-    parts, *moved = lax.optimization_barrier((parts, *moved))
-    ops = [ops[0], *moved]
     if pos_count > 1:
         parts = lax.psum(jnp.sum(parts.astype(F32), 0, keepdims=True), "pos")
-    copies = simple(
+    copies = call(
         functools.partial(soften_kernel, scale=scale, part=part),
         (parts,),
         shape((chips, tied_rows, reads), BF16),
-    )
+        8,
+    )
+    copies, *moved = lax.optimization_barrier((copies, *moved))
+    ops = [ops[0], *moved]
     pairs = exchange(copies, same_core)
     lefts = [lefts[0]] + [swap(lefts[k], CORES * k) for k in range(1, KINDS)]
-    lefts_other = [left_other] + [swap(a, 1) for a in lefts[1:]]
     ops_other = [swap(a, 1) for a in ops]
     pairs_other = swap(pairs, 1)
 
     grad_own, grad_other = call(
-        back_kernel,
-        scalars,
-        (pairs, proj, weights, start, end),
+        functools.partial(back_kernel, col_dev=col_dev),
+        (pairs, proj, bounds, weights),
         (shape((reads, width), F32), shape((reads, width), F32)),
-        {2: heads_in},
-        [pltpu.VMEM((3, 2 * reads, half), BF16)],
-    )
+        12,
+        (3,),
+        [
+            pltpu.VMEM((3, 2 * reads, half), BF16),
+            pltpu.VMEM((3, width, half), BF16),
+            pltpu.SemaphoreType.DMA,
+        ],
+    )
+    grad_other, *lefts = lax.optimization_barrier((grad_other, *lefts))
+    lefts_other = [left_other] + [swap(a, 1) for a in lefts[1:]]
     grad_recv = swap(grad_other, 1)
 
     cells = 2 * KINDS * reads
-    (product,) = call(
-        weight_kernel,
-        scalars,
-        (pairs, pairs_other, start, end, *ops, *ops_other, *lefts, *lefts_other),
-        (shape((width, half), BF16),),
-        None,
+    product = call(
+        functools.partial(weight_kernel, col_dev=col_dev),
+        (pairs, pairs_other, bounds, *ops, *ops_other, *lefts, *lefts_other),
+        shape((width, half), BF16),
+        20,
+        (),
         [pltpu.VMEM((cells, half), BF16), pltpu.VMEM((cells, half), BF16)],
     )
-    payload = simple(
+    payload = call(
         functools.partial(pack_kernel, rows=rows),
         (grad_own, grad_recv, normed, inverse, product),
         shape((width, half + LANES), BF16),
+        8,
     )
     arrived = exchange(payload.reshape(count, chunk, half + LANES), None)
-    grad_input, sums = simple(
+    grad_input, sums = call(
         finish_kernel,
         (arrived,),
         (shape((rows, col_dev, width), BF16), shape((chunk, KINDS * width), F32)),
+        8,
     )
     weight_grads = lax.psum_scatter(sums, "pos", scatter_dimension=0, tiled=True)
     return (grad_input, weight_grads)

time: 111 us -> 102 us (0.919)
  waiting for transfers between devices: 27.9 us -> 24 us
  local copies, waits for them, and re-layouts: 3.59 us -> 0.22 us
  Pallas kernels: 14.4 us -> 12.8 us
    ppermute x16, waiting for transfers between devices: 27.9 us -> 6.02 us  [swap(): return lax.ppermute(array, 'read', [(i, i ^ bits) for i in range(count)])]
    all_to_all x2, waiting for transfers between devices: 0.01 us -> 18 us  [exchange(): lax.all_to_all(array, 'read', split_axis=0, concat_axis=0, tiled=True, ax...]
    unnamed x16 -> x0, local copies, waits for them, and re-layouts: 3.28 us -> none
    pallas_call x6, Pallas kernels: 14.4 us -> 12.8 us  [call(): pl.pallas_call(kernel, in_specs=[away if at in far else near for at in ra...]
  transfers between devices with their start and end apart: 18 -> 18, of which waited for: 10 -> 9; matrix products, arithmetic and copies ran while one was open for 0% -> 0% of each run, Pallas kernels for 6% -> 6%
where the time goes in v4:
time: 102 us
  blocking collectives  45.1 us (44%)
  waiting for transfers between devices  24 us (24%)
  starting transfers between devices  17.6 us (17%)
  Pallas kernels  12.8 us (13%)
  other arithmetic  1.06 us (1%)
    all_to_all x2, blocking collectives, exchange(): lax.all_to_all(array, 'read', split_axis=0, concat_axis=0, tiled=True, ax...  45.1 us
    all_to_all x2, waiting for transfers between devices, exchange(): lax.all_to_all(array, 'read', split_axis=0, concat_axis=0, tiled=True, ax...  18 us
    pallas_call x6, Pallas kernels, call(): pl.pallas_call(kernel, in_specs=[away if at in far else near for at in ra...  12.8 us
    ppermute x16, starting transfers between devices, swap(): return lax.ppermute(array, 'read', [(i, i ^ bits) for i in range(count)])  9.15 us
    all_to_all x2, starting transfers between devices, exchange(): lax.all_to_all(array, 'read', split_axis=0, concat_axis=0, tiled=True, ax...  8.46 us
    ppermute x16, waiting for transfers between devices, swap(): return lax.ppermute(array, 'read', [(i, i ^ bits) for i in range(count)])  6.02 us
  transfers between devices with their start and end apart: 18, of which 9 were waited for; matrix products, arithmetic and copies ran while one was open for 0% of the time, Pallas kernels for 6%

profile of v4, /device:TPU:0, one launch (start us, length us, event | category | flops | bytes accessed | tf_op | source)
XLA Modules:
  0.0 101.5 jit_solution(4297159687469744472)
XLA Ops:
  0.6 1.1 %pad_maximum_fusion = bf16[2,4,32,768]{3,2,1,0:T(8,128)(2,1)S(1)} fusion(bf16[1,4,32,768]{3,2,1,0:T(8,128)(2,1)} %bitcast.13, bf16[1,4,32,768]{3,2,1,0:T(8,128)(2,1)} %bitcast.14), kind=kLoop, calls=%fused_computation | loop fusion | flops 196608 | bytes 786432 | tf_op jit(solution)/shard_map/stack | solution.py:387
  1.7 0.2 copy.7
  1.9 20.3 %all_to_all.26 = bf16[32,8,768]{2,1,0:T(8,128)(2,1)S(1)} all-to-all(bf16[32,8,768]{2,1,0:T(8,128)(2,1)S(1)} %copy.7), channel_id=1, replica_groups=mesh['read'=32,'pos'=1] {'read'}, dimensions={0} | all-to-all | bytes 786432 | tf_op jit(solution)/shard_map/all_to_all | solution.py:346
  22.2 0.0 collective-permute-start
  22.2 1.7 %collective-permute-done.other = bf16[256,768]{1,0:T(8,128)(2,1)S(1)} collective-permute-done((bf16[256,768]{1,0:T(8,128)(2,1)S(1)}, bf16[256,768]{1,0:T(8,128)(2,1)S(1)}, u32[]{:S(2)}, u32[]{:S(2)}) %collective-permute-start) | collective-permute-done | bytes 393248 | tf_op jit(solution)/shard_map/ppermute | solution.py:384
  23.9 4.2 %shard_map.68 = (bf16[3,256,384]{2,1,0:T(8,128)(2,1)S(1)}, bf16[16,96,128]{2,1,0:T(8,128)(2,1)}, f32[128,768]{1,0:T(8,128)S(1)}, f32[128,128]{1,0:T(8,128)S(1)},...) custom-call(bf16[256,768]{1,0:T(8,128)(2,1)S(1)} %bitcast.11, ...), custom_call_target="tpu_custom_call" | custom-call | tf_op jit(solution)/shard_map/pallas_call | solution.py:357
  28.1 3.7 %all-to-all-start.1 = ((bf16[16,96,128]{2,1,0:T(8,128)(2,1)}), bf16[16,96,128]{2,1,0:T(8,128)(2,1)S(1)}, u32[]{:S(2)}, u32[]{:S(2)}) async-start(bf16[16,96,128]{2,1,0:T(8,128)(2,1)} %get-tuple-element.27), calls=%async_computation.1 | async-start | bytes 786432 | tf_op jit(solution)/shard_map/all_to_all | solution.py:346
  31.8 1.9 %collective-permute-start.1 = (bf16[256,384]{1,0:T(8,128)(2,1)S(1)}, bf16[256,384]{1,0:T(8,128)(2,1)S(1)}, u32[]{:S(2)}, u32[]{:S(2)}) collective-permute-start(bf16[256,384]{1,0:T(8,128)(2,1)S(1)} %get-tuple-element.28), channel_id=1, source_target_pairs={{0,2},{1,3},{2,0},{3,1},{4,6},{5,7},{6,4},{7,5},{8,10},{9,11},{10,... | collective-permute-start | bytes 589832 | tf_op jit(solution)/shard_map/ppermute | solution.py:384
  33.7 1.5 %collective-permute-start.2 = (bf16[256,384]{1,0:T(8,128)(2,1)S(1)}, bf16[256,384]{1,0:T(8,128)(2,1)S(1)}, u32[]{:S(2)}, u32[]{:S(2)}) collective-permute-start(bf16[256,384]{1,0:T(8,128)(2,1)S(1)} %get-tuple-element.29), channel_id=1, source_target_pairs={{0,4},{1,5},{2,6},{3,7},{4,0},{5,1},{6,2},{7,3},{8,12},{9,13},{10,... | collective-permute-start | bytes 589832 | tf_op jit(solution)/shard_map/ppermute | solution.py:384
  35.2 0.2 collective-permute-start.3
  35.4 9.6 %all-to-all-done.1.parts = bf16[16,96,128]{2,1,0:T(8,128)(2,1)S(1)} async-done(((bf16[16,96,128]{2,1,0:T(8,128)(2,1)}), bf16[16,96,128]{2,1,0:T(8,128)(2,1)S(1)}, u32[]{:S(2)}, u32[]{:S(2)}) %all-to-all-start.1) | async-done | bytes 393248 | tf_op jit(solution)/shard_map/all_to_all | solution.py:346
  44.9 1.0 shard_map.69
  45.9 0.0 collective-permute-done.1.refs_1_
  45.9 0.0 collective-permute-done.2.refs_2_
  45.9 2.1 %collective-permute-done.3.refs_3_ = bf16[256,384]{1,0:T(8,128)(2,1)S(1)} collective-permute-done((bf16[256,384]{1,0:T(8,128)(2,1)S(1)}, bf16[256,384]{1,0:T(8,128)(2,1)S(1)}, u32[]{:S(2)}, u32[]{:S(2)}) %collective-permute-start.3) | collective-permute-done | bytes 196640 | tf_op jit(solution)/shard_map/ppermute | solution.py:384
  48.0 4.8 %all-to-all-start.2 = ((bf16[16,96,128]{2,1,0:T(8,128)(2,1)}), bf16[16,96,128]{2,1,0:T(8,128)(2,1)S(1)}, u32[]{:S(2)}, u32[]{:S(2)}) async-start(bf16[16,96,128]{2,1,0:T(8,128)(2,1)} %shard_map.69), calls=%async_computation.2 | async-start | bytes 786432 | tf_op jit(solution)/shard_map/all_to_all | solution.py:346
  52.8 1.9 %collective-permute-start.4 = (bf16[128,768]{1,0:T(8,128)(2,1)}, bf16[128,768]{1,0:T(8,128)(2,1)S(1)}, u32[]{:S(2)}, u32[]{:S(2)}) collective-permute-start(bf16[128,768]{1,0:T(8,128)(2,1)} %get-tuple-element.37), channel_id=1, source_target_pairs={{0,2},{1,3},{2,0},{3,1},{4,6},{5,7},{6,4},{7,5},{8,10},{9,11},{10,... | collective-permute-start | bytes 589832 | tf_op jit(solution)/shard_map/ppermute | solution.py:384
  54.7 1.5 %collective-permute-start.5 = (bf16[128,768]{1,0:T(8,128)(2,1)}, bf16[128,768]{1,0:T(8,128)(2,1)S(1)}, u32[]{:S(2)}, u32[]{:S(2)}) collective-permute-start(bf16[128,768]{1,0:T(8,128)(2,1)} %get-tuple-element.38), channel_id=1, source_target_pairs={{0,4},{1,5},{2,6},{3,7},{4,0},{5,1},{6,2},{7,3},{8,12},{9,13},{10,... | collective-permute-start | bytes 589832 | tf_op jit(solution)/shard_map/ppermute | solution.py:384
  56.2 0.2 collective-permute-start.6
  56.3 0.0 collective-permute-start.9
  56.3 0.5 collective-permute-start.10
  56.8 8.5 %all-to-all-done.2.pairs = bf16[16,96,128]{2,1,0:T(8,128)(2,1)S(1)} async-done(((bf16[16,96,128]{2,1,0:T(8,128)(2,1)}), bf16[16,96,128]{2,1,0:T(8,128)(2,1)S(1)}, u32[]{:S(2)}, u32[]{:S(2)}) %all-to-all-start.2) | async-done | bytes 393248 | tf_op jit(solution)/shard_map/all_to_all | solution.py:346
  65.3 2.9 %shard_map.70 = (f32[128,768]{1,0:T(8,128)S(1)}, f32[128,768]{1,0:T(8,128)S(1)}) custom-call(bf16[16,96,128]{2,1,0:T(8,128)(2,1)S(1)} %all-to-all-done.2.pairs, bf16[3,256,384]{2,1,0:T(8,128)(2,1)S(1)} %get-tuple-element.32.proj, f32[128,128]{1,0:T(8,128)S(1)} %get-tuple-element.33.bounds, bf16[4,768,768]{2,1,0:T(8,128)(2,1)} %weights.3), custom_call_target="tpu_custom_call" | custom-call | tf_op jit(solution)/shard_map/pallas_call | solution.py:357
  68.2 0.0 collective-permute-done.4.refs_9_
  68.2 0.1 collective-permute-start.11
  68.3 0.0 collective-permute-done.5.refs_10_
  68.3 0.5 collective-permute-start.12
  68.8 0.0 collective-permute-done.6.refs_11_
  68.8 0.1 collective-permute-start.8
  68.9 0.0 collective-permute-done.9.refs_4_
  68.9 0.4 collective-permute-start.7
  69.3 0.0 collective-permute-done.10.refs_5_
  69.3 0.1 collective-permute-start.13
  69.4 0.3 collective-permute-done.11.refs_6_
  69.7 0.1 collective-permute-start.14
  69.9 0.1 collective-permute-done.12.refs_7_
  70.0 0.2 collective-permute-start.15
  70.2 1.2 %collective-permute-done.13.refs_13_ = bf16[128,768]{1,0:T(8,128)(2,1)S(1)} collective-permute-done((bf16[128,768]{1,0:T(8,128)(2,1)S(1)}, bf16[128,768]{1,0:T(8,128)(2,1)S(1)}, u32[]{:S(2)}, u32[]{:S(2)}) %collective-permute-start.13) | collective-permute-done | bytes 196640 | tf_op jit(solution)/shard_map/ppermute | solution.py:384
  71.4 0.3 collective-permute-done.14.refs_14_
  71.7 0.3 collective-permute-done.15.refs_15_
  72.0 0.0 collective-permute-done.8.pairs_other
  72.0 2.7 %shard_map.71.product = bf16[768,384]{1,0:T(8,128)(2,1)S(1)} custom-call(bf16[16,96,128]{2,1,0:T(8,128)(2,1)S(1)} %all-to-all-done.2.pairs, bf16[16,96,128]{2,1,0:T(8,128)(2,1)S(1)} %collective-permute-done.8.pairs_other, f32[128,128]{1,0:T(8,128)S(1)} %get-tuple-element.33.bounds, bf16[256,384]{1,0:T(8,128)(2,1)S(1)} %get-tuple-element.43.refs_0_, ...), custom_call_target="tpu_custom_call" | custom-call | tf_op jit(solution)/shard_map/pallas_call | solution.py:357
  74.7 0.0 collective-permute-done.7.grad_recv
  74.7 0.7 shard_map.72
  75.4 24.8 %all_to_all.27.arrived = bf16[32,24,512]{2,1,0:T(8,128)(2,1)S(1)} all-to-all(bf16[32,24,512]{2,1,0:T(8,128)(2,1)S(1)} %bitcast.9), channel_id=1, replica_groups=mesh['read'=32,'pos'=1] {'read'}, dimensions={0} | all-to-all | bytes 1572864 | tf_op jit(solution)/shard_map/all_to_all | solution.py:346
  100.3 1.3 %shard_map.73 = (bf16[4,32,768]{2,1,0:T(8,128)(2,1)}, f32[24,3072]{1,0:T(8,128)}) custom-call(bf16[32,24,512]{2,1,0:T(8,128)(2,1)S(1)} %all_to_all.27.arrived), custom_call_target="tpu_custom_call" | custom-call | tf_op jit(solution)/shard_map/pallas_call | solution.py:357
Async XLA Ops:
  22.2 1.7 %collective-permute-start = (bf16[256,768]{1,0:T(8,128)(2,1)S(1)}, bf16[256,768]{1,0:T(8,128)(2,1)S(1)}, u32[]{:S(2)}, u32[]{:S(2)}) collective-permute-start(bf16[256,768]{1,0:T(8,128)(2,1)S(1)} %bitcast.10), channel_id=1, source_target_pairs={{0,1},{1,0},{2,3},{3,2},{4,5},{5,4},{6,7},{7,6},{8,9},{9,8},{10,11... | collective-permute-start | bytes 1179656 | tf_op jit(solution)/shard_map/ppermute | solution.py:384
  28.1 16.8 %all-to-all-start.1 = ((bf16[16,96,128]{2,1,0:T(8,128)(2,1)}), bf16[16,96,128]{2,1,0:T(8,128)(2,1)S(1)}, u32[]{:S(2)}, u32[]{:S(2)}) async-start(bf16[16,96,128]{2,1,0:T(8,128)(2,1)} %get-tuple-element.27), calls=%async_computation.1 | async-start | bytes 786432 | tf_op jit(solution)/shard_map/all_to_all | solution.py:346
  31.8 14.1 %collective-permute-start.1 = (bf16[256,384]{1,0:T(8,128)(2,1)S(1)}, bf16[256,384]{1,0:T(8,128)(2,1)S(1)}, u32[]{:S(2)}, u32[]{:S(2)}) collective-permute-start(bf16[256,384]{1,0:T(8,128)(2,1)S(1)} %get-tuple-element.28), channel_id=1, source_target_pairs={{0,2},{1,3},{2,0},{3,1},{4,6},{5,7},{6,4},{7,5},{8,10},{9,11},{10,... | collective-permute-start | bytes 589832 | tf_op jit(solution)/shard_map/ppermute | solution.py:384
  33.7 12.1 %collective-permute-start.2 = (bf16[256,384]{1,0:T(8,128)(2,1)S(1)}, bf16[256,384]{1,0:T(8,128)(2,1)S(1)}, u32[]{:S(2)}, u32[]{:S(2)}) collective-permute-start(bf16[256,384]{1,0:T(8,128)(2,1)S(1)} %get-tuple-element.29), channel_id=1, source_target_pairs={{0,4},{1,5},{2,6},{3,7},{4,0},{5,1},{6,2},{7,3},{8,12},{9,13},{10,... | collective-permute-start | bytes 589832 | tf_op jit(solution)/shard_map/ppermute | solution.py:384
  35.2 12.8 %collective-permute-start.3 = (bf16[256,384]{1,0:T(8,128)(2,1)S(1)}, bf16[256,384]{1,0:T(8,128)(2,1)S(1)}, u32[]{:S(2)}, u32[]{:S(2)}) collective-permute-start(bf16[256,384]{1,0:T(8,128)(2,1)S(1)} %get-tuple-element.30), channel_id=1, source_target_pairs={{0,6},{1,7},{2,4},{3,5},{4,2},{5,3},{6,0},{7,1},{8,14},{9,15},{10,... | collective-permute-start | bytes 589832 | tf_op jit(solution)/shard_map/ppermute | solution.py:384
  48.0 17.3 %all-to-all-start.2 = ((bf16[16,96,128]{2,1,0:T(8,128)(2,1)}), bf16[16,96,128]{2,1,0:T(8,128)(2,1)S(1)}, u32[]{:S(2)}, u32[]{:S(2)}) async-start(bf16[16,96,128]{2,1,0:T(8,128)(2,1)} %shard_map.69), calls=%async_computation.2 | async-start | bytes 786432 | tf_op jit(solution)/shard_map/all_to_all | solution.py:346
  52.8 15.4 %collective-permute-start.4 = (bf16[128,768]{1,0:T(8,128)(2,1)}, bf16[128,768]{1,0:T(8,128)(2,1)S(1)}, u32[]{:S(2)}, u32[]{:S(2)}) collective-permute-start(bf16[128,768]{1,0:T(8,128)(2,1)} %get-tuple-element.37), channel_id=1, source_target_pairs={{0,2},{1,3},{2,0},{3,1},{4,6},{5,7},{6,4},{7,5},{8,10},{9,11},{10,... | collective-permute-start | bytes 589832 | tf_op jit(solution)/shard_map/ppermute | solution.py:384
  54.7 13.6 %collective-permute-start.5 = (bf16[128,768]{1,0:T(8,128)(2,1)}, bf16[128,768]{1,0:T(8,128)(2,1)S(1)}, u32[]{:S(2)}, u32[]{:S(2)}) collective-permute-start(bf16[128,768]{1,0:T(8,128)(2,1)} %get-tuple-element.38), channel_id=1, source_target_pairs={{0,4},{1,5},{2,6},{3,7},{4,0},{5,1},{6,2},{7,3},{8,12},{9,13},{10,... | collective-permute-start | bytes 589832 | tf_op jit(solution)/shard_map/ppermute | solution.py:384
  56.2 12.6 %collective-permute-start.6 = (bf16[128,768]{1,0:T(8,128)(2,1)}, bf16[128,768]{1,0:T(8,128)(2,1)S(1)}, u32[]{:S(2)}, u32[]{:S(2)}) collective-permute-start(bf16[128,768]{1,0:T(8,128)(2,1)} %get-tuple-element.39), channel_id=1, source_target_pairs={{0,6},{1,7},{2,4},{3,5},{4,2},{5,3},{6,0},{7,1},{8,14},{9,15},{10,... | collective-permute-start | bytes 589832 | tf_op jit(solution)/shard_map/ppermute | solution.py:384
  56.3 12.6 %collective-permute-start.9 = (bf16[256,384]{1,0:T(8,128)(2,1)S(1)}, bf16[256,384]{1,0:T(8,128)(2,1)S(1)}, u32[]{:S(2)}, u32[]{:S(2)}) collective-permute-start(bf16[256,384]{1,0:T(8,128)(2,1)S(1)} %get-tuple-element.43.refs_0_), channel_id=1, source_target_pairs={{0,1},{1,0},{2,3},{3,2},{4,5},{5,4},{6,7},{7,6},{8,9},{9,8},{10,11... | collective-permute-start | bytes 589832 | tf_op jit(solution)/shard_map/ppermute | solution.py:384
  56.3 13.0 %collective-permute-start.10 = (bf16[256,384]{1,0:T(8,128)(2,1)S(1)}, bf16[256,384]{1,0:T(8,128)(2,1)}, u32[]{:S(2)}, u32[]{:S(2)}) collective-permute-start(bf16[256,384]{1,0:T(8,128)(2,1)S(1)} %collective-permute-done.1.refs_1_), channel_id=1, source_target_pairs={{0,1},{1,0},{2,3},{3,2},{4,5},{5,4},{6,7},{7,6},{8,9},{9,8},{10,11... | collective-permute-start | bytes 589832 | tf_op jit(solution)/shard_map/ppermute | solution.py:384
  68.2 1.5 %collective-permute-start.11 = (bf16[256,384]{1,0:T(8,128)(2,1)S(1)}, bf16[256,384]{1,0:T(8,128)(2,1)S(1)}, u32[]{:S(2)}, u32[]{:S(2)}) collective-permute-start(bf16[256,384]{1,0:T(8,128)(2,1)S(1)} %collective-permute-done.2.refs_2_), channel_id=1, source_target_pairs={{0,1},{1,0},{2,3},{3,2},{4,5},{5,4},{6,7},{7,6},{8,9},{9,8},{10,11... | collective-permute-start | bytes 589832 | tf_op jit(solution)/shard_map/ppermute | solution.py:384
  68.3 1.7 %collective-permute-start.12 = (bf16[256,384]{1,0:T(8,128)(2,1)S(1)}, bf16[256,384]{1,0:T(8,128)(2,1)S(1)}, u32[]{:S(2)}, u32[]{:S(2)}) collective-permute-start(bf16[256,384]{1,0:T(8,128)(2,1)S(1)} %collective-permute-done.3.refs_3_), channel_id=1, source_target_pairs={{0,1},{1,0},{2,3},{3,2},{4,5},{5,4},{6,7},{7,6},{8,9},{9,8},{10,11... | collective-permute-start | bytes 589832 | tf_op jit(solution)/shard_map/ppermute | solution.py:384
  68.8 3.2 %collective-permute-start.8 = (bf16[16,96,128]{2,1,0:T(8,128)(2,1)S(1)}, bf16[16,96,128]{2,1,0:T(8,128)(2,1)S(1)}, u32[]{:S(2)}, u32[]{:S(2)}) collective-permute-start(bf16[16,96,128]{2,1,0:T(8,128)(2,1)S(1)} %all-to-all-done.2.pairs), channel_id=1, source_target_pairs={{0,1},{1,0},{2,3},{3,2},{4,5},{5,4},{6,7},{7,6},{8,9},{9,8},{10,11... | collective-permute-start | bytes 1179656 | tf_op jit(solution)/shard_map/ppermute | solution.py:384
  68.9 5.8 %collective-permute-start.7 = (f32[128,768]{1,0:T(8,128)S(1)}, f32[128,768]{1,0:T(8,128)S(1)}, u32[]{:S(2)}, u32[]{:S(2)}) collective-permute-start(f32[128,768]{1,0:T(8,128)S(1)} %get-tuple-element.40), channel_id=1, source_target_pairs={{0,1},{1,0},{2,3},{3,2},{4,5},{5,4},{6,7},{7,6},{8,9},{9,8},{10,11... | collective-permute-start | bytes 1179656 | tf_op jit(solution)/shard_map/ppermute | solution.py:384
  69.3 2.1 %collective-permute-start.13 = (bf16[128,768]{1,0:T(8,128)(2,1)S(1)}, bf16[128,768]{1,0:T(8,128)(2,1)S(1)}, u32[]{:S(2)}, u32[]{:S(2)}) collective-permute-start(bf16[128,768]{1,0:T(8,128)(2,1)S(1)} %collective-permute-done.4.refs_9_), channel_id=1, source_target_pairs={{0,1},{1,0},{2,3},{3,2},{4,5},{5,4},{6,7},{7,6},{8,9},{9,8},{10,11... | collective-permute-start | bytes 589832 | tf_op jit(solution)/shard_map/ppermute | solution.py:384
  69.7 2.0 %collective-permute-start.14 = (bf16[128,768]{1,0:T(8,128)(2,1)S(1)}, bf16[128,768]{1,0:T(8,128)(2,1)S(1)}, u32[]{:S(2)}, u32[]{:S(2)}) collective-permute-start(bf16[128,768]{1,0:T(8,128)(2,1)S(1)} %collective-permute-done.5.refs_10_), channel_id=1, source_target_pairs={{0,1},{1,0},{2,3},{3,2},{4,5},{5,4},{6,7},{7,6},{8,9},{9,8},{10,11... | collective-permute-start | bytes 589832 | tf_op jit(solution)/shard_map/ppermute | solution.py:384
  70.0 2.0 %collective-permute-start.15 = (bf16[128,768]{1,0:T(8,128)(2,1)S(1)}, bf16[128,768]{1,0:T(8,128)(2,1)S(1)}, u32[]{:S(2)}, u32[]{:S(2)}) collective-permute-start(bf16[128,768]{1,0:T(8,128)(2,1)S(1)} %collective-permute-done.6.refs_11_), channel_id=1, source_target_pairs={{0,1},{1,0},{2,3},{3,2},{4,5},{5,4},{6,7},{7,6},{8,9},{9,8},{10,11... | collective-permute-start | bytes 589832 | tf_op jit(solution)/shard_map/ppermute | solution.py:384

commit v5 on v4

--- a/solution.py
+++ b/solution.py
@@ -223,11 +223,9 @@
     other[...] = total[cells:]
 
 
-def weight_kernel(pairs, pairs_other, bounds, *refs, col_dev):
-    ops, ops_other, lefts, lefts_other = (
-        refs[at * KINDS : (at + 1) * KINDS] for at in range(4)
-    )
-    product, right, right_other = refs[4 * KINDS :]
+def weight_kernel(pairs, bounds, *refs, col_dev):
+    ops, lefts, lefts_other = (refs[at * KINDS : (at + 1) * KINDS] for at in range(3))
+    product, spare, right = refs[3 * KINDS :]
     cells, width = lefts[0].shape
     half = ops[0].shape[1]
     me, core, kind = position()
@@ -235,31 +233,6 @@
     low = first_heads(cells, 2 * KINDS * LANES)
     use_probs = kind >= 2
     use_flip = (kind == 1) | (kind == 2)
-
-    def gradient(source, operands, covered, out, swapped):
-        for pair in range(half // LANES):
-            cat = jnp.concatenate([slab(operand[...], pair) for operand in operands], axis=1)
-            maps = []
-            for odd in range(2):
-                probs, mixed = head_maps(source, 2 * pair + odd, cells)
-                if swapped:
-                    chosen = probs
-                else:
-                    chosen = jnp.where(use_probs, probs, mixed)
-                    chosen = jnp.where(use_flip, chosen.T, chosen)
-                maps.append(chosen.astype(BF16))
-            result = dot(jnp.concatenate(maps, axis=0), cat)
-            result = jnp.where(low, result[:cells], result[cells:])
-            if covered is not None:
-                result = result * covered
-            result = result.astype(BF16)
-            lanes = slice(pair * LANES, (pair + 1) * LANES)
-            for at in range(2 * KINDS):
-                to = at ^ 1 if swapped else at
-                out[to * cells : (to + 1) * cells, lanes] = result[
-                    :, at * LANES : (at + 1) * LANES
-                ]
-
     first, last = bounds[:, 0:1], bounds[:, 1:2]
     masks = []
     for at in range(2 * KINDS):
@@ -267,33 +240,47 @@
         masks.append(jnp.broadcast_to(mask, (cells, LANES)))
     covered = jnp.concatenate(masks, axis=1)
     covered = jnp.where(kind == KINDS - 1, 1.0, covered)
-    gradient(pairs, ops, covered, right, False)
+
+    for pair in range(half // LANES):
+        cat = jnp.concatenate([slab(operand[...], pair) for operand in ops], axis=1)
+        maps = []
+        for odd in range(2):
+            probs, mixed = head_maps(pairs, 2 * pair + odd, cells)
+            chosen = jnp.where(use_probs, probs, mixed)
+            chosen = jnp.where(use_flip, chosen.T, chosen)
+            maps.append(chosen.astype(BF16))
+        result = dot(jnp.concatenate(maps, axis=0), cat)
+        result = (jnp.where(low, result[:cells], result[cells:]) * covered).astype(BF16)
+        lanes = slice(pair * LANES, (pair + 1) * LANES)
+        for at in range(2 * KINDS):
+            right[at * cells : (at + 1) * cells, lanes] = result[
+                :, at * LANES : (at + 1) * LANES
+            ]
+
+    left = jnp.concatenate(
+        [ref[...] for pair in zip(lefts, lefts_other) for ref in pair], axis=0
+    )
 
     @pl.when(kind < KINDS - 1)
     def _():
-        left = jnp.concatenate(
-            [ref[...] for pair in zip(lefts, lefts_other) for ref in pair], axis=0
-        )
         product[...] = dot(left, right[...], (0, 0)).astype(BF16)
 
     @pl.when(kind == KINDS - 1)
     def _():
-        gradient(pairs_other, ops_other, None, right_other, True)
-        for side in range(CORES):
-
-            @pl.when(core == side)
-            def _():
-                lanes = slice(side * half, (side + 1) * half)
-                ups = jnp.concatenate(
-                    [ref[:, lanes] for pair in zip(lefts, lefts_other) for ref in pair], axis=0
-                )
-                mine = dot(right[...], ups, (0, 0)).astype(BF16)
-                theirs = dot(right_other[...], ups, (0, 0)).astype(BF16)
-                product[side * half : (side + 1) * half, :] = mine
-                product[(1 - side) * half : (2 - side) * half, :] = theirs
-
-
-def pack_kernel(grad_own, grad_recv, normed, inverse, product, payload, *, rows):
+        rows = dot(right[...], left, (0, 0)).astype(BF16)
+
+        @pl.when(core == 0)
+        def _():
+            product[:half] = rows[:, :half]
+            spare[...] = rows[:, half:]
+
+        @pl.when(core == 1)
+        def _():
+            product[:half] = rows[:, half:]
+            spare[...] = rows[:, :half]
+
+
+def pack_kernel(grad_own, grad_recv, normed, inverse, product, spare, payload, *, rows):
     cells, width = normed.shape
     tiles = width // LANES
     half = product.shape[1]
@@ -310,7 +297,25 @@
         tile, cell = lax.div(spot, cells), lax.rem(spot, cells)
         return at == lax.div(cell, rows) * group + tile * rows + lax.rem(cell, rows)
 
-    payload[:, :half] = product[...]
+    _, core, kind = position()
+
+    @pl.when((kind < KINDS - 1) | (core == 0))
+    def _():
+        payload[:half, :half] = product[:half]
+
+    @pl.when(kind < KINDS - 1)
+    def _():
+        payload[half:, :half] = product[half:]
+
+    @pl.when((kind == KINDS - 1) & (core == 0))
+    def _():
+        payload[half:, :half] = spare[...]
+
+    @pl.when((kind == KINDS - 1) & (core == 1))
+    def _():
+        payload[:half, :half] = spare[...]
+        payload[half:, :half] = product[:half]
+
     payload[:, half:] = dot(indicator(width, tiles * cells, place), stack).astype(BF16)
 
 
@@ -413,7 +418,7 @@
     ops, lefts = pieces[:KINDS], pieces[KINDS:]
 
     parts = exchange(tied, same_core)
-    moved = [swap(ops[k], CORES * k) for k in range(1, KINDS)]
+    moved = [swap(lefts[k], CORES * k) for k in range(1, KINDS)]
     if pos_count > 1:
         parts = lax.psum(jnp.sum(parts.astype(F32), 0, keepdims=True), "pos")
     copies = call(
@@ -423,11 +428,10 @@
         8,
     )
     copies, *moved = lax.optimization_barrier((copies, *moved))
-    ops = [ops[0], *moved]
+    lefts = [lefts[0], *moved]
+    lefts_other = [left_other] + [swap(a, 1) for a in moved]
     pairs = exchange(copies, same_core)
-    lefts = [lefts[0]] + [swap(lefts[k], CORES * k) for k in range(1, KINDS)]
-    ops_other = [swap(a, 1) for a in ops]
-    pairs_other = swap(pairs, 1)
+    ops = [ops[0]] + [swap(ops[k], CORES * k) for k in range(1, KINDS)]
 
     grad_own, grad_other = call(
         functools.partial(back_kernel, col_dev=col_dev),
@@ -441,22 +445,22 @@
             pltpu.SemaphoreType.DMA,
         ],
     )
-    grad_other, *lefts = lax.optimization_barrier((grad_other, *lefts))
-    lefts_other = [left_other] + [swap(a, 1) for a in lefts[1:]]
+    grad_other, *ops = lax.optimization_barrier((grad_other, *ops))
     grad_recv = swap(grad_other, 1)
 
     cells = 2 * KINDS * reads
-    product = call(
+    product, spare = call(
         functools.partial(weight_kernel, col_dev=col_dev),
-        (pairs, pairs_other, bounds, *ops, *ops_other, *lefts, *lefts_other),
-        shape((width, half), BF16),
+        (pairs, bounds, *ops, *lefts, *lefts_other),
+        (shape((width, half), BF16), shape((half, half), BF16)),
         20,
         (),
-        [pltpu.VMEM((cells, half), BF16), pltpu.VMEM((cells, half), BF16)],
-    )
+        [pltpu.VMEM((cells, half), BF16)],
+    )
+    spare = swap(spare, 1)
     payload = call(
         functools.partial(pack_kernel, rows=rows),
-        (grad_own, grad_recv, normed, inverse, product),
+        (grad_own, grad_recv, normed, inverse, product, spare),
         shape((width, half + LANES), BF16),
         8,
     )

time: 102 us -> 99.9 us (0.979)
    all_to_all x2, waiting for transfers between devices: 18 us -> 10 us  [exchange(): lax.all_to_all(array, 'read', split_axis=0, concat_axis=0, tiled=True, ax...]
    ppermute x16 -> x12, waiting for transfers between devices: 6.02 us -> 13.1 us  [swap(): return lax.ppermute(array, 'read', [(i, i ^ bits) for i in range(count)])]
    ppermute x16 -> x12, starting transfers between devices: 9.15 us -> 8.19 us  [swap(): return lax.ppermute(array, 'read', [(i, i ^ bits) for i in range(count)])]
  transfers between devices with their start and end apart: 18 -> 14, of which waited for: 9 -> 7; matrix products, arithmetic and copies ran while one was open for 0% -> 0% of each run, Pallas kernels for 6% -> 7%
where the time goes in v5:
time: 99.9 us; the launch traced here: 99.5 us
  blocking collectives  44.7 us (45%)
  waiting for transfers between devices  23.1 us (23%)
  starting transfers between devices  16.7 us (17%)
  Pallas kernels  13 us (13%)
  other arithmetic  1.06 us (1%)
    all_to_all x2, blocking collectives, exchange(): lax.all_to_all(array, 'read', split_axis=0, concat_axis=0, tiled=True, ax...  44.7 us
    ppermute x12, waiting for transfers between devices, swap(): return lax.ppermute(array, 'read', [(i, i ^ bits) for i in range(count)])  13.1 us
    pallas_call x6, Pallas kernels, call(): pl.pallas_call(kernel, in_specs=[away if at in far else near for at in ra...  13 us
    all_to_all x2, waiting for transfers between devices, exchange(): lax.all_to_all(array, 'read', split_axis=0, concat_axis=0, tiled=True, ax...  10 us
    all_to_all x2, starting transfers between devices, exchange(): lax.all_to_all(array, 'read', split_axis=0, concat_axis=0, tiled=True, ax...  8.47 us
    ppermute x12, starting transfers between devices, swap(): return lax.ppermute(array, 'read', [(i, i ^ bits) for i in range(count)])  8.19 us
  transfers between devices with their start and end apart: 14, of which 7 were waited for; matrix products, arithmetic and copies ran while one was open for 0% of the time, Pallas kernels for 7%

profile of v5, /device:TPU:0, one launch (start us, length us, event | category | flops | bytes accessed | tf_op | source)
XLA Modules:
  0.0 99.5 jit_solution(3372555327861105439)
XLA Ops:
  0.6 1.1 %pad_maximum_fusion = bf16[2,4,32,768]{3,2,1,0:T(8,128)(2,1)S(1)} fusion(bf16[1,4,32,768]{3,2,1,0:T(8,128)(2,1)} %bitcast.13, bf16[1,4,32,768]{3,2,1,0:T(8,128)(2,1)} %bitcast.14), kind=kLoop, calls=%fused_computation | loop fusion | flops 196608 | bytes 786432 | tf_op jit(solution)/shard_map/stack | solution.py:392
  1.7 0.2 copy.7
  1.9 20.3 %all_to_all.26 = bf16[32,8,768]{2,1,0:T(8,128)(2,1)S(1)} all-to-all(bf16[32,8,768]{2,1,0:T(8,128)(2,1)S(1)} %copy.7), channel_id=1, replica_groups=mesh['read'=32,'pos'=1] {'read'}, dimensions={0} | all-to-all | bytes 786432 | tf_op jit(solution)/shard_map/all_to_all | solution.py:351
  22.2 0.0 collective-permute-start
  22.2 1.7 %collective-permute-done.other = bf16[256,768]{1,0:T(8,128)(2,1)S(1)} collective-permute-done((bf16[256,768]{1,0:T(8,128)(2,1)S(1)}, bf16[256,768]{1,0:T(8,128)(2,1)S(1)}, u32[]{:S(2)}, u32[]{:S(2)}) %collective-permute-start) | collective-permute-done | bytes 393248 | tf_op jit(solution)/shard_map/ppermute | solution.py:389
  23.9 4.2 %shard_map.68 = (bf16[3,256,384]{2,1,0:T(8,128)(2,1)S(1)}, bf16[16,96,128]{2,1,0:T(8,128)(2,1)}, f32[128,768]{1,0:T(8,128)S(1)}, f32[128,128]{1,0:T(8,128)S(1)},...) custom-call(bf16[256,768]{1,0:T(8,128)(2,1)S(1)} %bitcast.11, ...), custom_call_target="tpu_custom_call" | custom-call | tf_op jit(solution)/shard_map/pallas_call | solution.py:362
  28.1 3.7 %all-to-all-start.1 = ((bf16[16,96,128]{2,1,0:T(8,128)(2,1)}), bf16[16,96,128]{2,1,0:T(8,128)(2,1)S(1)}, u32[]{:S(2)}, u32[]{:S(2)}) async-start(bf16[16,96,128]{2,1,0:T(8,128)(2,1)} %get-tuple-element.29), calls=%async_computation.1 | async-start | bytes 786432 | tf_op jit(solution)/shard_map/all_to_all | solution.py:351
  31.8 1.9 %collective-permute-start.1 = (bf16[128,768]{1,0:T(8,128)(2,1)S(1)}, bf16[128,768]{1,0:T(8,128)(2,1)S(1)}, u32[]{:S(2)}, u32[]{:S(2)}) collective-permute-start(bf16[128,768]{1,0:T(8,128)(2,1)S(1)} %get-tuple-element.30), channel_id=1, source_target_pairs={{0,2},{1,3},{2,0},{3,1},{4,6},{5,7},{6,4},{7,5},{8,10},{9,11},{10,... | collective-permute-start | bytes 589832 | tf_op jit(solution)/shard_map/ppermute | solution.py:389
  33.7 1.5 %collective-permute-start.2 = (bf16[128,768]{1,0:T(8,128)(2,1)S(1)}, bf16[128,768]{1,0:T(8,128)(2,1)S(1)}, u32[]{:S(2)}, u32[]{:S(2)}) collective-permute-start(bf16[128,768]{1,0:T(8,128)(2,1)S(1)} %get-tuple-element.31), channel_id=1, source_target_pairs={{0,4},{1,5},{2,6},{3,7},{4,0},{5,1},{6,2},{7,3},{8,12},{9,13},{10,... | collective-permute-start | bytes 589832 | tf_op jit(solution)/shard_map/ppermute | solution.py:389
  35.2 0.2 collective-permute-start.3
  35.4 9.5 %all-to-all-done.1.parts = bf16[16,96,128]{2,1,0:T(8,128)(2,1)S(1)} async-done(((bf16[16,96,128]{2,1,0:T(8,128)(2,1)}), bf16[16,96,128]{2,1,0:T(8,128)(2,1)S(1)}, u32[]{:S(2)}, u32[]{:S(2)}) %all-to-all-start.1) | async-done | bytes 393248 | tf_op jit(solution)/shard_map/all_to_all | solution.py:351
  44.9 1.0 shard_map.69
  45.9 0.0 collective-permute-done.1.refs_5_
  45.9 0.0 collective-permute-done.2.refs_6_
  45.9 2.1 %collective-permute-done.3.refs_7_ = bf16[128,768]{1,0:T(8,128)(2,1)S(1)} collective-permute-done((bf16[128,768]{1,0:T(8,128)(2,1)S(1)}, bf16[128,768]{1,0:T(8,128)(2,1)S(1)}, u32[]{:S(2)}, u32[]{:S(2)}) %collective-permute-start.3) | collective-permute-done | bytes 196640 | tf_op jit(solution)/shard_map/ppermute | solution.py:389
  48.0 4.8 %all-to-all-start.2 = ((bf16[16,96,128]{2,1,0:T(8,128)(2,1)}), bf16[16,96,128]{2,1,0:T(8,128)(2,1)S(1)}, u32[]{:S(2)}, u32[]{:S(2)}) async-start(bf16[16,96,128]{2,1,0:T(8,128)(2,1)} %shard_map.69), calls=%async_computation.2 | async-start | bytes 786432 | tf_op jit(solution)/shard_map/all_to_all | solution.py:351
  52.8 1.9 %collective-permute-start.4 = (bf16[256,384]{1,0:T(8,128)(2,1)}, bf16[256,384]{1,0:T(8,128)(2,1)S(1)}, u32[]{:S(2)}, u32[]{:S(2)}) collective-permute-start(bf16[256,384]{1,0:T(8,128)(2,1)} %get-tuple-element.39), channel_id=1, source_target_pairs={{0,2},{1,3},{2,0},{3,1},{4,6},{5,7},{6,4},{7,5},{8,10},{9,11},{10,... | collective-permute-start | bytes 589832 | tf_op jit(solution)/shard_map/ppermute | solution.py:389
  54.7 1.5 %collective-permute-start.5 = (bf16[256,384]{1,0:T(8,128)(2,1)}, bf16[256,384]{1,0:T(8,128)(2,1)S(1)}, u32[]{:S(2)}, u32[]{:S(2)}) collective-permute-start(bf16[256,384]{1,0:T(8,128)(2,1)} %get-tuple-element.40), channel_id=1, source_target_pairs={{0,4},{1,5},{2,6},{3,7},{4,0},{5,1},{6,2},{7,3},{8,12},{9,13},{10,... | collective-permute-start | bytes 589832 | tf_op jit(solution)/shard_map/ppermute | solution.py:389
  56.2 0.2 collective-permute-start.6
  56.3 0.0 collective-permute-start.8
  56.3 0.5 collective-permute-start.9
  56.8 8.0 %collective-permute-done.4.refs_1_ = bf16[256,384]{1,0:T(8,128)(2,1)S(1)} collective-permute-done((bf16[256,384]{1,0:T(8,128)(2,1)}, bf16[256,384]{1,0:T(8,128)(2,1)S(1)}, u32[]{:S(2)}, u32[]{:S(2)}) %collective-permute-start.4) | collective-permute-done | bytes 196640 | tf_op jit(solution)/shard_map/ppermute | solution.py:389
  64.8 0.0 collective-permute-start.10
  64.8 0.5 all-to-all-done.2.pairs
  65.3 2.9 %shard_map.70 = (f32[128,768]{1,0:T(8,128)S(1)}, f32[128,768]{1,0:T(8,128)S(1)}) custom-call(bf16[16,96,128]{2,1,0:T(8,128)(2,1)S(1)} %all-to-all-done.2.pairs, bf16[3,256,384]{2,1,0:T(8,128)(2,1)S(1)} %get-tuple-element.34.proj, f32[128,128]{1,0:T(8,128)S(1)} %get-tuple-element.35.bounds, bf16[4,768,768]{2,1,0:T(8,128)(2,1)} %weights.3), custom_call_target="tpu_custom_call" | custom-call | tf_op jit(solution)/shard_map/pallas_call | solution.py:362
  68.2 0.0 collective-permute-done.5.refs_2_
  68.2 0.1 collective-permute-done.6.refs_3_
  68.3 0.0 collective-permute-start.7
  68.3 0.0 collective-permute-done.8.refs_9_
  68.3 0.0 collective-permute-done.9.refs_10_
  68.3 0.0 collective-permute-done.10.refs_11_
  68.3 2.9 %shard_map.71 = (bf16[768,384]{1,0:T(8,128)(2,1)S(1)}, bf16[384,384]{1,0:T(8,128)(2,1)S(1)}) custom-call(bf16[16,96,128]{2,1,0:T(8,128)(2,1)S(1)} %all-to-all-done.2.pairs, f32[128,128]{1,0:T(8,128)S(1)} %get-tuple-element.35.bounds, bf16[256,384]{1,0:T(8,128)(2,1)S(1)} %get-tuple-element.45.refs_0_, bf16[256,384]{1,0:T(8,128)(2,1)S(1)} %collective-permute-done.4.refs_1_, ...), custom_call_target="tpu_custom_call" | custom-call | tf_op jit(solution)/shard_map/pallas_call | solution.py:362
  71.3 0.6 collective-permute-start.11
  71.8 1.2 %collective-permute-done.11.spare = bf16[384,384]{1,0:T(8,128)(2,1)S(1)} collective-permute-done((bf16[384,384]{1,0:T(8,128)(2,1)S(1)}, bf16[384,384]{1,0:T(8,128)(2,1)S(1)}, u32[]{:S(2)}, u32[]{:S(2)}) %collective-permute-start.11) | collective-permute-done | bytes 294944 | tf_op jit(solution)/shard_map/ppermute | solution.py:389
  73.1 0.0 collective-permute-done.7.grad_recv
  73.1 0.7 shard_map.72
  73.8 24.4 %all_to_all.27.arrived = bf16[32,24,512]{2,1,0:T(8,128)(2,1)S(1)} all-to-all(bf16[32,24,512]{2,1,0:T(8,128)(2,1)S(1)} %bitcast.9), channel_id=1, replica_groups=mesh['read'=32,'pos'=1] {'read'}, dimensions={0} | all-to-all | bytes 1572864 | tf_op jit(solution)/shard_map/all_to_all | solution.py:351
  98.2 1.3 %shard_map.73 = (bf16[4,32,768]{2,1,0:T(8,128)(2,1)}, f32[24,3072]{1,0:T(8,128)}) custom-call(bf16[32,24,512]{2,1,0:T(8,128)(2,1)S(1)} %all_to_all.27.arrived), custom_call_target="tpu_custom_call" | custom-call | tf_op jit(solution)/shard_map/pallas_call | solution.py:362
Async XLA Ops:
  22.2 1.7 %collective-permute-start = (bf16[256,768]{1,0:T(8,128)(2,1)S(1)}, bf16[256,768]{1,0:T(8,128)(2,1)S(1)}, u32[]{:S(2)}, u32[]{:S(2)}) collective-permute-start(bf16[256,768]{1,0:T(8,128)(2,1)S(1)} %bitcast.10), channel_id=1, source_target_pairs={{0,1},{1,0},{2,3},{3,2},{4,5},{5,4},{6,7},{7,6},{8,9},{9,8},{10,11... | collective-permute-start | bytes 1179656 | tf_op jit(solution)/shard_map/ppermute | solution.py:389
  28.1 16.8 %all-to-all-start.1 = ((bf16[16,96,128]{2,1,0:T(8,128)(2,1)}), bf16[16,96,128]{2,1,0:T(8,128)(2,1)S(1)}, u32[]{:S(2)}, u32[]{:S(2)}) async-start(bf16[16,96,128]{2,1,0:T(8,128)(2,1)} %get-tuple-element.29), calls=%async_computation.1 | async-start | bytes 786432 | tf_op jit(solution)/shard_map/all_to_all | solution.py:351
  31.8 14.1 %collective-permute-start.1 = (bf16[128,768]{1,0:T(8,128)(2,1)S(1)}, bf16[128,768]{1,0:T(8,128)(2,1)S(1)}, u32[]{:S(2)}, u32[]{:S(2)}) collective-permute-start(bf16[128,768]{1,0:T(8,128)(2,1)S(1)} %get-tuple-element.30), channel_id=1, source_target_pairs={{0,2},{1,3},{2,0},{3,1},{4,6},{5,7},{6,4},{7,5},{8,10},{9,11},{10,... | collective-permute-start | bytes 589832 | tf_op jit(solution)/shard_map/ppermute | solution.py:389
  33.7 12.1 %collective-permute-start.2 = (bf16[128,768]{1,0:T(8,128)(2,1)S(1)}, bf16[128,768]{1,0:T(8,128)(2,1)S(1)}, u32[]{:S(2)}, u32[]{:S(2)}) collective-permute-start(bf16[128,768]{1,0:T(8,128)(2,1)S(1)} %get-tuple-element.31), channel_id=1, source_target_pairs={{0,4},{1,5},{2,6},{3,7},{4,0},{5,1},{6,2},{7,3},{8,12},{9,13},{10,... | collective-permute-start | bytes 589832 | tf_op jit(solution)/shard_map/ppermute | solution.py:389
  35.2 12.8 %collective-permute-start.3 = (bf16[128,768]{1,0:T(8,128)(2,1)S(1)}, bf16[128,768]{1,0:T(8,128)(2,1)S(1)}, u32[]{:S(2)}, u32[]{:S(2)}) collective-permute-start(bf16[128,768]{1,0:T(8,128)(2,1)S(1)} %get-tuple-element.32), channel_id=1, source_target_pairs={{0,6},{1,7},{2,4},{3,5},{4,2},{5,3},{6,0},{7,1},{8,14},{9,15},{10,... | collective-permute-start | bytes 589832 | tf_op jit(solution)/shard_map/ppermute | solution.py:389
  48.0 17.3 %all-to-all-start.2 = ((bf16[16,96,128]{2,1,0:T(8,128)(2,1)}), bf16[16,96,128]{2,1,0:T(8,128)(2,1)S(1)}, u32[]{:S(2)}, u32[]{:S(2)}) async-start(bf16[16,96,128]{2,1,0:T(8,128)(2,1)} %shard_map.69), calls=%async_computation.2 | async-start | bytes 786432 | tf_op jit(solution)/shard_map/all_to_all | solution.py:351
  52.8 12.0 %collective-permute-start.4 = (bf16[256,384]{1,0:T(8,128)(2,1)}, bf16[256,384]{1,0:T(8,128)(2,1)S(1)}, u32[]{:S(2)}, u32[]{:S(2)}) collective-permute-start(bf16[256,384]{1,0:T(8,128)(2,1)} %get-tuple-element.39), channel_id=1, source_target_pairs={{0,2},{1,3},{2,0},{3,1},{4,6},{5,7},{6,4},{7,5},{8,10},{9,11},{10,... | collective-permute-start | bytes 589832 | tf_op jit(solution)/shard_map/ppermute | solution.py:389
  54.7 13.5 %collective-permute-start.5 = (bf16[256,384]{1,0:T(8,128)(2,1)}, bf16[256,384]{1,0:T(8,128)(2,1)S(1)}, u32[]{:S(2)}, u32[]{:S(2)}) collective-permute-start(bf16[256,384]{1,0:T(8,128)(2,1)} %get-tuple-element.40), channel_id=1, source_target_pairs={{0,4},{1,5},{2,6},{3,7},{4,0},{5,1},{6,2},{7,3},{8,12},{9,13},{10,... | collective-permute-start | bytes 589832 | tf_op jit(solution)/shard_map/ppermute | solution.py:389
  56.2 12.2 %collective-permute-start.6 = (bf16[256,384]{1,0:T(8,128)(2,1)}, bf16[256,384]{1,0:T(8,128)(2,1)S(1)}, u32[]{:S(2)}, u32[]{:S(2)}) collective-permute-start(bf16[256,384]{1,0:T(8,128)(2,1)} %get-tuple-element.41), channel_id=1, source_target_pairs={{0,6},{1,7},{2,4},{3,5},{4,2},{5,3},{6,0},{7,1},{8,14},{9,15},{10,... | collective-permute-start | bytes 589832 | tf_op jit(solution)/shard_map/ppermute | solution.py:389
  56.3 12.0 %collective-permute-start.8 = (bf16[128,768]{1,0:T(8,128)(2,1)S(1)}, bf16[128,768]{1,0:T(8,128)(2,1)S(1)}, u32[]{:S(2)}, u32[]{:S(2)}) collective-permute-start(bf16[128,768]{1,0:T(8,128)(2,1)S(1)} %collective-permute-done.1.refs_5_), channel_id=1, source_target_pairs={{0,1},{1,0},{2,3},{3,2},{4,5},{5,4},{6,7},{7,6},{8,9},{9,8},{10,11... | collective-permute-start | bytes 589832 | tf_op jit(solution)/shard_map/ppermute | solution.py:389
  56.3 12.0 %collective-permute-start.9 = (bf16[128,768]{1,0:T(8,128)(2,1)S(1)}, bf16[128,768]{1,0:T(8,128)(2,1)}, u32[]{:S(2)}, u32[]{:S(2)}) collective-permute-start(bf16[128,768]{1,0:T(8,128)(2,1)S(1)} %collective-permute-done.2.refs_6_), channel_id=1, source_target_pairs={{0,1},{1,0},{2,3},{3,2},{4,5},{5,4},{6,7},{7,6},{8,9},{9,8},{10,11... | collective-permute-start | bytes 589832 | tf_op jit(solution)/shard_map/ppermute | solution.py:389
  64.8 3.5 %collective-permute-start.10 = (bf16[128,768]{1,0:T(8,128)(2,1)S(1)}, bf16[128,768]{1,0:T(8,128)(2,1)}, u32[]{:S(2)}, u32[]{:S(2)}) collective-permute-start(bf16[128,768]{1,0:T(8,128)(2,1)S(1)} %collective-permute-done.3.refs_7_), channel_id=1, source_target_pairs={{0,1},{1,0},{2,3},{3,2},{4,5},{5,4},{6,7},{7,6},{8,9},{9,8},{10,11... | collective-permute-start | bytes 589832 | tf_op jit(solution)/shard_map/ppermute | solution.py:389
  68.3 4.7 %collective-permute-start.7 = (f32[128,768]{1,0:T(8,128)S(1)}, f32[128,768]{1,0:T(8,128)S(1)}, u32[]{:S(2)}, u32[]{:S(2)}) collective-permute-start(f32[128,768]{1,0:T(8,128)S(1)} %get-tuple-element.42), channel_id=1, source_target_pairs={{0,1},{1,0},{2,3},{3,2},{4,5},{5,4},{6,7},{7,6},{8,9},{9,8},{10,11... | collective-permute-start | bytes 1179656 | tf_op jit(solution)/shard_map/ppermute | solution.py:389
  71.3 1.8 %collective-permute-start.11 = (bf16[384,384]{1,0:T(8,128)(2,1)S(1)}, bf16[384,384]{1,0:T(8,128)(2,1)S(1)}, u32[]{:S(2)}, u32[]{:S(2)}) collective-permute-start(bf16[384,384]{1,0:T(8,128)(2,1)S(1)} %get-tuple-element.55), channel_id=1, source_target_pairs={{0,1},{1,0},{2,3},{3,2},{4,5},{5,4},{6,7},{7,6},{8,9},{9,8},{10,11... | collective-permute-start | bytes 884744 | tf_op jit(solution)/shard_map/ppermute | solution.py:389

commit v6 on v5

v6 whole, which is shorter than its diff:
```python
import functools
import math

import jax
import jax.numpy as jnp
from jax import lax
from jax.experimental import pallas as pl
from jax.experimental.pallas import tpu as pltpu
from jax.sharding import PartitionSpec as P

HEADS = 12
HEAD_DIM = 64
CORES = 2
KINDS = 4
LANES = 128
MIB = 1024 * 1024

BF16 = jnp.bfloat16
F32 = jnp.float32


def dot(left, right, contract=(1, 0)):
    return lax.dot_general(
        left, right, (((contract[0],), (contract[1],)), ((), ())), preferred_element_type=F32
    )


def upright(lanes):
    size = lanes.shape[1]
    rows = lax.broadcasted_iota(jnp.int32, (size, size), 0)
    cols = lax.broadcasted_iota(jnp.int32, (size, size), 1)
    spread = jnp.broadcast_to(lanes.astype(F32), (size, size))
    return jnp.sum(jnp.where(rows == cols, spread, 0.0), -1, keepdims=True)


def row_mask(start, end, column):
    column = column.astype(F32)
    return ((start <= column) & (column < end)).astype(F32)


def first_heads(rows, lanes):
    at = lax.broadcasted_iota(jnp.int32, (rows, lanes), 1)
    return lax.rem(at, LANES) < HEAD_DIM


def slab(array, at):
    reads = array.shape[0] // 2
    lanes = slice(at * LANES, (at + 1) * LANES)
    return jnp.concatenate([array[:reads, lanes], array[reads:, lanes]], axis=1)


def indicator(rows, cols, place):
    at = lax.broadcasted_iota(jnp.int32, (rows, cols), 0)
    spot = lax.broadcasted_iota(jnp.int32, (rows, cols), 1)
    return place(at, spot).astype(F32).astype(BF16)


def position():
    me = lax.axis_index("read")
    core = jnp.bitwise_and(me, CORES - 1)
    kind = jnp.bitwise_and(jnp.right_shift(me, 1), KINDS - 1)
    return me, core, kind


def head_lanes(core, half):
    return pl.ds(pl.multiple_of(core * half, LANES), half)


def part_rows(arrived, rows, cells):
    def pick(shift):
        return indicator(
            cells,
            2 * cells,
            lambda at, spot: spot == lax.div(at, rows) * (2 * rows) + lax.rem(at, rows) + shift,
        )

    both = jnp.concatenate(arrived, axis=1)
    width = arrived[0].shape[1]
    source, upstream = dot(pick(0), both), dot(pick(rows), both).astype(BF16)

    def stack(array):
        return jnp.concatenate(
            [array[:, at * width : (at + 1) * width] for at in range(len(arrived))], axis=0
        )

    return stack(source), stack(upstream)


def normalise(source):
    inverse = lax.rsqrt(jnp.mean(source * source, -1, keepdims=True) + 1e-05)
    return source * inverse, inverse


def project_kernel(
    own, other, weights, start, end, proj, tied, normed_own, bounds, heads_in, heads_out,
    start_here, end_here, sems, *, rows, col_dev
):
    cells = own.shape[0] // 2
    half = own.shape[1] // CORES
    me, core, _ = position()
    first_col = lax.axis_index("pos") * col_dev
    copies = [
        pltpu.make_async_copy(start, start_here, sems.at[0]),
        pltpu.make_async_copy(end, end_here, sems.at[1]),
    ]
    for at in range(3):
        copies.append(
            pltpu.make_async_copy(
                weights.at[at, :, head_lanes(core, half)], heads_in.at[at], sems.at[2 + at]
            )
        )
    copies.append(
        pltpu.make_async_copy(weights.at[3, head_lanes(core, half), :], heads_out, sems.at[5])
    )
    for copy in copies:
        copy.start()

    source, upstream = part_rows([own[...], other[...]], rows, cells)
    normed32, inverse = normalise(source)
    normed = normed32.astype(BF16)
    normed_own[...] = normed32[:cells]
    copies[0].wait()
    copies[1].wait()
    first, last = upright(start_here[...]), upright(end_here[...])
    lane = lax.broadcasted_iota(jnp.int32, bounds.shape, 1)
    bounds[...] = jnp.where(lane == 0, first, jnp.where(lane == 1, last, inverse[:cells]))
    covered = jnp.concatenate(
        [
            row_mask(first, last, first_col + me),
            row_mask(first, last, first_col + jnp.bitwise_xor(me, 1)),
        ],
        axis=0,
    )
    copies[2].wait()
    query = (dot(normed, heads_in[0]) * covered).astype(BF16)
    copies[3].wait()
    keys = (dot(normed, heads_in[1]) * covered).astype(BF16)
    copies[4].wait()
    values = (dot(normed, heads_in[2]) * covered).astype(BF16)
    copies[5].wait()
    back_out = dot(upstream, heads_out[...], (1, 1)).astype(BF16)
    proj[0] = keys
    proj[1] = query
    proj[2] = back_out

    low = first_heads(cells, 2 * LANES)
    chips = tied.shape[0]
    part = cells // chips

    def both_heads(array):
        return jnp.concatenate([jnp.where(low, array, 0), jnp.where(low, 0, array)], axis=0)

    for pair in range(half // LANES):
        logits = dot(both_heads(slab(query, pair)), slab(keys, pair), (1, 1))
        slopes = dot(both_heads(slab(back_out, pair)), slab(values, pair), (1, 1))
        for odd in range(2):
            here = slice(odd * cells, (odd + 1) * cells)
            both = jnp.concatenate(
                [
                    logits[here].reshape(chips, part, cells),
                    slopes[here].reshape(chips, part, cells),
                ],
                axis=1,
            )
            spot = (2 * pair + odd) * 2 * part
            tied[:, spot : spot + 2 * part, :] = both.astype(BF16)


def operand_kernel(weights, bounds, *refs, rows, col_dev, slots):
    *raw, left, ops, heads, heads_back, sem = refs
    width = raw[0].shape[1]
    half = width // CORES
    cells = bounds.shape[0]
    per_block = len(raw) // (2 * len(slots))
    me, core, kind = position()
    first_col = lax.axis_index("pos") * col_dev
    for at, source_of in ((0, 1), (1, 0), (3, 2)):

        @pl.when(kind == at)
        def _():
            copy = pltpu.make_async_copy(
                weights.at[source_of, :, head_lanes(core, half)], heads, sem
            )
            copy.start()
            copy.wait()

    @pl.when(kind == 2)
    def _():
        copy = pltpu.make_async_copy(
            weights.at[3, head_lanes(core, half), :], heads_back, sem
        )
        copy.start()
        copy.wait()

    blocks = []
    for at in range(0, len(raw), per_block):
        pieces = [ref[...] for ref in raw[at : at + per_block]]
        blocks.append(pieces[0] if per_block == 1 else jnp.concatenate(pieces, axis=0))
    source, upstream = part_rows(blocks, rows, cells)
    normed = normalise(source)[0].astype(BF16)
    first, last = bounds[:, 0:1], bounds[:, 1:2]
    covered = jnp.concatenate(
        [
            row_mask(first, last, first_col + jnp.bitwise_xor(me, 2 * slot + side))
            for slot in slots
            for side in range(2)
        ],
        axis=0,
    )

    @pl.when(kind == 2)
    def _():
        ops[...] = dot(upstream, heads_back[...], (1, 1)).astype(BF16)

    @pl.when(kind != 2)
    def _():
        ops[...] = (dot(normed, heads[...]) * covered).astype(BF16)

    @pl.when(kind == KINDS - 1)
    def _():
        left[...] = upstream

    @pl.when(kind < KINDS - 1)
    def _():
        left[...] = normed


def soften_kernel(parts, copies, *, scale, part):
    total = jnp.sum(parts[...].astype(F32), axis=0)
    blocks = total.reshape(-1, 2 * part, total.shape[-1])
    logits = blocks[:, :part] * scale
    slopes = blocks[:, part:]
    expon = jnp.exp(logits)
    probs = expon / jnp.sum(expon, -1, keepdims=True)
    mixed = scale * probs * (slopes - jnp.sum(probs * slopes, -1, keepdims=True))
    result = jnp.concatenate([probs, mixed], axis=1).reshape(total.shape).astype(BF16)
    for chip in range(copies.shape[0]):
        copies[chip] = result


def head_maps(pairs, head, cells):
    part = cells // pairs.shape[0]
    both = pairs[:, head * 2 * part : (head + 1) * 2 * part, :].astype(F32)
    return both[:, :part].reshape(cells, cells), both[:, part:].reshape(cells, cells)


def gradient_kernel(
    pairs, proj, bounds, ops_near, ops_far, weights, left_near, left_far, own, other, product, spare,
    grads, right, heads_in, left, sems, *, col_dev
):
    cells = proj.shape[1] // 2
    half = proj.shape[2]
    me, core, kind = position()
    first_col = lax.axis_index("pos") * col_dev
    copies = [
        pltpu.make_async_copy(
            weights.at[at, :, head_lanes(core, half)], heads_in.at[at], sems.at[at]
        )
        for at in range(3)
    ]
    near = left_near.shape[0]
    copies.append(pltpu.make_async_copy(left_near, left.at[pl.ds(0, near)], sems.at[3]))
    copies.append(
        pltpu.make_async_copy(left_far, left.at[pl.ds(near, left_far.shape[0])], sems.at[4])
    )
    for at in (3, 4, 0, 1, 2):
        copies[at].start()
    first, last = bounds[:, 0:1], bounds[:, 1:2]
    masks = []
    for at in range(2 * KINDS):
        mask = row_mask(first, last, first_col + jnp.bitwise_xor(me, at))
        masks.append(jnp.broadcast_to(mask, (cells, LANES)))
    covered = jnp.concatenate(masks[:2], axis=1)
    plane_covered = jnp.where(kind == KINDS - 1, 1.0, jnp.concatenate(masks, axis=1))
    low = first_heads(cells, 2 * LANES)
    plane_low = first_heads(cells, 2 * KINDS * LANES)
    use_probs = kind >= 2
    use_flip = (kind == 1) | (kind == 2)

    for pair in range(half // LANES):
        lanes = slice(pair * LANES, (pair + 1) * LANES)

        def store(at, maps, operand):
            result = dot(jnp.concatenate(maps, axis=0), operand)
            result = (jnp.where(low, result[:cells], result[cells:]) * covered).astype(BF16)
            grads[at, :cells, lanes] = result[:, :LANES]
            grads[at, cells:, lanes] = result[:, LANES:]

        maps = [head_maps(pairs, 2 * pair + odd, cells) for odd in range(2)]
        flips = [(a.T, b.T) for a, b in maps]

        store(0, [b.astype(BF16) for _, b in maps], slab(proj[0], pair))
        store(1, [b.astype(BF16) for _, b in flips], slab(proj[1], pair))
        store(2, [a.astype(BF16) for a, _ in flips], slab(proj[2], pair))

        chosen = []
        for (a, b), (a_flip, b_flip) in zip(maps, flips):
            flat = jnp.where(use_probs, a, b)
            flip = jnp.where(use_probs, a_flip, b_flip)
            chosen.append(jnp.where(use_flip, flip, flat).astype(BF16))
        cat = jnp.concatenate(
            [
                ops[at : at + cells, lanes]
                for ops in (ops_near, ops_far)
                for at in range(0, ops.shape[0], cells)
            ],
            axis=1,
        )
        result = dot(jnp.concatenate(chosen, axis=0), cat)
        result = jnp.where(plane_low, result[:cells], result[cells:]) * plane_covered
        result = result.astype(BF16)
        for at in range(2 * KINDS):
            right[at * cells : (at + 1) * cells, lanes] = result[
                :, at * LANES : (at + 1) * LANES
            ]

    copies[3].wait()
    copies[4].wait()

    @pl.when(kind < KINDS - 1)
    def _():
        product[...] = dot(left[...], right[...], (0, 0)).astype(BF16)

    @pl.when(kind == KINDS - 1)
    def _():
        rows = dot(right[...], left[...], (0, 0)).astype(BF16)

        @pl.when(core == 0)
        def _():
            product[:half] = rows[:, :half]
            spare[...] = rows[:, half:]

        @pl.when(core == 1)
        def _():
            product[:half] = rows[:, half:]
            spare[...] = rows[:, :half]

    total = None
    for at in range(3):
        copies[at].wait()
        term = dot(grads[at], heads_in[at], (1, 1))
        total = term if total is None else total + term
    own[...] = total[:cells]
    other[...] = total[cells:]


def pack_kernel(grad_own, grad_recv, normed, bounds, product, spare, payload, *, rows):
    cells, width = normed.shape
    tiles = width // LANES
    half = product.shape[1]
    group = rows * tiles
    grad_norm = grad_own[...] + grad_recv[...]
    mean = jnp.mean(grad_norm * normed[...], -1, keepdims=True)
    result = (grad_norm - normed[...] * mean) * bounds[:, 2:3]
    result = result.astype(BF16)
    stack = jnp.concatenate(
        [result[:, t * LANES : (t + 1) * LANES] for t in range(tiles)], axis=0
    )

    def place(at, spot):
        tile, cell = lax.div(spot, cells), lax.rem(spot, cells)
        return at == lax.div(cell, rows) * group + tile * rows + lax.rem(cell, rows)

    _, core, kind = position()

    @pl.when((kind < KINDS - 1) | (core == 0))
    def _():
        payload[:half, :half] = product[:half]

    @pl.when(kind < KINDS - 1)
    def _():
        payload[half:, :half] = product[half:]

    @pl.when((kind == KINDS - 1) & (core == 0))
    def _():
        payload[half:, :half] = spare[...]

    @pl.when((kind == KINDS - 1) & (core == 1))
    def _():
        payload[:half, :half] = spare[...]
        payload[half:, :half] = product[:half]

    payload[:, half:] = dot(indicator(width, tiles * cells, place), stack).astype(BF16)


def finish_kernel(arrived, grad_input, sums):
    count, chunk, wide = arrived.shape
    rows, cols, width = grad_input.shape
    half = wide - LANES
    group = KINDS * CORES
    for kind in range(KINDS):
        for core in range(CORES):
            total = None
            for base in range(0, count, group):
                term = arrived[base + kind * CORES + core, :, :half].astype(F32)
                total = term if total is None else total + term
            spot = kind * width + core * half
            sums[:, spot : spot + half] = total
    flat = arrived[:, :, half:].astype(F32).reshape(count * chunk, LANES).astype(BF16)
    cells = rows * cols

    def place(at, spot):
        tile, cell = lax.div(at, cells), lax.rem(at, cells)
        return spot == lax.rem(cell, cols) * chunk + tile * rows + lax.div(cell, cols)

    tiles = width // LANES
    moved = dot(indicator(tiles * cells, count * chunk, place), flat).astype(BF16)
    for tile in range(tiles):
        for row in range(rows):
            spot = tile * cells + row * cols
            grad_input[row, :, tile * LANES : (tile + 1) * LANES] = moved[spot : spot + cols]


def exchange(array, groups):
    return lax.all_to_all(
        array, "read", split_axis=0, concat_axis=0, tiled=True, axis_index_groups=groups
    )


def call(kernel, args, outs, mib, far=(), scratch=(), cost=None):
    args = [
        pltpu.with_memory_space_constraint(arg, pltpu.HBM) if at in far else arg
        for at, arg in enumerate(args)
    ]
    near, away = (pl.BlockSpec(memory_space=space) for space in (pltpu.VMEM, pltpu.HBM))
    return pl.pallas_call(
        kernel,
        in_specs=[away if at in far else near for at in range(len(args))],
        out_specs=jax.tree.map(lambda _: near, outs),
        out_shape=outs,
        scratch_shapes=scratch,
        cost_estimate=cost,
        compiler_params=pltpu.CompilerParams(vmem_limit_bytes=mib * MIB),
    )(*args)


def shards(features, grad_out, weights, read_start, read_end):
    rows, col_dev, width = features.shape
    count = lax.axis_size("read")
    pos_count = lax.axis_size("pos")
    scale = 1.0 / math.sqrt(HEAD_DIM * col_dev * pos_count)
    reads = rows * count
    chips = count // CORES
    half = width // CORES
    part = reads // chips
    tied_rows = (HEADS // CORES) * 2 * part
    chunk = width // count
    start = read_start.reshape(1, reads)
    end = read_end.reshape(1, reads)

    same_core = [list(range(c, count, CORES)) for c in range(CORES)]

    def swap(array, bits):
        return lax.ppermute(array, "read", [(i, i ^ bits) for i in range(count)])

    shape = jax.ShapeDtypeStruct
    send = jnp.stack([features, grad_out]).transpose(2, 0, 1, 3).reshape(-1, width)
    own = exchange(send, None)
    other = swap(own, 1)
    proj, tied, normed, bounds = call(
        functools.partial(project_kernel, rows=rows, col_dev=col_dev),
        (own, other, weights, start, end),
        (
            shape((KINDS - 1, 2 * reads, half), BF16),
            shape((chips, tied_rows, reads), BF16),
            shape((reads, width), F32),
            shape((reads, LANES), F32),
        ),
        20,
        (2, 3, 4),
        [
            pltpu.VMEM((3, width, half), BF16),
            pltpu.VMEM((half, width), BF16),
            pltpu.VMEM((1, reads), jnp.int32),
            pltpu.VMEM((1, reads), jnp.int32),
            pltpu.SemaphoreType.DMA((6,)),
        ],
    )

    parts = exchange(tied, same_core)
    raw = {1: swap(own, CORES), 2: swap(own, 2 * CORES)}
    if pos_count > 1:
        parts = lax.psum(jnp.sum(parts.astype(F32), 0, keepdims=True), "pos")
    copies = call(
        functools.partial(soften_kernel, scale=scale, part=part),
        (parts,),
        shape((chips, tied_rows, reads), BF16),
        8,
    )
    pairs = exchange(copies, same_core)
    diagonal = [swap(raw[1][:reads], 2 * CORES), swap(raw[2][reads:], CORES)]

    def operands(slots, blocks):
        count_here = 2 * reads * len(slots)
        return call(
            functools.partial(operand_kernel, rows=rows, col_dev=col_dev, slots=slots),
            (weights, bounds, *blocks),
            (shape((count_here, width), BF16), shape((count_here, half), BF16)),
            24,
            (0,),
            [
                pltpu.VMEM((width, half), BF16),
                pltpu.VMEM((half, width), BF16),
                pltpu.SemaphoreType.DMA,
            ],
            pl.CostEstimate(flops=4 * 10**9, bytes_accessed=8 * MIB, transcendentals=0),
        )

    left_near, ops_near = operands(
        (0, 1, 2), (own, other, raw[1], swap(raw[1], 1), raw[2], swap(raw[2], 1))
    )
    left_far, ops_far = operands((3,), (*diagonal, *[swap(a, 1) for a in diagonal]))

    grad_own, grad_other, product, spare = call(
        functools.partial(gradient_kernel, col_dev=col_dev),
        (pairs, proj, bounds, ops_near, ops_far, weights, left_near, left_far),
        (
            shape((reads, width), F32),
            shape((reads, width), F32),
            shape((width, half), BF16),
            shape((half, half), BF16),
        ),
        24,
        (5, 6, 7),
        [
            pltpu.VMEM((3, 2 * reads, half), BF16),
            pltpu.VMEM((2 * KINDS * reads, half), BF16),
            pltpu.VMEM((3, width, half), BF16),
            pltpu.VMEM((2 * KINDS * reads, width), BF16),
            pltpu.SemaphoreType.DMA((5,)),
        ],
    )
    grad_recv = swap(grad_other, 1)
    spare = swap(spare, 1)
    payload = call(
        functools.partial(pack_kernel, rows=rows),
        (grad_own, grad_recv, normed, bounds, product, spare),
        shape((width, half + LANES), BF16),
        8,
    )
    arrived = exchange(payload.reshape(count, chunk, half + LANES), None)
    grad_input, sums = call(
        finish_kernel,
        (arrived,),
        (shape((rows, col_dev, width), BF16), shape((chunk, KINDS * width), F32)),
        8,
    )
    weight_grads = lax.psum_scatter(sums, "pos", scatter_dimension=0, tiled=True)
    return (grad_input, weight_grads)


def solution(mesh):
    in_specs = (P("read", "pos", None), P("read", "pos", None), P(), P(), P())
    out_specs = (P("read", "pos", None), P(("read", "pos"), None))
    return jax.shard_map(shards, mesh=mesh, in_specs=in_specs, out_specs=out_specs, check_vma=False)
```

time: 99.9 us -> 95.3 us (0.954)
  waiting for transfers between devices: 23.1 us -> 15.2 us
  Pallas kernels: 13 us -> 18.3 us
  starting transfers between devices: 16.7 us -> 13.1 us
  local copies, waits for them, and re-layouts: 0.22 us -> 3.02 us
  blocking collectives: 44.7 us -> 43.4 us
    all_to_all x2, waiting for transfers between devices: 10 us -> 3.18 us  [exchange(): lax.all_to_all(array, 'read', split_axis=0, concat_axis=0, tiled=True, ax...]
    pallas_call x6 -> x7, Pallas kernels: 13 us -> 18.3 us  [call(): pl.pallas_call(kernel, in_specs=[away if at in far else near for at in ra...]
    unnamed x0 -> x8, local copies, waits for them, and re-layouts: none -> 2.77 us
    ppermute x12 -> x11, starting transfers between devices: 8.19 us -> 5.59 us  [swap(): return lax.ppermute(array, 'read', [(i, i ^ bits) for i in range(count)])]
    all_to_all x2, blocking collectives: 44.7 us -> 43.4 us  [exchange(): lax.all_to_all(array, 'read', split_axis=0, concat_axis=0, tiled=True, ax...]
    ppermute x12 -> x11, waiting for transfers between devices: 13.1 us -> 12 us  [swap(): return lax.ppermute(array, 'read', [(i, i ^ bits) for i in range(count)])]
  transfers between devices with their start and end apart: 14 -> 13, of which waited for: 7 -> 6; matrix products, arithmetic and copies ran while one was open for 0% -> 0% of each run, Pallas kernels for 7% -> 13%
where the time goes in v6:
time: 95.3 us; the launch traced here: 94.8 us
  blocking collectives  43.4 us (46%)
  Pallas kernels  18.3 us (19%)
  waiting for transfers between devices  15.2 us (16%)
  starting transfers between devices  13.1 us (14%)
  local copies, waits for them, and re-layouts  3.02 us (3%)
  other arithmetic  1.06 us (1%)
    all_to_all x2, blocking collectives, exchange(): lax.all_to_all(array, 'read', split_axis=0, concat_axis=0, tiled=True, ax...  43.4 us
    pallas_call x7, Pallas kernels, call(): pl.pallas_call(kernel, in_specs=[away if at in far else near for at in ra...  18.3 us
    ppermute x11, waiting for transfers between devices, swap(): return lax.ppermute(array, 'read', [(i, i ^ bits) for i in range(count)])  12 us
    all_to_all x2, starting transfers between devices, exchange(): lax.all_to_all(array, 'read', split_axis=0, concat_axis=0, tiled=True, ax...  7.5 us
    ppermute x11, starting transfers between devices, swap(): return lax.ppermute(array, 'read', [(i, i ^ bits) for i in range(count)])  5.59 us
    all_to_all x2, waiting for transfers between devices, exchange(): lax.all_to_all(array, 'read', split_axis=0, concat_axis=0, tiled=True, ax...  3.18 us
    unnamed x8, local copies, waits for them, and re-layouts  2.77 us
  transfers between devices with their start and end apart: 13, of which 6 were waited for; matrix products, arithmetic and copies ran while one was open for 0% of the time, Pallas kernels for 13%

profile of v6, /device:TPU:0, one launch (start us, length us, event | category | flops | bytes accessed | tf_op | source)
XLA Modules:
  0.0 94.8 jit_solution(11245345828056504632)
XLA Ops:
  0.6 1.1 %pad_maximum_fusion = bf16[2,4,32,768]{3,2,1,0:T(8,128)(2,1)S(1)} fusion(bf16[1,4,32,768]{3,2,1,0:T(8,128)(2,1)} %bitcast.16, bf16[1,4,32,768]{3,2,1,0:T(8,128)(2,1)} %bitcast.17), kind=kLoop, calls=%fused_computation | loop fusion | flops 196608 | bytes 786432 | tf_op jit(solution)/shard_map/stack | solution.py:457
  1.7 0.2 copy.7
  1.9 20.3 %all_to_all.26 = bf16[32,8,768]{2,1,0:T(8,128)(2,1)S(1)} all-to-all(bf16[32,8,768]{2,1,0:T(8,128)(2,1)S(1)} %copy.7), channel_id=1, replica_groups=mesh['read'=32,'pos'=1] {'read'}, dimensions={0} | all-to-all | bytes 786432 | tf_op jit(solution)/shard_map/all_to_all | solution.py:415
  22.2 0.0 collective-permute-start
  22.2 1.0 %collective-permute-start.1 = (bf16[256,768]{1,0:T(8,128)(2,1)S(1)}, bf16[256,768]{1,0:T(8,128)(2,1)S(1)}, u32[]{:S(2)}, u32[]{:S(2)}) collective-permute-start(bf16[256,768]{1,0:T(8,128)(2,1)S(1)} %bitcast.11), channel_id=1, source_target_pairs={{0,2},{1,3},{2,0},{3,1},{4,6},{5,7},{6,4},{7,5},{8,10},{9,11},{10,... | collective-permute-start | bytes 1179656 | tf_op jit(solution)/shard_map/ppermute | solution.py:454
  23.2 1.0 %collective-permute-start.3 = (bf16[256,768]{1,0:T(8,128)(2,1)S(1)}, bf16[256,768]{1,0:T(8,128)(2,1)S(1)}, u32[]{:S(2)}, u32[]{:S(2)}) collective-permute-start(bf16[256,768]{1,0:T(8,128)(2,1)S(1)} %bitcast.12), channel_id=1, source_target_pairs={{0,4},{1,5},{2,6},{3,7},{4,0},{5,1},{6,2},{7,3},{8,12},{9,13},{10,... | collective-permute-start | bytes 1179656 | tf_op jit(solution)/shard_map/ppermute | solution.py:454
  24.2 0.0 collective-permute-done.other.refs_1_
  24.2 4.0 %shard_map.68 = (bf16[3,256,384]{2,1,0:T(8,128)(2,1)S(1)}, bf16[16,96,128]{2,1,0:T(8,128)(2,1)}, f32[128,768]{1,0:T(8,128)S(1)}, f32[128,128]{1,0:T(8,128)S(1)}) custom-call(bf16[256,768]{1,0:T(8,128)(2,1)S(1)} %bitcast.13, bf16[256,768]{1,0:T(8,128)(2,1)S(1)} %collective-permute-done.other.refs_1_, bf16[4,768,768]{2,1,0:T(8,128)(2,1)} %weights.7, ...), custom_call_target="tpu_custom_call" | custom-call | tf_op jit(solution)/shard_map/pallas_call | solution.py:426
  28.1 3.6 %all-to-all-start.1 = ((bf16[16,96,128]{2,1,0:T(8,128)(2,1)}), bf16[16,96,128]{2,1,0:T(8,128)(2,1)S(1)}, u32[]{:S(2)}, u32[]{:S(2)}) async-start(bf16[16,96,128]{2,1,0:T(8,128)(2,1)} %get-tuple-element.14), calls=%async_computation.1 | async-start | bytes 786432 | tf_op jit(solution)/shard_map/all_to_all | solution.py:415
  31.7 2.0 %collective-permute-done.1.refs_2_ = bf16[256,768]{1,0:T(8,128)(2,1)S(1)} collective-permute-done((bf16[256,768]{1,0:T(8,128)(2,1)S(1)}, bf16[256,768]{1,0:T(8,128)(2,1)S(1)}, u32[]{:S(2)}, u32[]{:S(2)}) %collective-permute-start.1) | collective-permute-done | bytes 393248 | tf_op jit(solution)/shard_map/ppermute | solution.py:454
  33.7 0.0 collective-permute-start.2
  33.7 0.2 collective-permute-done.3.refs_4_
  33.9 0.0 copy-start.2
  33.9 0.3 collective-permute-start.4
  34.3 1.5 %collective-permute-start.5 = (bf16[128,768]{1,0:T(8,128)(2,1)S(1)}, bf16[128,768]{1,0:T(8,128)(2,1)S(1)}, u32[]{:S(2)}, u32[]{:S(2)}) collective-permute-start(bf16[128,768]{1,0:T(8,128)(2,1)S(1)} %slice.8), channel_id=1, source_target_pairs={{0,4},{1,5},{2,6},{3,7},{4,0},{5,1},{6,2},{7,3},{8,12},{9,13},{10,... | collective-permute-start | bytes 589832 | tf_op jit(solution)/shard_map/ppermute | solution.py:454
  35.8 1.2 %collective-permute-start.6 = (bf16[128,768]{1,0:T(8,128)(2,1)S(1)}, bf16[128,768]{1,0:T(8,128)(2,1)}, u32[]{:S(2)}, u32[]{:S(2)}) collective-permute-start(bf16[128,768]{1,0:T(8,128)(2,1)S(1)} %slice.9), channel_id=1, source_target_pairs={{0,2},{1,3},{2,0},{3,1},{4,6},{5,7},{6,4},{7,5},{8,10},{9,11},{10,... | collective-permute-start | bytes 589832 | tf_op jit(solution)/shard_map/ppermute | solution.py:454
  37.0 6.0 %collective-permute-done.5.refs_0_ = bf16[128,768]{1,0:T(8,128)(2,1)S(1)} collective-permute-done((bf16[128,768]{1,0:T(8,128)(2,1)S(1)}, bf16[128,768]{1,0:T(8,128)(2,1)S(1)}, u32[]{:S(2)}, u32[]{:S(2)}) %collective-permute-start.5) | collective-permute-done | bytes 196640 | tf_op jit(solution)/shard_map/ppermute | solution.py:454
  43.0 0.0 collective-permute-start.7
  43.0 2.1 %collective-permute-done.6.refs_1_ = bf16[128,768]{1,0:T(8,128)(2,1)} collective-permute-done((bf16[128,768]{1,0:T(8,128)(2,1)S(1)}, bf16[128,768]{1,0:T(8,128)(2,1)}, u32[]{:S(2)}, u32[]{:S(2)}) %collective-permute-start.6) | collective-permute-done | bytes 196640 | tf_op jit(solution)/shard_map/ppermute | solution.py:454
  45.1 0.0 collective-permute-start.8
  45.1 0.0 all-to-all-done.1.parts
  45.1 1.0 %shard_map.69 = bf16[16,96,128]{2,1,0:T(8,128)(2,1)} custom-call(bf16[16,96,128]{2,1,0:T(8,128)(2,1)S(1)} %all-to-all-done.1.parts), custom_call_target="tpu_custom_call" | custom-call | tf_op jit(solution)/shard_map/pallas_call | solution.py:426
  46.1 3.9 %all-to-all-start.2 = ((bf16[16,96,128]{2,1,0:T(8,128)(2,1)}), bf16[16,96,128]{2,1,0:T(8,128)(2,1)S(1)}, u32[]{:S(2)}, u32[]{:S(2)}) async-start(bf16[16,96,128]{2,1,0:T(8,128)(2,1)} %shard_map.69), calls=%async_computation.2 | async-start | bytes 786432 | tf_op jit(solution)/shard_map/all_to_all | solution.py:415
  50.0 0.0 collective-permute-done.2.refs_3_
  50.0 0.0 collective-permute-done.4.refs_5_
  50.1 0.0 copy-done.2
  50.1 0.0 copy-start.3
  50.1 1.0 %copy-done.3 = bf16[256,768]{1,0:T(8,128)(2,1)S(1)} copy-done((bf16[256,768]{1,0:T(8,128)(2,1)S(1)}, bf16[256,768]{1,0:T(8,128)(2,1)}, u32[]{:S(2)}) %copy-start.3) | copy-done | bytes 393240
  51.1 4.1 %shard_map.70 = (bf16[768,768]{1,0:T(8,128)(2,1)S(1)}, bf16[768,384]{1,0:T(8,128)(2,1)S(1)}) custom-call(bf16[4,768,768]{2,1,0:T(8,128)(2,1)} %weights.7, f32[128,128]{1,0:T(8,128)S(1)} %get-tuple-element.16.bounds, bf16[256,768]{1,0:T(8,128)(2,1)S(1)} %bitcast.14, bf16[256,768]{1,0:T(8,128)(2,1)S(1)} %collective-permute-done.other.refs_1_, ...), custom_call_target="tpu_custom_call" | custom-call | flops 4000000000 | bytes 8388608 | tf_op jit(solution)/shard_map/pallas_call | solution.py:426
  55.2 0.0 copy-start
  55.2 1.0 %copy-done = bf16[768,768]{1,0:T(8,128)(2,1)} copy-done((bf16[768,768]{1,0:T(8,128)(2,1)}, bf16[768,768]{1,0:T(8,128)(2,1)S(1)}, u32[]{:S(2)}) %copy-start) | copy-done | bytes 1179672
  56.2 0.0 collective-permute-done.7.refs_2_
  56.2 0.0 collective-permute-done.8.refs_3_
  56.2 3.0 %shard_map.71 = (bf16[256,768]{1,0:T(8,128)(2,1)S(1)}, bf16[256,384]{1,0:T(8,128)(2,1)S(1)}) custom-call(bf16[4,768,768]{2,1,0:T(8,128)(2,1)} %weights.7, f32[128,128]{1,0:T(8,128)S(1)} %get-tuple-element.16.bounds, bf16[128,768]{1,0:T(8,128)(2,1)S(1)} %collective-permute-done.5.refs_0_, bf16[128,768]{1,0:T(8,128)(2,1)} %collective-permute-done.6.refs_1_, ...), custom_call_target="tpu_custom_call" | custom-call | flops 4000000000 | bytes 8388608 | tf_op jit(solution)/shard_map/pallas_call | solution.py:426
  59.3 0.0 copy-start.1
  59.3 0.7 copy-done.1
  60.0 3.2 %all-to-all-done.2.pairs = bf16[16,96,128]{2,1,0:T(8,128)(2,1)S(1)} async-done(((bf16[16,96,128]{2,1,0:T(8,128)(2,1)}), bf16[16,96,128]{2,1,0:T(8,128)(2,1)S(1)}, u32[]{:S(2)}, u32[]{:S(2)}) %all-to-all-start.2) | async-done | bytes 393248 | tf_op jit(solution)/shard_map/all_to_all | solution.py:415
  63.2 4.2 %shard_map.72 = (f32[128,768]{1,0:T(8,128)S(1)}, f32[128,768]{1,0:T(8,128)S(1)}, bf16[768,384]{1,0:T(8,128)(2,1)S(1)}, bf16[384,384]{1,0:T(8,128)(2,1)S(1)}) custom-call(bf16[16,96,128]{2,1,0:T(8,128)(2,1)S(1)} %all-to-all-done.2.pairs, bf16[3,256,384]{2,1,0:T(8,128)(2,1)S(1)} %get-tuple-element.15.proj, f32[128,128]{1,0:T(8,128)S(1)} %get-tuple-element.16.bounds, ...), custom_call_target="tpu_custom_call" | custom-call | tf_op jit(solution)/shard_map/pallas_call | solution.py:426
  67.5 0.1 collective-permute-start.9
  67.5 0.5 collective-permute-start.10
  68.0 1.6 %collective-permute-done.10.spare = bf16[384,384]{1,0:T(8,128)(2,1)S(1)} collective-permute-done((bf16[384,384]{1,0:T(8,128)(2,1)S(1)}, bf16[384,384]{1,0:T(8,128)(2,1)S(1)}, u32[]{:S(2)}, u32[]{:S(2)}) %collective-permute-start.10) | collective-permute-done | bytes 294944 | tf_op jit(solution)/shard_map/ppermute | solution.py:454
  69.7 0.0 collective-permute-done.9.grad_recv
  69.7 0.7 shard_map.73
  70.4 23.1 %all_to_all.27.arrived = bf16[32,24,512]{2,1,0:T(8,128)(2,1)S(1)} all-to-all(bf16[32,24,512]{2,1,0:T(8,128)(2,1)S(1)} %bitcast.9), channel_id=1, replica_groups=mesh['read'=32,'pos'=1] {'read'}, dimensions={0} | all-to-all | bytes 1572864 | tf_op jit(solution)/shard_map/all_to_all | solution.py:415
  93.5 1.3 %shard_map.74 = (bf16[4,32,768]{2,1,0:T(8,128)(2,1)}, f32[24,3072]{1,0:T(8,128)}) custom-call(bf16[32,24,512]{2,1,0:T(8,128)(2,1)S(1)} %all_to_all.27.arrived), custom_call_target="tpu_custom_call" | custom-call | tf_op jit(solution)/shard_map/pallas_call | solution.py:426
  (2 shorter events, 0.0 us)
Async XLA Ops:
  22.2 2.0 %collective-permute-start = (bf16[256,768]{1,0:T(8,128)(2,1)S(1)}, bf16[256,768]{1,0:T(8,128)(2,1)S(1)}, u32[]{:S(2)}, u32[]{:S(2)}) collective-permute-start(bf16[256,768]{1,0:T(8,128)(2,1)S(1)} %bitcast.10), channel_id=1, source_target_pairs={{0,1},{1,0},{2,3},{3,2},{4,5},{5,4},{6,7},{7,6},{8,9},{9,8},{10,11... | collective-permute-start | bytes 1179656 | tf_op jit(solution)/shard_map/ppermute | solution.py:454
  22.2 11.5 %collective-permute-start.1 = (bf16[256,768]{1,0:T(8,128)(2,1)S(1)}, bf16[256,768]{1,0:T(8,128)(2,1)S(1)}, u32[]{:S(2)}, u32[]{:S(2)}) collective-permute-start(bf16[256,768]{1,0:T(8,128)(2,1)S(1)} %bitcast.11), channel_id=1, source_target_pairs={{0,2},{1,3},{2,0},{3,1},{4,6},{5,7},{6,4},{7,5},{8,10},{9,11},{10,... | collective-permute-start | bytes 1179656 | tf_op jit(solution)/shard_map/ppermute | solution.py:454
  23.2 10.8 %collective-permute-start.3 = (bf16[256,768]{1,0:T(8,128)(2,1)S(1)}, bf16[256,768]{1,0:T(8,128)(2,1)S(1)}, u32[]{:S(2)}, u32[]{:S(2)}) collective-permute-start(bf16[256,768]{1,0:T(8,128)(2,1)S(1)} %bitcast.12), channel_id=1, source_target_pairs={{0,4},{1,5},{2,6},{3,7},{4,0},{5,1},{6,2},{7,3},{8,12},{9,13},{10,... | collective-permute-start | bytes 1179656 | tf_op jit(solution)/shard_map/ppermute | solution.py:454
  28.1 17.0 %all-to-all-start.1 = ((bf16[16,96,128]{2,1,0:T(8,128)(2,1)}), bf16[16,96,128]{2,1,0:T(8,128)(2,1)S(1)}, u32[]{:S(2)}, u32[]{:S(2)}) async-start(bf16[16,96,128]{2,1,0:T(8,128)(2,1)} %get-tuple-element.14), calls=%async_computation.1 | async-start | bytes 786432 | tf_op jit(solution)/shard_map/all_to_all | solution.py:415
  33.7 16.3 %collective-permute-start.2 = (bf16[256,768]{1,0:T(8,128)(2,1)S(1)}, bf16[256,768]{1,0:T(8,128)(2,1)}, u32[]{:S(2)}, u32[]{:S(2)}) collective-permute-start(bf16[256,768]{1,0:T(8,128)(2,1)S(1)} %collective-permute-done.1.refs_2_), channel_id=1, source_target_pairs={{0,1},{1,0},{2,3},{3,2},{4,5},{5,4},{6,7},{7,6},{8,9},{9,8},{10,11... | collective-permute-start | bytes 1179656 | tf_op jit(solution)/shard_map/ppermute | solution.py:454
  33.9 16.1 %copy-start.2 = (bf16[256,768]{1,0:T(8,128)(2,1)}, bf16[256,768]{1,0:T(8,128)(2,1)S(1)}, u32[]{:S(2)}) copy-start(bf16[256,768]{1,0:T(8,128)(2,1)S(1)} %collective-permute-done.3.refs_4_) | copy-start | bytes 1179652
  33.9 16.1 %collective-permute-start.4 = (bf16[256,768]{1,0:T(8,128)(2,1)S(1)}, bf16[256,768]{1,0:T(8,128)(2,1)}, u32[]{:S(2)}, u32[]{:S(2)}) collective-permute-start(bf16[256,768]{1,0:T(8,128)(2,1)S(1)} %collective-permute-done.3.refs_4_), channel_id=1, source_target_pairs={{0,1},{1,0},{2,3},{3,2},{4,5},{5,4},{6,7},{7,6},{8,9},{9,8},{10,11... | collective-permute-start | bytes 1179656 | tf_op jit(solution)/shard_map/ppermute | solution.py:454
  34.3 8.8 %collective-permute-start.5 = (bf16[128,768]{1,0:T(8,128)(2,1)S(1)}, bf16[128,768]{1,0:T(8,128)(2,1)S(1)}, u32[]{:S(2)}, u32[]{:S(2)}) collective-permute-start(bf16[128,768]{1,0:T(8,128)(2,1)S(1)} %slice.8), channel_id=1, source_target_pairs={{0,4},{1,5},{2,6},{3,7},{4,0},{5,1},{6,2},{7,3},{8,12},{9,13},{10,... | collective-permute-start | bytes 589832 | tf_op jit(solution)/shard_map/ppermute | solution.py:454
  35.8 9.3 %collective-permute-start.6 = (bf16[128,768]{1,0:T(8,128)(2,1)S(1)}, bf16[128,768]{1,0:T(8,128)(2,1)}, u32[]{:S(2)}, u32[]{:S(2)}) collective-permute-start(bf16[128,768]{1,0:T(8,128)(2,1)S(1)} %slice.9), channel_id=1, source_target_pairs={{0,2},{1,3},{2,0},{3,1},{4,6},{5,7},{6,4},{7,5},{8,10},{9,11},{10,... | collective-permute-start | bytes 589832 | tf_op jit(solution)/shard_map/ppermute | solution.py:454
  43.0 13.2 %collective-permute-start.7 = (bf16[128,768]{1,0:T(8,128)(2,1)S(1)}, bf16[128,768]{1,0:T(8,128)(2,1)}, u32[]{:S(2)}, u32[]{:S(2)}) collective-permute-start(bf16[128,768]{1,0:T(8,128)(2,1)S(1)} %collective-permute-done.5.refs_0_), channel_id=1, source_target_pairs={{0,1},{1,0},{2,3},{3,2},{4,5},{5,4},{6,7},{7,6},{8,9},{9,8},{10,11... | collective-permute-start | bytes 589832 | tf_op jit(solution)/shard_map/ppermute | solution.py:454
  45.1 11.1 %collective-permute-start.8 = (bf16[128,768]{1,0:T(8,128)(2,1)}, bf16[128,768]{1,0:T(8,128)(2,1)}, u32[]{:S(2)}, u32[]{:S(2)}) collective-permute-start(bf16[128,768]{1,0:T(8,128)(2,1)} %collective-permute-done.6.refs_1_), channel_id=1, source_target_pairs={{0,1},{1,0},{2,3},{3,2},{4,5},{5,4},{6,7},{7,6},{8,9},{9,8},{10,11... | collective-permute-start | bytes 589832 | tf_op jit(solution)/shard_map/ppermute | solution.py:454
  46.1 17.1 %all-to-all-start.2 = ((bf16[16,96,128]{2,1,0:T(8,128)(2,1)}), bf16[16,96,128]{2,1,0:T(8,128)(2,1)S(1)}, u32[]{:S(2)}, u32[]{:S(2)}) async-start(bf16[16,96,128]{2,1,0:T(8,128)(2,1)} %shard_map.69), calls=%async_computation.2 | async-start | bytes 786432 | tf_op jit(solution)/shard_map/all_to_all | solution.py:415
  50.1 1.0 %copy-start.3 = (bf16[256,768]{1,0:T(8,128)(2,1)S(1)}, bf16[256,768]{1,0:T(8,128)(2,1)}, u32[]{:S(2)}) copy-start(bf16[256,768]{1,0:T(8,128)(2,1)} %copy-done.2) | copy-start | bytes 1179652
  55.2 1.0 %copy-start = (bf16[768,768]{1,0:T(8,128)(2,1)}, bf16[768,768]{1,0:T(8,128)(2,1)S(1)}, u32[]{:S(2)}) copy-start(bf16[768,768]{1,0:T(8,128)(2,1)S(1)} %get-tuple-element.19.left_near) | copy-start | bytes 3538948
  59.3 0.8 copy-start.1
  67.5 2.2 %collective-permute-start.9 = (f32[128,768]{1,0:T(8,128)S(1)}, f32[128,768]{1,0:T(8,128)S(1)}, u32[]{:S(2)}, u32[]{:S(2)}) collective-permute-start(f32[128,768]{1,0:T(8,128)S(1)} %get-tuple-element.22), channel_id=1, source_target_pairs={{0,1},{1,0},{2,3},{3,2},{4,5},{5,4},{6,7},{7,6},{8,9},{9,8},{10,11... | collective-permute-start | bytes 1179656 | tf_op jit(solution)/shard_map/ppermute | solution.py:454
  67.5 2.1 %collective-permute-start.10 = (bf16[384,384]{1,0:T(8,128)(2,1)S(1)}, bf16[384,384]{1,0:T(8,128)(2,1)S(1)}, u32[]{:S(2)}, u32[]{:S(2)}) collective-permute-start(bf16[384,384]{1,0:T(8,128)(2,1)S(1)} %get-tuple-element.25), channel_id=1, source_target_pairs={{0,1},{1,0},{2,3},{3,2},{4,5},{5,4},{6,7},{7,6},{8,9},{9,8},{10,11... | collective-permute-start | bytes 884744 | tf_op jit(solution)/shard_map/ppermute | solution.py:454

commit v7 on v6

--- a/solution.py
+++ b/solution.py
@@ -166,47 +166,42 @@
             tied[:, spot : spot + 2 * part, :] = both.astype(BF16)
 
 
-def operand_kernel(weights, bounds, *refs, rows, col_dev, slots):
+def operand_kernel(weights, bounds, *refs, rows, col_dev):
     *raw, left, ops, heads, heads_back, sem = refs
-    width = raw[0].shape[1]
+    width = left.shape[1]
     half = width // CORES
     cells = bounds.shape[0]
-    per_block = len(raw) // (2 * len(slots))
     me, core, kind = position()
     first_col = lax.axis_index("pos") * col_dev
+    fetches = []
     for at, source_of in ((0, 1), (1, 0), (3, 2)):
-
-        @pl.when(kind == at)
-        def _():
-            copy = pltpu.make_async_copy(
-                weights.at[source_of, :, head_lanes(core, half)], heads, sem
-            )
-            copy.start()
-            copy.wait()
-
-    @pl.when(kind == 2)
-    def _():
         copy = pltpu.make_async_copy(
-            weights.at[3, head_lanes(core, half), :], heads_back, sem
+            weights.at[source_of, :, head_lanes(core, half)], heads, sem
         )
-        copy.start()
-        copy.wait()
-
-    blocks = []
-    for at in range(0, len(raw), per_block):
-        pieces = [ref[...] for ref in raw[at : at + per_block]]
-        blocks.append(pieces[0] if per_block == 1 else jnp.concatenate(pieces, axis=0))
+        fetches.append((kind == at, copy))
+    copy = pltpu.make_async_copy(weights.at[3, head_lanes(core, half), :], heads_back, sem)
+    fetches.append((kind == 2, copy))
+    for here, copy in fetches:
+        pl.when(here)(copy.start)
+
+    blocks, pieces = [], []
+    for ref in raw:
+        pieces.append(ref[...])
+        if sum(piece.shape[0] for piece in pieces) == 2 * cells:
+            blocks.append(jnp.concatenate(pieces, axis=0) if len(pieces) > 1 else pieces[0])
+            pieces = []
     source, upstream = part_rows(blocks, rows, cells)
     normed = normalise(source)[0].astype(BF16)
     first, last = bounds[:, 0:1], bounds[:, 1:2]
     covered = jnp.concatenate(
         [
-            row_mask(first, last, first_col + jnp.bitwise_xor(me, 2 * slot + side))
-            for slot in slots
-            for side in range(2)
+            row_mask(first, last, first_col + jnp.bitwise_xor(me, at))
+            for at in range(2 * KINDS)
         ],
         axis=0,
     )
+    for here, copy in fetches:
+        pl.when(here)(copy.wait)
 
     @pl.when(kind == 2)
     def _():
@@ -245,8 +240,8 @@
 
 
 def gradient_kernel(
-    pairs, proj, bounds, ops_near, ops_far, weights, left_near, left_far, own, other, product, spare,
-    grads, right, heads_in, left, sems, *, col_dev
+    pairs, proj, bounds, ops, weights, left_far, own, other, product, spare, grads, right, heads_in,
+    left, sems, *, col_dev
 ):
     cells = proj.shape[1] // 2
     half = proj.shape[2]
@@ -258,12 +253,8 @@
         )
         for at in range(3)
     ]
-    near = left_near.shape[0]
-    copies.append(pltpu.make_async_copy(left_near, left.at[pl.ds(0, near)], sems.at[3]))
-    copies.append(
-        pltpu.make_async_copy(left_far, left.at[pl.ds(near, left_far.shape[0])], sems.at[4])
-    )
-    for at in (3, 4, 0, 1, 2):
+    copies.append(pltpu.make_async_copy(left_far, left, sems.at[3]))
+    for at in (3, 0, 1, 2):
         copies[at].start()
     first, last = bounds[:, 0:1], bounds[:, 1:2]
     masks = []
@@ -299,12 +290,7 @@
             flip = jnp.where(use_probs, a_flip, b_flip)
             chosen.append(jnp.where(use_flip, flip, flat).astype(BF16))
         cat = jnp.concatenate(
-            [
-                ops[at : at + cells, lanes]
-                for ops in (ops_near, ops_far)
-                for at in range(0, ops.shape[0], cells)
-            ],
-            axis=1,
+            [ops[at : at + cells, lanes] for at in range(0, ops.shape[0], cells)], axis=1
         )
         result = dot(jnp.concatenate(chosen, axis=0), cat)
         result = jnp.where(plane_low, result[:cells], result[cells:]) * plane_covered
@@ -315,7 +301,6 @@
             ]
 
     copies[3].wait()
-    copies[4].wait()
 
     @pl.when(kind < KINDS - 1)
     def _():
@@ -341,7 +326,7 @@
         term = dot(grads[at], heads_in[at], (1, 1))
         total = term if total is None else total + term
     own[...] = total[:cells]
-    other[...] = total[cells:]
+    other[...] = total[cells:].astype(BF16)
 
 
 def pack_kernel(grad_own, grad_recv, normed, bounds, product, spare, payload, *, rows):
@@ -349,7 +334,7 @@
     tiles = width // LANES
     half = product.shape[1]
     group = rows * tiles
-    grad_norm = grad_own[...] + grad_recv[...]
+    grad_norm = grad_own[...] + grad_recv[...].astype(F32)
     mean = jnp.mean(grad_norm * normed[...], -1, keepdims=True)
     result = (grad_norm - normed[...] * mean) * bounds[:, 2:3]
     result = result.astype(BF16)
@@ -487,47 +472,46 @@
         shape((chips, tied_rows, reads), BF16),
         8,
     )
+    held_bounds = bounds
     pairs = exchange(copies, same_core)
     diagonal = [swap(raw[1][:reads], 2 * CORES), swap(raw[2][reads:], CORES)]
 
-    def operands(slots, blocks):
-        count_here = 2 * reads * len(slots)
-        return call(
-            functools.partial(operand_kernel, rows=rows, col_dev=col_dev, slots=slots),
-            (weights, bounds, *blocks),
-            (shape((count_here, width), BF16), shape((count_here, half), BF16)),
-            24,
-            (0,),
-            [
-                pltpu.VMEM((width, half), BF16),
-                pltpu.VMEM((half, width), BF16),
-                pltpu.SemaphoreType.DMA,
-            ],
-            pl.CostEstimate(flops=4 * 10**9, bytes_accessed=8 * MIB, transcendentals=0),
-        )
-
-    left_near, ops_near = operands(
-        (0, 1, 2), (own, other, raw[1], swap(raw[1], 1), raw[2], swap(raw[2], 1))
-    )
-    left_far, ops_far = operands((3,), (*diagonal, *[swap(a, 1) for a in diagonal]))
+    blocks = [own, other]
+    for near in (raw[1], raw[2]):
+        blocks += [near, swap(near, 1)]
+    blocks += [*diagonal, *[swap(a, 1) for a in diagonal]]
+    cells = 2 * KINDS * reads
+    left, ops = call(
+        functools.partial(operand_kernel, rows=rows, col_dev=col_dev),
+        (weights, held_bounds, *blocks),
+        (shape((cells, width), BF16), shape((cells, half), BF16)),
+        24,
+        (0,),
+        [
+            pltpu.VMEM((width, half), BF16),
+            pltpu.VMEM((half, width), BF16),
+            pltpu.SemaphoreType.DMA,
+        ],
+        pl.CostEstimate(flops=16 * 10**9, bytes_accessed=8 * MIB, transcendentals=0),
+    )
 
     grad_own, grad_other, product, spare = call(
         functools.partial(gradient_kernel, col_dev=col_dev),
-        (pairs, proj, bounds, ops_near, ops_far, weights, left_near, left_far),
+        (pairs, proj, bounds, ops, weights, left),
         (
             shape((reads, width), F32),
-            shape((reads, width), F32),
+            shape((reads, width), BF16),
             shape((width, half), BF16),
             shape((half, half), BF16),
         ),
         24,
-        (5, 6, 7),
+        (4, 5),
         [
             pltpu.VMEM((3, 2 * reads, half), BF16),
-            pltpu.VMEM((2 * KINDS * reads, half), BF16),
+            pltpu.VMEM((cells, half), BF16),
             pltpu.VMEM((3, width, half), BF16),
-            pltpu.VMEM((2 * KINDS * reads, width), BF16),
-            pltpu.SemaphoreType.DMA((5,)),
+            pltpu.VMEM((cells, width), BF16),
+            pltpu.SemaphoreType.DMA((4,)),
         ],
     )
     grad_recv = swap(grad_other, 1)

time: 95.3 us -> 94.3 us (0.990)
  Pallas kernels: 18.3 us -> 15.6 us
  local copies, waits for them, and re-layouts: 3.02 us -> 4.15 us
    pallas_call x7 -> x6, Pallas kernels: 18.3 us -> 15.6 us  [call(): pl.pallas_call(kernel, in_specs=[away if at in far else near for at in ra...]
    all_to_all x2, waiting for transfers between devices: 3.18 us -> 5.57 us  [exchange(): lax.all_to_all(array, 'read', split_axis=0, concat_axis=0, tiled=True, ax...]
    ppermute x11, waiting for transfers between devices: 12 us -> 10.4 us  [swap(): return lax.ppermute(array, 'read', [(i, i ^ bits) for i in range(count)])]
    unnamed x8 -> x10, local copies, waits for them, and re-layouts: 2.77 us -> 3.9 us
  transfers between devices with their start and end apart: 13 -> 13, of which waited for: 6 -> 7; matrix products, arithmetic and copies ran while one was open for 0% -> 0% of each run, Pallas kernels for 13% -> 10%
where the time goes in v7:
time: 94.3 us; the launch traced here: 93.7 us
  blocking collectives  43.3 us (46%)
  waiting for transfers between devices  15.9 us (17%)
  Pallas kernels  15.6 us (17%)
  starting transfers between devices  12.9 us (14%)
  local copies, waits for them, and re-layouts  4.15 us (4%)
  other arithmetic  1.06 us (1%)
    all_to_all x2, blocking collectives, exchange(): lax.all_to_all(array, 'read', split_axis=0, concat_axis=0, tiled=True, ax...  43.3 us
    pallas_call x6, Pallas kernels, call(): pl.pallas_call(kernel, in_specs=[away if at in far else near for at in ra...  15.6 us
    ppermute x11, waiting for transfers between devices, swap(): return lax.ppermute(array, 'read', [(i, i ^ bits) for i in range(count)])  10.4 us
    all_to_all x2, starting transfers between devices, exchange(): lax.all_to_all(array, 'read', split_axis=0, concat_axis=0, tiled=True, ax...  7.85 us
    all_to_all x2, waiting for transfers between devices, exchange(): lax.all_to_all(array, 'read', split_axis=0, concat_axis=0, tiled=True, ax...  5.57 us
    ppermute x11, starting transfers between devices, swap(): return lax.ppermute(array, 'read', [(i, i ^ bits) for i in range(count)])  5.04 us
    unnamed x10, local copies, waits for them, and re-layouts  3.9 us
  transfers between devices with their start and end apart: 13, of which 7 were waited for; matrix products, arithmetic and copies ran while one was open for 0% of the time, Pallas kernels for 10%

profile of v7, /device:TPU:0, one launch (start us, length us, event | category | flops | bytes accessed | tf_op | source)
XLA Modules:
  0.0 93.7 jit_solution(17699144835120035070)
XLA Ops:
  0.6 1.1 %pad_maximum_fusion = bf16[2,4,32,768]{3,2,1,0:T(8,128)(2,1)S(1)} fusion(bf16[1,4,32,768]{3,2,1,0:T(8,128)(2,1)} %bitcast.16, bf16[1,4,32,768]{3,2,1,0:T(8,128)(2,1)} %bitcast.17), kind=kLoop, calls=%fused_computation | loop fusion | flops 196608 | bytes 786432 | tf_op jit(solution)/shard_map/stack | solution.py:442
  1.7 0.2 copy.7
  1.9 20.3 %all_to_all.26 = bf16[32,8,768]{2,1,0:T(8,128)(2,1)S(1)} all-to-all(bf16[32,8,768]{2,1,0:T(8,128)(2,1)S(1)} %copy.7), channel_id=1, replica_groups=mesh['read'=32,'pos'=1] {'read'}, dimensions={0} | all-to-all | bytes 786432 | tf_op jit(solution)/shard_map/all_to_all | solution.py:400
  22.2 0.0 collective-permute-start
  22.2 1.0 %collective-permute-start.3 = (bf16[256,768]{1,0:T(8,128)(2,1)S(1)}, bf16[256,768]{1,0:T(8,128)(2,1)S(1)}, u32[]{:S(2)}, u32[]{:S(2)}) collective-permute-start(bf16[256,768]{1,0:T(8,128)(2,1)S(1)} %bitcast.11), channel_id=1, source_target_pairs={{0,4},{1,5},{2,6},{3,7},{4,0},{5,1},{6,2},{7,3},{8,12},{9,13},{10,... | collective-permute-start | bytes 1179656 | tf_op jit(solution)/shard_map/ppermute | solution.py:439
  23.2 1.0 %collective-permute-start.1 = (bf16[256,768]{1,0:T(8,128)(2,1)S(1)}, bf16[256,768]{1,0:T(8,128)(2,1)S(1)}, u32[]{:S(2)}, u32[]{:S(2)}) collective-permute-start(bf16[256,768]{1,0:T(8,128)(2,1)S(1)} %bitcast.12), channel_id=1, source_target_pairs={{0,2},{1,3},{2,0},{3,1},{4,6},{5,7},{6,4},{7,5},{8,10},{9,11},{10,... | collective-permute-start | bytes 1179656 | tf_op jit(solution)/shard_map/ppermute | solution.py:439
  24.2 0.0 collective-permute-done.other.refs_1_
  24.2 4.0 %shard_map.68 = (bf16[3,256,384]{2,1,0:T(8,128)(2,1)S(1)}, bf16[16,96,128]{2,1,0:T(8,128)(2,1)}, f32[128,768]{1,0:T(8,128)S(1)}, f32[128,128]{1,0:T(8,128)S(1)}) custom-call(bf16[256,768]{1,0:T(8,128)(2,1)S(1)} %bitcast.13, bf16[256,768]{1,0:T(8,128)(2,1)S(1)} %collective-permute-done.other.refs_1_, bf16[4,768,768]{2,1,0:T(8,128)(2,1)} %weights.5, ...), custom_call_target="tpu_custom_call" | custom-call | tf_op jit(solution)/shard_map/pallas_call | solution.py:411
  28.1 3.6 %all-to-all-start.1 = ((bf16[16,96,128]{2,1,0:T(8,128)(2,1)}), bf16[16,96,128]{2,1,0:T(8,128)(2,1)S(1)}, u32[]{:S(2)}, u32[]{:S(2)}) async-start(bf16[16,96,128]{2,1,0:T(8,128)(2,1)} %get-tuple-element.12), calls=%async_computation.1 | async-start | bytes 786432 | tf_op jit(solution)/shard_map/all_to_all | solution.py:400
  31.7 2.0 %collective-permute-done.3.refs_4_ = bf16[256,768]{1,0:T(8,128)(2,1)S(1)} collective-permute-done((bf16[256,768]{1,0:T(8,128)(2,1)S(1)}, bf16[256,768]{1,0:T(8,128)(2,1)S(1)}, u32[]{:S(2)}, u32[]{:S(2)}) %collective-permute-start.3) | collective-permute-done | bytes 393248 | tf_op jit(solution)/shard_map/ppermute | solution.py:439
  33.8 0.5 collective-permute-start.6
  34.3 0.3 collective-permute-done.1.refs_2_
  34.6 0.0 copy-start.1
  34.6 1.3 %collective-permute-start.5 = (bf16[128,768]{1,0:T(8,128)(2,1)S(1)}, bf16[128,768]{1,0:T(8,128)(2,1)}, u32[]{:S(2)}, u32[]{:S(2)}) collective-permute-start(bf16[128,768]{1,0:T(8,128)(2,1)S(1)} %slice.8), channel_id=1, source_target_pairs={{0,4},{1,5},{2,6},{3,7},{4,0},{5,1},{6,2},{7,3},{8,12},{9,13},{10,... | collective-permute-start | bytes 589832 | tf_op jit(solution)/shard_map/ppermute | solution.py:439
  35.9 0.0 collective-permute-start.4
  35.9 0.5 collective-permute-start.2
  36.4 6.4 %collective-permute-done.6.refs_7_ = bf16[128,768]{1,0:T(8,128)(2,1)} collective-permute-done((bf16[128,768]{1,0:T(8,128)(2,1)S(1)}, bf16[128,768]{1,0:T(8,128)(2,1)}, u32[]{:S(2)}, u32[]{:S(2)}) %collective-permute-start.6) | collective-permute-done | bytes 196640 | tf_op jit(solution)/shard_map/ppermute | solution.py:439
  42.7 0.0 collective-permute-start.8
  42.8 0.4 collective-permute-done.5.refs_6_
  43.1 0.1 collective-permute-start.7
  43.3 1.4 %all-to-all-done.1.parts = bf16[16,96,128]{2,1,0:T(8,128)(2,1)S(1)} async-done(((bf16[16,96,128]{2,1,0:T(8,128)(2,1)}), bf16[16,96,128]{2,1,0:T(8,128)(2,1)S(1)}, u32[]{:S(2)}, u32[]{:S(2)}) %all-to-all-start.1) | async-done | bytes 393248 | tf_op jit(solution)/shard_map/all_to_all | solution.py:400
  44.7 1.0 %shard_map.69 = bf16[16,96,128]{2,1,0:T(8,128)(2,1)} custom-call(bf16[16,96,128]{2,1,0:T(8,128)(2,1)S(1)} %all-to-all-done.1.parts), custom_call_target="tpu_custom_call" | custom-call | tf_op jit(solution)/shard_map/pallas_call | solution.py:411
  45.6 4.3 %all-to-all-start.2 = ((bf16[16,96,128]{2,1,0:T(8,128)(2,1)}), bf16[16,96,128]{2,1,0:T(8,128)(2,1)S(1)}, u32[]{:S(2)}, u32[]{:S(2)}) async-start(bf16[16,96,128]{2,1,0:T(8,128)(2,1)} %shard_map.69), calls=%async_computation.2 | async-start | bytes 786432 | tf_op jit(solution)/shard_map/all_to_all | solution.py:400
  49.9 0.0 collective-permute-done.8.refs_9_
  49.9 0.0 collective-permute-done.4.refs_5_
  49.9 0.0 copy-start.3
  50.0 0.8 copy-done.3
  50.7 0.0 collective-permute-done.7.refs_8_
  50.7 0.0 collective-permute-done.2.refs_3_
  50.7 0.0 copy-done.1
  50.7 0.0 copy-start.2
  50.7 1.0 %copy-done.2 = bf16[256,768]{1,0:T(8,128)(2,1)S(1)} copy-done((bf16[256,768]{1,0:T(8,128)(2,1)S(1)}, bf16[256,768]{1,0:T(8,128)(2,1)}, u32[]{:S(2)}) %copy-start.2) | copy-done | bytes 393240
  51.7 0.0 copy-start.4
  51.7 1.0 %copy-done.4 = bf16[256,768]{1,0:T(8,128)(2,1)S(1)} copy-done((bf16[256,768]{1,0:T(8,128)(2,1)S(1)}, bf16[256,768]{1,0:T(8,128)(2,1)}, u32[]{:S(2)}) %copy-start.4) | copy-done | bytes 393240
  52.7 4.7 %shard_map.70 = (bf16[1024,768]{1,0:T(8,128)(2,1)S(1)}, bf16[1024,384]{1,0:T(8,128)(2,1)S(1)}) custom-call(bf16[4,768,768]{2,1,0:T(8,128)(2,1)} %weights.5, f32[128,128]{1,0:T(8,128)S(1)} %get-tuple-element.14.bounds, bf16[256,768]{1,0:T(8,128)(2,1)S(1)} %bitcast.14, bf16[256,768]{1,0:T(8,128)(2,1)S(1)} %collective-permute-done.other.refs_1_, ...), custom_call_target="tpu_custom_call" | custom-call | flops 16000000000 | bytes 8388608 | tf_op jit(solution)/shard_map/pallas_call | solution.py:411
  57.4 0.0 copy-start
  57.5 1.2 %copy-done = bf16[1024,768]{1,0:T(8,128)(2,1)} copy-done((bf16[1024,768]{1,0:T(8,128)(2,1)}, bf16[1024,768]{1,0:T(8,128)(2,1)S(1)}, u32[]{:S(2)}) %copy-start) | copy-done | bytes 1572888
  58.6 4.2 %all-to-all-done.2.pairs = bf16[16,96,128]{2,1,0:T(8,128)(2,1)S(1)} async-done(((bf16[16,96,128]{2,1,0:T(8,128)(2,1)}), bf16[16,96,128]{2,1,0:T(8,128)(2,1)S(1)}, u32[]{:S(2)}, u32[]{:S(2)}) %all-to-all-start.2) | async-done | bytes 393248 | tf_op jit(solution)/shard_map/all_to_all | solution.py:400
  62.8 4.0 %shard_map.71 = (f32[128,768]{1,0:T(8,128)S(1)}, bf16[128,768]{1,0:T(8,128)(2,1)S(1)}, bf16[768,384]{1,0:T(8,128)(2,1)S(1)}, bf16[384,384]{1,0:T(8,128)(2,1)S(1)}) custom-call(bf16[16,96,128]{2,1,0:T(8,128)(2,1)S(1)} %all-to-all-done.2.pairs, bf16[3,256,384]{2,1,0:T(8,128)(2,1)S(1)} %get-tuple-element.13.proj, f32[128,128]{1,0:T(8,128)S(1)} %get-tuple-element.14.bounds, ...), custom_call_target="tpu_custom_call" | custom-call | tf_op jit(solution)/shard_map/pallas_call | solution.py:411
  66.8 0.1 collective-permute-start.10
  66.9 0.5 collective-permute-start.9
  67.4 1.4 %collective-permute-done.9.grad_recv = bf16[128,768]{1,0:T(8,128)(2,1)S(1)} collective-permute-done((bf16[128,768]{1,0:T(8,128)(2,1)S(1)}, bf16[128,768]{1,0:T(8,128)(2,1)S(1)}, u32[]{:S(2)}, u32[]{:S(2)}) %collective-permute-start.9) | collective-permute-done | bytes 196640 | tf_op jit(solution)/shard_map/ppermute | solution.py:439
  68.7 0.0 collective-permute-done.10.spare
  68.7 0.7 shard_map.72
  69.4 23.0 %all_to_all.27.arrived = bf16[32,24,512]{2,1,0:T(8,128)(2,1)S(1)} all-to-all(bf16[32,24,512]{2,1,0:T(8,128)(2,1)S(1)} %bitcast.9), channel_id=1, replica_groups=mesh['read'=32,'pos'=1] {'read'}, dimensions={0} | all-to-all | bytes 1572864 | tf_op jit(solution)/shard_map/all_to_all | solution.py:400
  92.5 1.3 %shard_map.73 = (bf16[4,32,768]{2,1,0:T(8,128)(2,1)}, f32[24,3072]{1,0:T(8,128)}) custom-call(bf16[32,24,512]{2,1,0:T(8,128)(2,1)S(1)} %all_to_all.27.arrived), custom_call_target="tpu_custom_call" | custom-call | tf_op jit(solution)/shard_map/pallas_call | solution.py:411
  (2 shorter events, 0.0 us)
Async XLA Ops:
  22.2 2.0 %collective-permute-start = (bf16[256,768]{1,0:T(8,128)(2,1)S(1)}, bf16[256,768]{1,0:T(8,128)(2,1)S(1)}, u32[]{:S(2)}, u32[]{:S(2)}) collective-permute-start(bf16[256,768]{1,0:T(8,128)(2,1)S(1)} %bitcast.10), channel_id=1, source_target_pairs={{0,1},{1,0},{2,3},{3,2},{4,5},{5,4},{6,7},{7,6},{8,9},{9,8},{10,11... | collective-permute-start | bytes 1179656 | tf_op jit(solution)/shard_map/ppermute | solution.py:439
  22.2 11.5 %collective-permute-start.3 = (bf16[256,768]{1,0:T(8,128)(2,1)S(1)}, bf16[256,768]{1,0:T(8,128)(2,1)S(1)}, u32[]{:S(2)}, u32[]{:S(2)}) collective-permute-start(bf16[256,768]{1,0:T(8,128)(2,1)S(1)} %bitcast.11), channel_id=1, source_target_pairs={{0,4},{1,5},{2,6},{3,7},{4,0},{5,1},{6,2},{7,3},{8,12},{9,13},{10,... | collective-permute-start | bytes 1179656 | tf_op jit(solution)/shard_map/ppermute | solution.py:439
  23.2 11.4 %collective-permute-start.1 = (bf16[256,768]{1,0:T(8,128)(2,1)S(1)}, bf16[256,768]{1,0:T(8,128)(2,1)S(1)}, u32[]{:S(2)}, u32[]{:S(2)}) collective-permute-start(bf16[256,768]{1,0:T(8,128)(2,1)S(1)} %bitcast.12), channel_id=1, source_target_pairs={{0,2},{1,3},{2,0},{3,1},{4,6},{5,7},{6,4},{7,5},{8,10},{9,11},{10,... | collective-permute-start | bytes 1179656 | tf_op jit(solution)/shard_map/ppermute | solution.py:439
  28.1 16.5 %all-to-all-start.1 = ((bf16[16,96,128]{2,1,0:T(8,128)(2,1)}), bf16[16,96,128]{2,1,0:T(8,128)(2,1)S(1)}, u32[]{:S(2)}, u32[]{:S(2)}) async-start(bf16[16,96,128]{2,1,0:T(8,128)(2,1)} %get-tuple-element.12), calls=%async_computation.1 | async-start | bytes 786432 | tf_op jit(solution)/shard_map/all_to_all | solution.py:400
  33.8 9.0 %collective-permute-start.6 = (bf16[128,768]{1,0:T(8,128)(2,1)S(1)}, bf16[128,768]{1,0:T(8,128)(2,1)}, u32[]{:S(2)}, u32[]{:S(2)}) collective-permute-start(bf16[128,768]{1,0:T(8,128)(2,1)S(1)} %slice.9), channel_id=1, source_target_pairs={{0,2},{1,3},{2,0},{3,1},{4,6},{5,7},{6,4},{7,5},{8,10},{9,11},{10,... | collective-permute-start | bytes 589832 | tf_op jit(solution)/shard_map/ppermute | solution.py:439
  34.6 16.2 %copy-start.1 = (bf16[256,768]{1,0:T(8,128)(2,1)}, bf16[256,768]{1,0:T(8,128)(2,1)S(1)}, u32[]{:S(2)}) copy-start(bf16[256,768]{1,0:T(8,128)(2,1)S(1)} %collective-permute-done.1.refs_2_) | copy-start | bytes 1179652
  34.6 8.5 %collective-permute-start.5 = (bf16[128,768]{1,0:T(8,128)(2,1)S(1)}, bf16[128,768]{1,0:T(8,128)(2,1)}, u32[]{:S(2)}, u32[]{:S(2)}) collective-permute-start(bf16[128,768]{1,0:T(8,128)(2,1)S(1)} %slice.8), channel_id=1, source_target_pairs={{0,4},{1,5},{2,6},{3,7},{4,0},{5,1},{6,2},{7,3},{8,12},{9,13},{10,... | collective-permute-start | bytes 589832 | tf_op jit(solution)/shard_map/ppermute | solution.py:439
  35.9 14.1 %collective-permute-start.4 = (bf16[256,768]{1,0:T(8,128)(2,1)S(1)}, bf16[256,768]{1,0:T(8,128)(2,1)S(1)}, u32[]{:S(2)}, u32[]{:S(2)}) collective-permute-start(bf16[256,768]{1,0:T(8,128)(2,1)S(1)} %collective-permute-done.3.refs_4_), channel_id=1, source_target_pairs={{0,1},{1,0},{2,3},{3,2},{4,5},{5,4},{6,7},{7,6},{8,9},{9,8},{10,11... | collective-permute-start | bytes 1179656 | tf_op jit(solution)/shard_map/ppermute | solution.py:439
  35.9 14.8 %collective-permute-start.2 = (bf16[256,768]{1,0:T(8,128)(2,1)S(1)}, bf16[256,768]{1,0:T(8,128)(2,1)}, u32[]{:S(2)}, u32[]{:S(2)}) collective-permute-start(bf16[256,768]{1,0:T(8,128)(2,1)S(1)} %collective-permute-done.1.refs_2_), channel_id=1, source_target_pairs={{0,1},{1,0},{2,3},{3,2},{4,5},{5,4},{6,7},{7,6},{8,9},{9,8},{10,11... | collective-permute-start | bytes 1179656 | tf_op jit(solution)/shard_map/ppermute | solution.py:439
  42.7 7.2 %collective-permute-start.8 = (bf16[128,768]{1,0:T(8,128)(2,1)}, bf16[128,768]{1,0:T(8,128)(2,1)}, u32[]{:S(2)}, u32[]{:S(2)}) collective-permute-start(bf16[128,768]{1,0:T(8,128)(2,1)} %collective-permute-done.6.refs_7_), channel_id=1, source_target_pairs={{0,1},{1,0},{2,3},{3,2},{4,5},{5,4},{6,7},{7,6},{8,9},{9,8},{10,11... | collective-permute-start | bytes 589832 | tf_op jit(solution)/shard_map/ppermute | solution.py:439
  43.1 7.6 %collective-permute-start.7 = (bf16[128,768]{1,0:T(8,128)(2,1)}, bf16[128,768]{1,0:T(8,128)(2,1)}, u32[]{:S(2)}, u32[]{:S(2)}) collective-permute-start(bf16[128,768]{1,0:T(8,128)(2,1)} %collective-permute-done.5.refs_6_), channel_id=1, source_target_pairs={{0,1},{1,0},{2,3},{3,2},{4,5},{5,4},{6,7},{7,6},{8,9},{9,8},{10,11... | collective-permute-start | bytes 589832 | tf_op jit(solution)/shard_map/ppermute | solution.py:439
  45.6 17.2 %all-to-all-start.2 = ((bf16[16,96,128]{2,1,0:T(8,128)(2,1)}), bf16[16,96,128]{2,1,0:T(8,128)(2,1)S(1)}, u32[]{:S(2)}, u32[]{:S(2)}) async-start(bf16[16,96,128]{2,1,0:T(8,128)(2,1)} %shard_map.69), calls=%async_computation.2 | async-start | bytes 786432 | tf_op jit(solution)/shard_map/all_to_all | solution.py:400
  49.9 0.8 copy-start.3
  50.7 1.0 %copy-start.2 = (bf16[256,768]{1,0:T(8,128)(2,1)S(1)}, bf16[256,768]{1,0:T(8,128)(2,1)}, u32[]{:S(2)}) copy-start(bf16[256,768]{1,0:T(8,128)(2,1)} %copy-done.1) | copy-start | bytes 1179652
  51.7 1.0 %copy-start.4 = (bf16[256,768]{1,0:T(8,128)(2,1)S(1)}, bf16[256,768]{1,0:T(8,128)(2,1)}, u32[]{:S(2)}) copy-start(bf16[256,768]{1,0:T(8,128)(2,1)} %copy-done.3) | copy-start | bytes 1179652
  57.4 1.2 %copy-start = (bf16[1024,768]{1,0:T(8,128)(2,1)}, bf16[1024,768]{1,0:T(8,128)(2,1)S(1)}, u32[]{:S(2)}) copy-start(bf16[1024,768]{1,0:T(8,128)(2,1)S(1)} %get-tuple-element.16.left_far) | copy-start | bytes 4718596
  66.8 1.9 %collective-permute-start.10 = (bf16[384,384]{1,0:T(8,128)(2,1)S(1)}, bf16[384,384]{1,0:T(8,128)(2,1)S(1)}, u32[]{:S(2)}, u32[]{:S(2)}) collective-permute-start(bf16[384,384]{1,0:T(8,128)(2,1)S(1)} %get-tuple-element.21), channel_id=1, source_target_pairs={{0,1},{1,0},{2,3},{3,2},{4,5},{5,4},{6,7},{7,6},{8,9},{9,8},{10,11... | collective-permute-start | bytes 884744 | tf_op jit(solution)/shard_map/ppermute | solution.py:439
  66.9 1.9 %collective-permute-start.9 = (bf16[128,768]{1,0:T(8,128)(2,1)S(1)}, bf16[128,768]{1,0:T(8,128)(2,1)S(1)}, u32[]{:S(2)}, u32[]{:S(2)}) collective-permute-start(bf16[128,768]{1,0:T(8,128)(2,1)S(1)} %get-tuple-element.18), channel_id=1, source_target_pairs={{0,1},{1,0},{2,3},{3,2},{4,5},{5,4},{6,7},{7,6},{8,9},{9,8},{10,11... | collective-permute-start | bytes 589832 | tf_op jit(solution)/shard_map/ppermute | solution.py:439

commit v8 on v7

--- a/solution.py
+++ b/solution.py
@@ -91,39 +91,57 @@
     return source * inverse, inverse
 
 
+def arrange_kernel(
+    features, grad_out, weights, start, end, send, heads_in, heads_out, bounds, arrived, start_here,
+    end_here, sems
+):
+    rows, cols, width = features.shape
+    half = width // CORES
+    _, core, _ = position()
+    copies = [
+        pltpu.make_async_copy(features, arrived.at[0], sems.at[0]),
+        pltpu.make_async_copy(grad_out, arrived.at[1], sems.at[1]),
+        pltpu.make_async_copy(start, start_here, sems.at[2]),
+        pltpu.make_async_copy(end, end_here, sems.at[3]),
+        pltpu.make_async_copy(
+            weights.at[pl.ds(0, 3), :, head_lanes(core, half)], heads_in, sems.at[4]
+        ),
+        pltpu.make_async_copy(weights.at[3, head_lanes(core, half), :], heads_out, sems.at[5]),
+    ]
+    for copy in copies:
+        copy.start()
+    cells = rows * cols
+
+    def place(at, spot):
+        return spot == lax.rem(at, 2 * rows) * cols + lax.div(at, 2 * rows)
+
+    order = indicator(2 * cells, 2 * cells, place)
+    copies[0].wait()
+    copies[1].wait()
+    send[...] = dot(order, arrived[...].reshape(2 * cells, width)).astype(BF16)
+    copies[2].wait()
+    copies[3].wait()
+    first, last = upright(start_here[...]), upright(end_here[...])
+    lane = lax.broadcasted_iota(jnp.int32, bounds.shape, 1)
+    bounds[...] = jnp.where(lane == 0, first, last)
+    copies[4].wait()
+    copies[5].wait()
+
+
 def project_kernel(
-    own, other, weights, start, end, proj, tied, normed_own, bounds, heads_in, heads_out,
-    start_here, end_here, sems, *, rows, col_dev
+    own, other, heads_in, heads_out, bounds, proj, tied, normed_own, scales, *, rows, col_dev
 ):
     cells = own.shape[0] // 2
     half = own.shape[1] // CORES
-    me, core, _ = position()
+    me, _, _ = position()
     first_col = lax.axis_index("pos") * col_dev
-    copies = [
-        pltpu.make_async_copy(start, start_here, sems.at[0]),
-        pltpu.make_async_copy(end, end_here, sems.at[1]),
-    ]
-    for at in range(3):
-        copies.append(
-            pltpu.make_async_copy(
-                weights.at[at, :, head_lanes(core, half)], heads_in.at[at], sems.at[2 + at]
-            )
-        )
-    copies.append(
-        pltpu.make_async_copy(weights.at[3, head_lanes(core, half), :], heads_out, sems.at[5])
-    )
-    for copy in copies:
-        copy.start()
-
     source, upstream = part_rows([own[...], other[...]], rows, cells)
     normed32, inverse = normalise(source)
     normed = normed32.astype(BF16)
     normed_own[...] = normed32[:cells]
-    copies[0].wait()
-    copies[1].wait()
-    first, last = upright(start_here[...]), upright(end_here[...])
-    lane = lax.broadcasted_iota(jnp.int32, bounds.shape, 1)
-    bounds[...] = jnp.where(lane == 0, first, jnp.where(lane == 1, last, inverse[:cells]))
+    first, last = bounds[:, 0:1], bounds[:, 1:2]
+    lane = lax.broadcasted_iota(jnp.int32, scales.shape, 1)
+    scales[...] = jnp.where(lane == 0, first, jnp.where(lane == 1, last, inverse[:cells]))
     covered = jnp.concatenate(
         [
             row_mask(first, last, first_col + me),
@@ -131,13 +149,9 @@
         ],
         axis=0,
     )
-    copies[2].wait()
     query = (dot(normed, heads_in[0]) * covered).astype(BF16)
-    copies[3].wait()
     keys = (dot(normed, heads_in[1]) * covered).astype(BF16)
-    copies[4].wait()
     values = (dot(normed, heads_in[2]) * covered).astype(BF16)
-    copies[5].wait()
     back_out = dot(upstream, heads_out[...], (1, 1)).astype(BF16)
     proj[0] = keys
     proj[1] = query
@@ -439,27 +453,36 @@
         return lax.ppermute(array, "read", [(i, i ^ bits) for i in range(count)])
 
     shape = jax.ShapeDtypeStruct
-    send = jnp.stack([features, grad_out]).transpose(2, 0, 1, 3).reshape(-1, width)
-    own = exchange(send, None)
+    send, heads_in, heads_out, bounds = call(
+        arrange_kernel,
+        (features, grad_out, weights, start, end),
+        (
+            shape((2 * reads, width), BF16),
+            shape((3, width, half), BF16),
+            shape((half, width), BF16),
+            shape((reads, LANES), F32),
+        ),
+        8,
+        (0, 1, 2, 3, 4),
+        [
+            pltpu.VMEM((2, *features.shape), BF16),
+            pltpu.VMEM((1, reads), jnp.int32),
+            pltpu.VMEM((1, reads), jnp.int32),
+            pltpu.SemaphoreType.DMA((6,)),
+        ],
+    )
+    own = exchange(send.reshape(count, 2 * rows, width), None).reshape(send.shape)
     other = swap(own, 1)
     proj, tied, normed, bounds = call(
         functools.partial(project_kernel, rows=rows, col_dev=col_dev),
-        (own, other, weights, start, end),
+        (own, other, heads_in, heads_out, bounds),
         (
             shape((KINDS - 1, 2 * reads, half), BF16),
             shape((chips, tied_rows, reads), BF16),
             shape((reads, width), F32),
             shape((reads, LANES), F32),
         ),
-        20,
-        (2, 3, 4),
-        [
-            pltpu.VMEM((3, width, half), BF16),
-            pltpu.VMEM((half, width), BF16),
-            pltpu.VMEM((1, reads), jnp.int32),
-            pltpu.VMEM((1, reads), jnp.int32),
-            pltpu.SemaphoreType.DMA((6,)),
-        ],
+        16,
     )
 
     parts = exchange(tied, same_core)

time: 94.3 us -> 93.6 us (level)
  other arithmetic: 1.06 us -> 0 us
    ppermute x11, starting transfers between devices: 5.04 us -> 6.32 us  [swap(): return lax.ppermute(array, 'read', [(i, i ^ bits) for i in range(count)])]
    all_to_all x2, waiting for transfers between devices: 5.57 us -> 4.47 us  [exchange(): lax.all_to_all(array, 'read', split_axis=0, concat_axis=0, tiled=True, ax...]
    another operation x1 -> x0, other arithmetic: 1.06 us -> none  [shards(): jnp.stack([features, grad_out]).transpose(2, 0, 1, 3).reshape(-1, width)]
    pallas_call x6 -> x7, Pallas kernels: 15.6 us -> 15.9 us  [call(): pl.pallas_call(kernel, in_specs=[away if at in far else near for at in ra...]
  transfers between devices with their start and end apart: 13 -> 13, of which waited for: 7 -> 6; matrix products, arithmetic and copies ran while one was open for 0% -> 0% of each run, Pallas kernels for 10% -> 9%
where the time goes in v8:
time: 93.6 us; the launch traced here: 93 us
  blocking collectives  43.3 us (46%)
  Pallas kernels  15.9 us (17%)
  waiting for transfers between devices  15.3 us (16%)
  starting transfers between devices  13.8 us (15%)
  local copies, waits for them, and re-layouts  3.94 us (4%)
    all_to_all x2, blocking collectives, exchange(): lax.all_to_all(array, 'read', split_axis=0, concat_axis=0, tiled=True, ax...  43.3 us
    pallas_call x7, Pallas kernels, call(): pl.pallas_call(kernel, in_specs=[away if at in far else near for at in ra...  15.9 us
    ppermute x11, waiting for transfers between devices, swap(): return lax.ppermute(array, 'read', [(i, i ^ bits) for i in range(count)])  10.8 us
    all_to_all x2, starting transfers between devices, exchange(): lax.all_to_all(array, 'read', split_axis=0, concat_axis=0, tiled=True, ax...  7.47 us
    ppermute x11, starting transfers between devices, swap(): return lax.ppermute(array, 'read', [(i, i ^ bits) for i in range(count)])  6.32 us
    all_to_all x2, waiting for transfers between devices, exchange(): lax.all_to_all(array, 'read', split_axis=0, concat_axis=0, tiled=True, ax...  4.47 us
    unnamed x10, local copies, waits for them, and re-layouts  3.92 us
  transfers between devices with their start and end apart: 13, of which 6 were waited for; matrix products, arithmetic and copies ran while one was open for 0% of the time, Pallas kernels for 9%

profile of v8, /device:TPU:0, one launch (start us, length us, event | category | flops | bytes accessed | tf_op | source)
XLA Modules:
  0.0 93.0 jit_solution(13399694903594240839)
XLA Ops:
  0.6 1.9 %shard_map.68 = (bf16[256,768]{1,0:T(8,128)(2,1)S(1)}, bf16[3,768,384]{2,1,0:T(8,128)(2,1)S(1)}, bf16[384,768]{1,0:T(8,128)(2,1)S(1)}, f32[128,128]{1,0:T(8,128)S(1)}) custom-call(bf16[4,32,768]{2,1,0:T(8,128)(2,1)} %features.1, bf16[4,32,768]{2,1,0:T(8,128)(2,1)} %grad_out.1, bf16[4,768,768]{2,1,0:T(8,128)(2,1)} %weights.5, s32[1,128]{1,0:T(1,128)} %bitcast.12, ...), custom_call_target="tpu_custom_call" | custom-call | tf_op jit(solution)/shard_map/pallas_call | solution.py:425
  2.5 20.3 %all_to_all.20 = bf16[32,8,768]{2,1,0:T(8,128)(2,1)S(1)} all-to-all(bf16[32,8,768]{2,1,0:T(8,128)(2,1)S(1)} %bitcast.11), channel_id=1, replica_groups=mesh['read'=32,'pos'=1] {'read'}, dimensions={0} | all-to-all | bytes 786432 | tf_op jit(solution)/shard_map/all_to_all | solution.py:414
  22.8 0.0 collective-permute-start
  22.8 1.0 %collective-permute-start.1 = (bf16[256,768]{1,0:T(8,128)(2,1)S(1)}, bf16[256,768]{1,0:T(8,128)(2,1)S(1)}, u32[]{:S(2)}, u32[]{:S(2)}) collective-permute-start(bf16[256,768]{1,0:T(8,128)(2,1)S(1)} %bitcast.7), channel_id=1, source_target_pairs={{0,2},{1,3},{2,0},{3,1},{4,6},{5,7},{6,4},{7,5},{8,10},{9,11},{10,... | collective-permute-start | bytes 1179656 | tf_op jit(solution)/shard_map/ppermute | solution.py:453
  23.8 1.0 %collective-permute-start.3 = (bf16[256,768]{1,0:T(8,128)(2,1)S(1)}, bf16[256,768]{1,0:T(8,128)(2,1)S(1)}, u32[]{:S(2)}, u32[]{:S(2)}) collective-permute-start(bf16[256,768]{1,0:T(8,128)(2,1)S(1)} %bitcast.8), channel_id=1, source_target_pairs={{0,4},{1,5},{2,6},{3,7},{4,0},{5,1},{6,2},{7,3},{8,12},{9,13},{10,... | collective-permute-start | bytes 1179656 | tf_op jit(solution)/shard_map/ppermute | solution.py:453
  24.8 0.0 collective-permute-done.other.refs_1_
  24.8 2.4 %shard_map.69 = (bf16[3,256,384]{2,1,0:T(8,128)(2,1)S(1)}, bf16[16,96,128]{2,1,0:T(8,128)(2,1)}, f32[128,768]{1,0:T(8,128)S(1)}, f32[128,128]{1,0:T(8,128)S(1)}) custom-call(bf16[256,768]{1,0:T(8,128)(2,1)S(1)} %bitcast.9, bf16[256,768]{1,0:T(8,128)(2,1)S(1)} %collective-permute-done.other.refs_1_, bf16[3,768,384]{2,1,0:T(8,128)(2,1)S(1)} %get-tuple-element.17.heads_in, ...), custom_call_target="tpu_custom_call" | custom-call | tf_op jit(solution)/shard_map/pallas_call | solution.py:425
  27.2 3.6 %all-to-all-start.1 = ((bf16[16,96,128]{2,1,0:T(8,128)(2,1)}), bf16[16,96,128]{2,1,0:T(8,128)(2,1)S(1)}, u32[]{:S(2)}, u32[]{:S(2)}) async-start(bf16[16,96,128]{2,1,0:T(8,128)(2,1)} %get-tuple-element.20), calls=%async_computation.1 | async-start | bytes 786432 | tf_op jit(solution)/shard_map/all_to_all | solution.py:414
  30.7 4.0 %collective-permute-done.1.refs_2_ = bf16[256,768]{1,0:T(8,128)(2,1)S(1)} collective-permute-done((bf16[256,768]{1,0:T(8,128)(2,1)S(1)}, bf16[256,768]{1,0:T(8,128)(2,1)S(1)}, u32[]{:S(2)}, u32[]{:S(2)}) %collective-permute-start.1) | collective-permute-done | bytes 393248 | tf_op jit(solution)/shard_map/ppermute | solution.py:453
  34.8 1.0 %collective-permute-start.5 = (bf16[128,768]{1,0:T(8,128)(2,1)S(1)}, bf16[128,768]{1,0:T(8,128)(2,1)}, u32[]{:S(2)}, u32[]{:S(2)}) collective-permute-start(bf16[128,768]{1,0:T(8,128)(2,1)S(1)} %slice.8), channel_id=1, source_target_pairs={{0,4},{1,5},{2,6},{3,7},{4,0},{5,1},{6,2},{7,3},{8,12},{9,13},{10,... | collective-permute-start | bytes 589832 | tf_op jit(solution)/shard_map/ppermute | solution.py:453
  35.8 0.6 collective-permute-done.3.refs_4_
  36.4 0.0 copy-start.1
  36.4 2.2 %collective-permute-start.6 = (bf16[128,768]{1,0:T(8,128)(2,1)S(1)}, bf16[128,768]{1,0:T(8,128)(2,1)}, u32[]{:S(2)}, u32[]{:S(2)}) collective-permute-start(bf16[128,768]{1,0:T(8,128)(2,1)S(1)} %slice.9), channel_id=1, source_target_pairs={{0,2},{1,3},{2,0},{3,1},{4,6},{5,7},{6,4},{7,5},{8,10},{9,11},{10,... | collective-permute-start | bytes 589832 | tf_op jit(solution)/shard_map/ppermute | solution.py:453
  38.6 0.0 collective-permute-start.2
  38.6 0.5 collective-permute-start.4
  39.1 3.8 %collective-permute-done.5.refs_6_ = bf16[128,768]{1,0:T(8,128)(2,1)} collective-permute-done((bf16[128,768]{1,0:T(8,128)(2,1)S(1)}, bf16[128,768]{1,0:T(8,128)(2,1)}, u32[]{:S(2)}, u32[]{:S(2)}) %collective-permute-start.5) | collective-permute-done | bytes 196640 | tf_op jit(solution)/shard_map/ppermute | solution.py:453
  42.9 0.0 collective-permute-start.7
  42.9 1.1 %collective-permute-done.6.refs_7_ = bf16[128,768]{1,0:T(8,128)(2,1)} collective-permute-done((bf16[128,768]{1,0:T(8,128)(2,1)S(1)}, bf16[128,768]{1,0:T(8,128)(2,1)}, u32[]{:S(2)}, u32[]{:S(2)}) %collective-permute-start.6) | collective-permute-done | bytes 196640 | tf_op jit(solution)/shard_map/ppermute | solution.py:453
  44.0 0.0 collective-permute-start.8
  44.0 0.0 all-to-all-done.1.parts
  44.0 1.0 %shard_map.70 = bf16[16,96,128]{2,1,0:T(8,128)(2,1)} custom-call(bf16[16,96,128]{2,1,0:T(8,128)(2,1)S(1)} %all-to-all-done.1.parts), custom_call_target="tpu_custom_call" | custom-call | tf_op jit(solution)/shard_map/pallas_call | solution.py:425
  45.0 3.9 %all-to-all-start.2 = ((bf16[16,96,128]{2,1,0:T(8,128)(2,1)}), bf16[16,96,128]{2,1,0:T(8,128)(2,1)S(1)}, u32[]{:S(2)}, u32[]{:S(2)}) async-start(bf16[16,96,128]{2,1,0:T(8,128)(2,1)} %shard_map.70), calls=%async_computation.2 | async-start | bytes 786432 | tf_op jit(solution)/shard_map/all_to_all | solution.py:414
  48.9 0.0 collective-permute-done.7.refs_8_
  48.9 0.0 collective-permute-done.8.refs_9_
  49.0 0.0 collective-permute-done.2.refs_3_
  49.0 0.0 copy-start.3
  49.0 0.8 copy-done.3
  49.7 0.0 collective-permute-done.4.refs_5_
  49.7 0.0 copy-done.1
  49.8 0.0 copy-start.2
  49.8 1.0 %copy-done.2 = bf16[256,768]{1,0:T(8,128)(2,1)S(1)} copy-done((bf16[256,768]{1,0:T(8,128)(2,1)S(1)}, bf16[256,768]{1,0:T(8,128)(2,1)}, u32[]{:S(2)}) %copy-start.2) | copy-done | bytes 393240
  50.7 0.0 copy-start.4
  50.8 1.0 %copy-done.4 = bf16[256,768]{1,0:T(8,128)(2,1)S(1)} copy-done((bf16[256,768]{1,0:T(8,128)(2,1)S(1)}, bf16[256,768]{1,0:T(8,128)(2,1)}, u32[]{:S(2)}) %copy-start.4) | copy-done | bytes 393240
  51.7 4.7 %shard_map.71 = (bf16[1024,768]{1,0:T(8,128)(2,1)S(1)}, bf16[1024,384]{1,0:T(8,128)(2,1)S(1)}) custom-call(bf16[4,768,768]{2,1,0:T(8,128)(2,1)} %weights.5, f32[128,128]{1,0:T(8,128)S(1)} %get-tuple-element.22.bounds, bf16[256,768]{1,0:T(8,128)(2,1)S(1)} %bitcast.10, bf16[256,768]{1,0:T(8,128)(2,1)S(1)} %collective-permute-done.other.refs_1_, ...), custom_call_target="tpu_custom_call" | custom-call | flops 16000000000 | bytes 8388608 | tf_op jit(solution)/shard_map/pallas_call | solution.py:425
  56.5 0.0 copy-start
  56.5 1.2 %copy-done = bf16[1024,768]{1,0:T(8,128)(2,1)} copy-done((bf16[1024,768]{1,0:T(8,128)(2,1)}, bf16[1024,768]{1,0:T(8,128)(2,1)S(1)}, u32[]{:S(2)}) %copy-start) | copy-done | bytes 1572888
  57.6 4.5 %all-to-all-done.2.pairs = bf16[16,96,128]{2,1,0:T(8,128)(2,1)S(1)} async-done(((bf16[16,96,128]{2,1,0:T(8,128)(2,1)}), bf16[16,96,128]{2,1,0:T(8,128)(2,1)S(1)}, u32[]{:S(2)}, u32[]{:S(2)}) %all-to-all-start.2) | async-done | bytes 393248 | tf_op jit(solution)/shard_map/all_to_all | solution.py:414
  62.1 4.0 %shard_map.72 = (f32[128,768]{1,0:T(8,128)S(1)}, bf16[128,768]{1,0:T(8,128)(2,1)S(1)}, bf16[768,384]{1,0:T(8,128)(2,1)S(1)}, bf16[384,384]{1,0:T(8,128)(2,1)S(1)}) custom-call(bf16[16,96,128]{2,1,0:T(8,128)(2,1)S(1)} %all-to-all-done.2.pairs, bf16[3,256,384]{2,1,0:T(8,128)(2,1)S(1)} %get-tuple-element.21.proj, f32[128,128]{1,0:T(8,128)S(1)} %get-tuple-element.22.bounds, ...), custom_call_target="tpu_custom_call" | custom-call | tf_op jit(solution)/shard_map/pallas_call | solution.py:425
  66.1 0.1 collective-permute-start.10
  66.2 0.5 collective-permute-start.9
  66.7 1.4 %collective-permute-done.9.grad_recv = bf16[128,768]{1,0:T(8,128)(2,1)S(1)} collective-permute-done((bf16[128,768]{1,0:T(8,128)(2,1)S(1)}, bf16[128,768]{1,0:T(8,128)(2,1)S(1)}, u32[]{:S(2)}, u32[]{:S(2)}) %collective-permute-start.9) | collective-permute-done | bytes 196640 | tf_op jit(solution)/shard_map/ppermute | solution.py:453
  68.0 0.0 collective-permute-done.10.spare
  68.0 0.7 shard_map.73
  68.7 23.0 %all_to_all.21.arrived = bf16[32,24,512]{2,1,0:T(8,128)(2,1)S(1)} all-to-all(bf16[32,24,512]{2,1,0:T(8,128)(2,1)S(1)} %bitcast.5), channel_id=1, replica_groups=mesh['read'=32,'pos'=1] {'read'}, dimensions={0} | all-to-all | bytes 1572864 | tf_op jit(solution)/shard_map/all_to_all | solution.py:414
  91.8 1.3 %shard_map.74 = (bf16[4,32,768]{2,1,0:T(8,128)(2,1)}, f32[24,3072]{1,0:T(8,128)}) custom-call(bf16[32,24,512]{2,1,0:T(8,128)(2,1)S(1)} %all_to_all.21.arrived), custom_call_target="tpu_custom_call" | custom-call | tf_op jit(solution)/shard_map/pallas_call | solution.py:425
  (2 shorter events, 0.0 us)
Async XLA Ops:
  22.8 2.0 %collective-permute-start = (bf16[256,768]{1,0:T(8,128)(2,1)S(1)}, bf16[256,768]{1,0:T(8,128)(2,1)S(1)}, u32[]{:S(2)}, u32[]{:S(2)}) collective-permute-start(bf16[256,768]{1,0:T(8,128)(2,1)S(1)} %bitcast.6), channel_id=1, source_target_pairs={{0,1},{1,0},{2,3},{3,2},{4,5},{5,4},{6,7},{7,6},{8,9},{9,8},{10,11... | collective-permute-start | bytes 1179656 | tf_op jit(solution)/shard_map/ppermute | solution.py:453
  22.8 11.9 %collective-permute-start.1 = (bf16[256,768]{1,0:T(8,128)(2,1)S(1)}, bf16[256,768]{1,0:T(8,128)(2,1)S(1)}, u32[]{:S(2)}, u32[]{:S(2)}) collective-permute-start(bf16[256,768]{1,0:T(8,128)(2,1)S(1)} %bitcast.7), channel_id=1, source_target_pairs={{0,2},{1,3},{2,0},{3,1},{4,6},{5,7},{6,4},{7,5},{8,10},{9,11},{10,... | collective-permute-start | bytes 1179656 | tf_op jit(solution)/shard_map/ppermute | solution.py:453
  23.8 12.6 %collective-permute-start.3 = (bf16[256,768]{1,0:T(8,128)(2,1)S(1)}, bf16[256,768]{1,0:T(8,128)(2,1)S(1)}, u32[]{:S(2)}, u32[]{:S(2)}) collective-permute-start(bf16[256,768]{1,0:T(8,128)(2,1)S(1)} %bitcast.8), channel_id=1, source_target_pairs={{0,4},{1,5},{2,6},{3,7},{4,0},{5,1},{6,2},{7,3},{8,12},{9,13},{10,... | collective-permute-start | bytes 1179656 | tf_op jit(solution)/shard_map/ppermute | solution.py:453
  27.2 16.8 %all-to-all-start.1 = ((bf16[16,96,128]{2,1,0:T(8,128)(2,1)}), bf16[16,96,128]{2,1,0:T(8,128)(2,1)S(1)}, u32[]{:S(2)}, u32[]{:S(2)}) async-start(bf16[16,96,128]{2,1,0:T(8,128)(2,1)} %get-tuple-element.20), calls=%async_computation.1 | async-start | bytes 786432 | tf_op jit(solution)/shard_map/all_to_all | solution.py:414
  34.8 8.1 %collective-permute-start.5 = (bf16[128,768]{1,0:T(8,128)(2,1)S(1)}, bf16[128,768]{1,0:T(8,128)(2,1)}, u32[]{:S(2)}, u32[]{:S(2)}) collective-permute-start(bf16[128,768]{1,0:T(8,128)(2,1)S(1)} %slice.8), channel_id=1, source_target_pairs={{0,4},{1,5},{2,6},{3,7},{4,0},{5,1},{6,2},{7,3},{8,12},{9,13},{10,... | collective-permute-start | bytes 589832 | tf_op jit(solution)/shard_map/ppermute | solution.py:453
  36.4 13.4 %copy-start.1 = (bf16[256,768]{1,0:T(8,128)(2,1)}, bf16[256,768]{1,0:T(8,128)(2,1)S(1)}, u32[]{:S(2)}) copy-start(bf16[256,768]{1,0:T(8,128)(2,1)S(1)} %collective-permute-done.3.refs_4_) | copy-start | bytes 1179652
  36.4 7.6 %collective-permute-start.6 = (bf16[128,768]{1,0:T(8,128)(2,1)S(1)}, bf16[128,768]{1,0:T(8,128)(2,1)}, u32[]{:S(2)}, u32[]{:S(2)}) collective-permute-start(bf16[128,768]{1,0:T(8,128)(2,1)S(1)} %slice.9), channel_id=1, source_target_pairs={{0,2},{1,3},{2,0},{3,1},{4,6},{5,7},{6,4},{7,5},{8,10},{9,11},{10,... | collective-permute-start | bytes 589832 | tf_op jit(solution)/shard_map/ppermute | solution.py:453
  38.6 10.3 %collective-permute-start.2 = (bf16[256,768]{1,0:T(8,128)(2,1)S(1)}, bf16[256,768]{1,0:T(8,128)(2,1)S(1)}, u32[]{:S(2)}, u32[]{:S(2)}) collective-permute-start(bf16[256,768]{1,0:T(8,128)(2,1)S(1)} %collective-permute-done.1.refs_2_), channel_id=1, source_target_pairs={{0,1},{1,0},{2,3},{3,2},{4,5},{5,4},{6,7},{7,6},{8,9},{9,8},{10,11... | collective-permute-start | bytes 1179656 | tf_op jit(solution)/shard_map/ppermute | solution.py:453
  38.6 11.1 %collective-permute-start.4 = (bf16[256,768]{1,0:T(8,128)(2,1)S(1)}, bf16[256,768]{1,0:T(8,128)(2,1)}, u32[]{:S(2)}, u32[]{:S(2)}) collective-permute-start(bf16[256,768]{1,0:T(8,128)(2,1)S(1)} %collective-permute-done.3.refs_4_), channel_id=1, source_target_pairs={{0,1},{1,0},{2,3},{3,2},{4,5},{5,4},{6,7},{7,6},{8,9},{9,8},{10,11... | collective-permute-start | bytes 1179656 | tf_op jit(solution)/shard_map/ppermute | solution.py:453
  42.9 6.0 %collective-permute-start.7 = (bf16[128,768]{1,0:T(8,128)(2,1)}, bf16[128,768]{1,0:T(8,128)(2,1)}, u32[]{:S(2)}, u32[]{:S(2)}) collective-permute-start(bf16[128,768]{1,0:T(8,128)(2,1)} %collective-permute-done.5.refs_6_), channel_id=1, source_target_pairs={{0,1},{1,0},{2,3},{3,2},{4,5},{5,4},{6,7},{7,6},{8,9},{9,8},{10,11... | collective-permute-start | bytes 589832 | tf_op jit(solution)/shard_map/ppermute | solution.py:453
  44.0 4.9 %collective-permute-start.8 = (bf16[128,768]{1,0:T(8,128)(2,1)}, bf16[128,768]{1,0:T(8,128)(2,1)}, u32[]{:S(2)}, u32[]{:S(2)}) collective-permute-start(bf16[128,768]{1,0:T(8,128)(2,1)} %collective-permute-done.6.refs_7_), channel_id=1, source_target_pairs={{0,1},{1,0},{2,3},{3,2},{4,5},{5,4},{6,7},{7,6},{8,9},{9,8},{10,11... | collective-permute-start | bytes 589832 | tf_op jit(solution)/shard_map/ppermute | solution.py:453
  45.0 17.1 %all-to-all-start.2 = ((bf16[16,96,128]{2,1,0:T(8,128)(2,1)}), bf16[16,96,128]{2,1,0:T(8,128)(2,1)S(1)}, u32[]{:S(2)}, u32[]{:S(2)}) async-start(bf16[16,96,128]{2,1,0:T(8,128)(2,1)} %shard_map.70), calls=%async_computation.2 | async-start | bytes 786432 | tf_op jit(solution)/shard_map/all_to_all | solution.py:414
  49.0 0.8 copy-start.3
  49.8 1.0 %copy-start.2 = (bf16[256,768]{1,0:T(8,128)(2,1)S(1)}, bf16[256,768]{1,0:T(8,128)(2,1)}, u32[]{:S(2)}) copy-start(bf16[256,768]{1,0:T(8,128)(2,1)} %copy-done.1) | copy-start | bytes 1179652
  50.7 1.0 %copy-start.4 = (bf16[256,768]{1,0:T(8,128)(2,1)S(1)}, bf16[256,768]{1,0:T(8,128)(2,1)}, u32[]{:S(2)}) copy-start(bf16[256,768]{1,0:T(8,128)(2,1)} %copy-done.3) | copy-start | bytes 1179652
  56.5 1.2 %copy-start = (bf16[1024,768]{1,0:T(8,128)(2,1)}, bf16[1024,768]{1,0:T(8,128)(2,1)S(1)}, u32[]{:S(2)}) copy-start(bf16[1024,768]{1,0:T(8,128)(2,1)S(1)} %get-tuple-element.24.left_far) | copy-start | bytes 4718596
  66.1 1.9 %collective-permute-start.10 = (bf16[384,384]{1,0:T(8,128)(2,1)S(1)}, bf16[384,384]{1,0:T(8,128)(2,1)S(1)}, u32[]{:S(2)}, u32[]{:S(2)}) collective-permute-start(bf16[384,384]{1,0:T(8,128)(2,1)S(1)} %get-tuple-element.29), channel_id=1, source_target_pairs={{0,1},{1,0},{2,3},{3,2},{4,5},{5,4},{6,7},{7,6},{8,9},{9,8},{10,11... | collective-permute-start | bytes 884744 | tf_op jit(solution)/shard_map/ppermute | solution.py:453
  66.2 1.9 %collective-permute-start.9 = (bf16[128,768]{1,0:T(8,128)(2,1)S(1)}, bf16[128,768]{1,0:T(8,128)(2,1)S(1)}, u32[]{:S(2)}, u32[]{:S(2)}) collective-permute-start(bf16[128,768]{1,0:T(8,128)(2,1)S(1)} %get-tuple-element.26), channel_id=1, source_target_pairs={{0,1},{1,0},{2,3},{3,2},{4,5},{5,4},{6,7},{7,6},{8,9},{9,8},{10,11... | collective-permute-start | bytes 589832 | tf_op jit(solution)/shard_map/ppermute | solution.py:453

commit v9 on v8

--- a/solution.py
+++ b/solution.py
@@ -16,6 +16,9 @@
 MIB = 1024 * 1024
 
 BF16 = jnp.bfloat16
+F16 = jnp.float16
+LOGIT_UNIT = 2.0
+SLOPE_UNIT = 1024.0
 F32 = jnp.float32
 
 
@@ -129,7 +132,8 @@
 
 
 def project_kernel(
-    own, other, heads_in, heads_out, bounds, proj, tied, normed_own, scales, *, rows, col_dev
+    own, other, heads_in, heads_out, bounds, proj, tied, normed_own, scales, *, rows, col_dev,
+    scale
 ):
     cells = own.shape[0] // 2
     half = own.shape[1] // CORES
@@ -171,13 +175,13 @@
             here = slice(odd * cells, (odd + 1) * cells)
             both = jnp.concatenate(
                 [
-                    logits[here].reshape(chips, part, cells),
-                    slopes[here].reshape(chips, part, cells),
+                    (logits[here] * (scale / LOGIT_UNIT)).reshape(chips, part, cells),
+                    (slopes[here] * (1.0 / SLOPE_UNIT)).reshape(chips, part, cells),
                 ],
                 axis=1,
             )
             spot = (2 * pair + odd) * 2 * part
-            tied[:, spot : spot + 2 * part, :] = both.astype(BF16)
+            tied[:, spot : spot + 2 * part, :] = both
 
 
 def operand_kernel(weights, bounds, *refs, rows, col_dev):
@@ -237,8 +241,8 @@
 def soften_kernel(parts, copies, *, scale, part):
     total = jnp.sum(parts[...].astype(F32), axis=0)
     blocks = total.reshape(-1, 2 * part, total.shape[-1])
-    logits = blocks[:, :part] * scale
-    slopes = blocks[:, part:]
+    logits = blocks[:, :part] * LOGIT_UNIT
+    slopes = blocks[:, part:] * SLOPE_UNIT
     expon = jnp.exp(logits)
     probs = expon / jnp.sum(expon, -1, keepdims=True)
     mixed = scale * probs * (slopes - jnp.sum(probs * slopes, -1, keepdims=True))
@@ -474,21 +478,22 @@
     own = exchange(send.reshape(count, 2 * rows, width), None).reshape(send.shape)
     other = swap(own, 1)
     proj, tied, normed, bounds = call(
-        functools.partial(project_kernel, rows=rows, col_dev=col_dev),
+        functools.partial(project_kernel, rows=rows, col_dev=col_dev, scale=scale),
         (own, other, heads_in, heads_out, bounds),
         (
             shape((KINDS - 1, 2 * reads, half), BF16),
-            shape((chips, tied_rows, reads), BF16),
+            shape((chips, tied_rows, reads), F32),
             shape((reads, width), F32),
             shape((reads, LANES), F32),
         ),
         16,
     )
 
-    parts = exchange(tied, same_core)
+    parts = exchange(tied.astype(F16), same_core)
     raw = {1: swap(own, CORES), 2: swap(own, 2 * CORES)}
+    parts = parts.astype(F32)
     if pos_count > 1:
-        parts = lax.psum(jnp.sum(parts.astype(F32), 0, keepdims=True), "pos")
+        parts = lax.psum(jnp.sum(parts, 0, keepdims=True), "pos")
     copies = call(
         functools.partial(soften_kernel, scale=scale, part=part),
         (parts,),
@@ -515,7 +520,7 @@
             pltpu.VMEM((half, width), BF16),
             pltpu.SemaphoreType.DMA,
         ],
-        pl.CostEstimate(flops=16 * 10**9, bytes_accessed=8 * MIB, transcendentals=0),
+        pl.CostEstimate(flops=40 * 10**9, bytes_accessed=8 * MIB, transcendentals=0),
     )
 
     grad_own, grad_other, product, spare = call(

time: 93.6 us -> 95 us (1.015)
  waiting for transfers between devices: 15.3 us -> 16.9 us
    ppermute x11, waiting for transfers between devices: 10.8 us -> 12.8 us  [swap(): return lax.ppermute(array, 'read', [(i, i ^ bits) for i in range(count)])]
  transfers between devices with their start and end apart: 13 -> 13, of which waited for: 6 -> 6; matrix products, arithmetic and copies ran while one was open for 0% -> 1% of each run, Pallas kernels for 9% -> 8%
where the time goes in v9:
time: 95 us; the launch traced here: 94.5 us
  blocking collectives  43.9 us (46%)
  waiting for transfers between devices  16.9 us (18%)
  Pallas kernels  15.2 us (16%)
  starting transfers between devices  12.9 us (14%)
  local copies, waits for them, and re-layouts  3.94 us (4%)
    all_to_all x2, blocking collectives, exchange(): lax.all_to_all(array, 'read', split_axis=0, concat_axis=0, tiled=True, ax...  43.9 us
    pallas_call x7, Pallas kernels, call(): pl.pallas_call(kernel, in_specs=[away if at in far else near for at in ra...  15.2 us
    ppermute x11, waiting for transfers between devices, swap(): return lax.ppermute(array, 'read', [(i, i ^ bits) for i in range(count)])  12.8 us
    all_to_all x2, starting transfers between devices, exchange(): lax.all_to_all(array, 'read', split_axis=0, concat_axis=0, tiled=True, ax...  7.1 us
    ppermute x11, starting transfers between devices, swap(): return lax.ppermute(array, 'read', [(i, i ^ bits) for i in range(count)])  5.78 us
    all_to_all x2, waiting for transfers between devices, exchange(): lax.all_to_all(array, 'read', split_axis=0, concat_axis=0, tiled=True, ax...  4.13 us
    unnamed x10, local copies, waits for them, and re-layouts  3.91 us
  transfers between devices with their start and end apart: 13, of which 6 were waited for; matrix products, arithmetic and copies ran while one was open for 1% of the time, Pallas kernels for 8%

profile of v9, /device:TPU:0, one launch (start us, length us, event | category | flops | bytes accessed | tf_op | source)
XLA Modules:
  0.0 94.5 jit_solution(14690242858365640194)
XLA Ops:
  0.6 1.9 %shard_map.68 = (bf16[256,768]{1,0:T(8,128)(2,1)S(1)}, bf16[3,768,384]{2,1,0:T(8,128)(2,1)S(1)}, bf16[384,768]{1,0:T(8,128)(2,1)S(1)}, f32[128,128]{1,0:T(8,128)S(1)}) custom-call(bf16[4,32,768]{2,1,0:T(8,128)(2,1)} %features.1, bf16[4,32,768]{2,1,0:T(8,128)(2,1)} %grad_out.1, bf16[4,768,768]{2,1,0:T(8,128)(2,1)} %weights.5, s32[1,128]{1,0:T(1,128)} %bitcast.12, ...), custom_call_target="tpu_custom_call" | custom-call | tf_op jit(solution)/shard_map/pallas_call | solution.py:429
  2.5 20.3 %all_to_all.20 = bf16[32,8,768]{2,1,0:T(8,128)(2,1)S(1)} all-to-all(bf16[32,8,768]{2,1,0:T(8,128)(2,1)S(1)} %bitcast.11), channel_id=1, replica_groups=mesh['read'=32,'pos'=1] {'read'}, dimensions={0} | all-to-all | bytes 786432 | tf_op jit(solution)/shard_map/all_to_all | solution.py:418
  22.8 0.0 collective-permute-start
  22.8 1.0 %collective-permute-start.1 = (bf16[256,768]{1,0:T(8,128)(2,1)S(1)}, bf16[256,768]{1,0:T(8,128)(2,1)S(1)}, u32[]{:S(2)}, u32[]{:S(2)}) collective-permute-start(bf16[256,768]{1,0:T(8,128)(2,1)S(1)} %bitcast.7), channel_id=1, source_target_pairs={{0,2},{1,3},{2,0},{3,1},{4,6},{5,7},{6,4},{7,5},{8,10},{9,11},{10,... | collective-permute-start | bytes 1179656 | tf_op jit(solution)/shard_map/ppermute | solution.py:457
  23.8 1.0 %collective-permute-start.3 = (bf16[256,768]{1,0:T(8,128)(2,1)S(1)}, bf16[256,768]{1,0:T(8,128)(2,1)S(1)}, u32[]{:S(2)}, u32[]{:S(2)}) collective-permute-start(bf16[256,768]{1,0:T(8,128)(2,1)S(1)} %bitcast.8), channel_id=1, source_target_pairs={{0,4},{1,5},{2,6},{3,7},{4,0},{5,1},{6,2},{7,3},{8,12},{9,13},{10,... | collective-permute-start | bytes 1179656 | tf_op jit(solution)/shard_map/ppermute | solution.py:457
  24.8 0.0 collective-permute-done.other.refs_1_
  24.8 1.6 %shard_map.69 = (bf16[3,256,384]{2,1,0:T(8,128)(2,1)S(1)}, f32[16,96,128]{2,1,0:T(8,128)S(1)}, f32[128,768]{1,0:T(8,128)S(1)}, f32[128,128]{1,0:T(8,128)S(1)}) custom-call(bf16[256,768]{1,0:T(8,128)(2,1)S(1)} %bitcast.9, bf16[256,768]{1,0:T(8,128)(2,1)S(1)} %collective-permute-done.other.refs_1_, bf16[3,768,384]{2,1,0:T(8,128)(2,1)S(1)} %get-tuple-element.17.heads_in, ...), custom_call_target="tpu_custom_call" | custom-call | tf_op jit(solution)/shard_map/pallas_call | solution.py:429
  26.4 0.8 convert_element_type.6
  27.2 3.6 %all-to-all-start.1 = ((f16[16,96,128]{2,1,0:T(8,128)(2,1)}), f16[16,96,128]{2,1,0:T(8,128)(2,1)S(1)}, u32[]{:S(2)}, u32[]{:S(2)}) async-start(f16[16,96,128]{2,1,0:T(8,128)(2,1)} %convert_element_type.6), calls=%async_computation.1 | async-start | bytes 786432 | tf_op jit(solution)/shard_map/all_to_all | solution.py:418
  30.8 3.9 %collective-permute-done.1.refs_2_ = bf16[256,768]{1,0:T(8,128)(2,1)S(1)} collective-permute-done((bf16[256,768]{1,0:T(8,128)(2,1)S(1)}, bf16[256,768]{1,0:T(8,128)(2,1)S(1)}, u32[]{:S(2)}, u32[]{:S(2)}) %collective-permute-start.1) | collective-permute-done | bytes 393248 | tf_op jit(solution)/shard_map/ppermute | solution.py:457
  34.7 1.1 %collective-permute-start.5 = (bf16[128,768]{1,0:T(8,128)(2,1)S(1)}, bf16[128,768]{1,0:T(8,128)(2,1)}, u32[]{:S(2)}, u32[]{:S(2)}) collective-permute-start(bf16[128,768]{1,0:T(8,128)(2,1)S(1)} %slice.8), channel_id=1, source_target_pairs={{0,4},{1,5},{2,6},{3,7},{4,0},{5,1},{6,2},{7,3},{8,12},{9,13},{10,... | collective-permute-start | bytes 589832 | tf_op jit(solution)/shard_map/ppermute | solution.py:457
  35.8 0.0 collective-permute-start.2
  35.8 0.6 collective-permute-done.3.refs_4_
  36.4 0.0 copy-start.1
  36.4 0.0 collective-permute-start.4
  36.4 2.2 %collective-permute-start.6 = (bf16[128,768]{1,0:T(8,128)(2,1)S(1)}, bf16[128,768]{1,0:T(8,128)(2,1)}, u32[]{:S(2)}, u32[]{:S(2)}) collective-permute-start(bf16[128,768]{1,0:T(8,128)(2,1)S(1)} %slice.9), channel_id=1, source_target_pairs={{0,2},{1,3},{2,0},{3,1},{4,6},{5,7},{6,4},{7,5},{8,10},{9,11},{10,... | collective-permute-start | bytes 589832 | tf_op jit(solution)/shard_map/ppermute | solution.py:457
  38.6 4.3 %collective-permute-done.5.refs_6_ = bf16[128,768]{1,0:T(8,128)(2,1)} collective-permute-done((bf16[128,768]{1,0:T(8,128)(2,1)S(1)}, bf16[128,768]{1,0:T(8,128)(2,1)}, u32[]{:S(2)}, u32[]{:S(2)}) %collective-permute-start.5) | collective-permute-done | bytes 196640 | tf_op jit(solution)/shard_map/ppermute | solution.py:457
  42.9 0.0 collective-permute-start.7
  42.9 2.6 %collective-permute-done.6.refs_7_ = bf16[128,768]{1,0:T(8,128)(2,1)} collective-permute-done((bf16[128,768]{1,0:T(8,128)(2,1)S(1)}, bf16[128,768]{1,0:T(8,128)(2,1)}, u32[]{:S(2)}, u32[]{:S(2)}) %collective-permute-start.6) | collective-permute-done | bytes 196640 | tf_op jit(solution)/shard_map/ppermute | solution.py:457
  45.5 0.0 collective-permute-start.8
  45.5 0.0 all-to-all-done.1
  45.5 0.1 convert_element_type.7.parts
  45.6 1.0 %shard_map.70 = bf16[16,96,128]{2,1,0:T(8,128)(2,1)} custom-call(f32[16,96,128]{2,1,0:T(8,128)S(1)} %convert_element_type.7.parts), custom_call_target="tpu_custom_call" | custom-call | tf_op jit(solution)/shard_map/pallas_call | solution.py:429
  46.5 0.0 copy-done.1
  46.5 3.6 %all-to-all-start.2 = ((bf16[16,96,128]{2,1,0:T(8,128)(2,1)}), bf16[16,96,128]{2,1,0:T(8,128)(2,1)S(1)}, u32[]{:S(2)}, u32[]{:S(2)}) async-start(bf16[16,96,128]{2,1,0:T(8,128)(2,1)} %shard_map.70), calls=%async_computation.2 | async-start | bytes 786432 | tf_op jit(solution)/shard_map/all_to_all | solution.py:418
  50.1 0.0 collective-permute-done.2.refs_3_
  50.1 0.0 copy-start.3
  50.1 0.8 copy-done.3
  50.9 0.0 collective-permute-done.4.refs_5_
  50.9 0.0 collective-permute-done.7.refs_8_
  50.9 0.0 collective-permute-done.8.refs_9_
  50.9 0.0 copy-start.2
  50.9 1.0 %copy-done.2 = bf16[256,768]{1,0:T(8,128)(2,1)S(1)} copy-done((bf16[256,768]{1,0:T(8,128)(2,1)S(1)}, bf16[256,768]{1,0:T(8,128)(2,1)}, u32[]{:S(2)}) %copy-start.2) | copy-done | bytes 393240
  51.9 0.0 copy-start.4
  51.9 1.0 %copy-done.4 = bf16[256,768]{1,0:T(8,128)(2,1)S(1)} copy-done((bf16[256,768]{1,0:T(8,128)(2,1)S(1)}, bf16[256,768]{1,0:T(8,128)(2,1)}, u32[]{:S(2)}) %copy-start.4) | copy-done | bytes 393240
  52.9 4.7 %shard_map.71 = (bf16[1024,768]{1,0:T(8,128)(2,1)S(1)}, bf16[1024,384]{1,0:T(8,128)(2,1)S(1)}) custom-call(bf16[4,768,768]{2,1,0:T(8,128)(2,1)} %weights.5, f32[128,128]{1,0:T(8,128)S(1)} %get-tuple-element.22.bounds, bf16[256,768]{1,0:T(8,128)(2,1)S(1)} %bitcast.10, bf16[256,768]{1,0:T(8,128)(2,1)S(1)} %collective-permute-done.other.refs_1_, ...), custom_call_target="tpu_custom_call" | custom-call | flops 40000000000 | bytes 8388608 | tf_op jit(solution)/shard_map/pallas_call | solution.py:429
  57.6 0.0 copy-start
  57.6 1.2 %copy-done = bf16[1024,768]{1,0:T(8,128)(2,1)} copy-done((bf16[1024,768]{1,0:T(8,128)(2,1)}, bf16[1024,768]{1,0:T(8,128)(2,1)S(1)}, u32[]{:S(2)}) %copy-start) | copy-done | bytes 1572888
  58.8 4.1 %all-to-all-done.2.pairs = bf16[16,96,128]{2,1,0:T(8,128)(2,1)S(1)} async-done(((bf16[16,96,128]{2,1,0:T(8,128)(2,1)}), bf16[16,96,128]{2,1,0:T(8,128)(2,1)S(1)}, u32[]{:S(2)}, u32[]{:S(2)}) %all-to-all-start.2) | async-done | bytes 393248 | tf_op jit(solution)/shard_map/all_to_all | solution.py:418
  62.9 4.0 %shard_map.72 = (f32[128,768]{1,0:T(8,128)S(1)}, bf16[128,768]{1,0:T(8,128)(2,1)S(1)}, bf16[768,384]{1,0:T(8,128)(2,1)S(1)}, bf16[384,384]{1,0:T(8,128)(2,1)S(1)}) custom-call(bf16[16,96,128]{2,1,0:T(8,128)(2,1)S(1)} %all-to-all-done.2.pairs, bf16[3,256,384]{2,1,0:T(8,128)(2,1)S(1)} %get-tuple-element.21.proj, f32[128,128]{1,0:T(8,128)S(1)} %get-tuple-element.22.bounds, ...), custom_call_target="tpu_custom_call" | custom-call | tf_op jit(solution)/shard_map/pallas_call | solution.py:429
  66.9 0.1 collective-permute-start.10
  67.0 0.5 collective-permute-start.9
  67.5 1.4 %collective-permute-done.9.grad_recv = bf16[128,768]{1,0:T(8,128)(2,1)S(1)} collective-permute-done((bf16[128,768]{1,0:T(8,128)(2,1)S(1)}, bf16[128,768]{1,0:T(8,128)(2,1)S(1)}, u32[]{:S(2)}, u32[]{:S(2)}) %collective-permute-start.9) | collective-permute-done | bytes 196640 | tf_op jit(solution)/shard_map/ppermute | solution.py:457
  68.9 0.0 collective-permute-done.10.spare
  68.9 0.7 shard_map.73
  69.6 23.7 %all_to_all.21.arrived = bf16[32,24,512]{2,1,0:T(8,128)(2,1)S(1)} all-to-all(bf16[32,24,512]{2,1,0:T(8,128)(2,1)S(1)} %bitcast.5), channel_id=1, replica_groups=mesh['read'=32,'pos'=1] {'read'}, dimensions={0} | all-to-all | bytes 1572864 | tf_op jit(solution)/shard_map/all_to_all | solution.py:418
  93.2 1.3 %shard_map.74 = (bf16[4,32,768]{2,1,0:T(8,128)(2,1)}, f32[24,3072]{1,0:T(8,128)}) custom-call(bf16[32,24,512]{2,1,0:T(8,128)(2,1)S(1)} %all_to_all.21.arrived), custom_call_target="tpu_custom_call" | custom-call | tf_op jit(solution)/shard_map/pallas_call | solution.py:429
  (2 shorter events, 0.0 us)
Async XLA Ops:
  22.8 2.0 %collective-permute-start = (bf16[256,768]{1,0:T(8,128)(2,1)S(1)}, bf16[256,768]{1,0:T(8,128)(2,1)S(1)}, u32[]{:S(2)}, u32[]{:S(2)}) collective-permute-start(bf16[256,768]{1,0:T(8,128)(2,1)S(1)} %bitcast.6), channel_id=1, source_target_pairs={{0,1},{1,0},{2,3},{3,2},{4,5},{5,4},{6,7},{7,6},{8,9},{9,8},{10,11... | collective-permute-start | bytes 1179656 | tf_op jit(solution)/shard_map/ppermute | solution.py:457
  22.8 11.9 %collective-permute-start.1 = (bf16[256,768]{1,0:T(8,128)(2,1)S(1)}, bf16[256,768]{1,0:T(8,128)(2,1)S(1)}, u32[]{:S(2)}, u32[]{:S(2)}) collective-permute-start(bf16[256,768]{1,0:T(8,128)(2,1)S(1)} %bitcast.7), channel_id=1, source_target_pairs={{0,2},{1,3},{2,0},{3,1},{4,6},{5,7},{6,4},{7,5},{8,10},{9,11},{10,... | collective-permute-start | bytes 1179656 | tf_op jit(solution)/shard_map/ppermute | solution.py:457
  23.8 12.6 %collective-permute-start.3 = (bf16[256,768]{1,0:T(8,128)(2,1)S(1)}, bf16[256,768]{1,0:T(8,128)(2,1)S(1)}, u32[]{:S(2)}, u32[]{:S(2)}) collective-permute-start(bf16[256,768]{1,0:T(8,128)(2,1)S(1)} %bitcast.8), channel_id=1, source_target_pairs={{0,4},{1,5},{2,6},{3,7},{4,0},{5,1},{6,2},{7,3},{8,12},{9,13},{10,... | collective-permute-start | bytes 1179656 | tf_op jit(solution)/shard_map/ppermute | solution.py:457
  27.2 18.2 %all-to-all-start.1 = ((f16[16,96,128]{2,1,0:T(8,128)(2,1)}), f16[16,96,128]{2,1,0:T(8,128)(2,1)S(1)}, u32[]{:S(2)}, u32[]{:S(2)}) async-start(f16[16,96,128]{2,1,0:T(8,128)(2,1)} %convert_element_type.6), calls=%async_computation.1 | async-start | bytes 786432 | tf_op jit(solution)/shard_map/all_to_all | solution.py:418
  34.7 8.2 %collective-permute-start.5 = (bf16[128,768]{1,0:T(8,128)(2,1)S(1)}, bf16[128,768]{1,0:T(8,128)(2,1)}, u32[]{:S(2)}, u32[]{:S(2)}) collective-permute-start(bf16[128,768]{1,0:T(8,128)(2,1)S(1)} %slice.8), channel_id=1, source_target_pairs={{0,4},{1,5},{2,6},{3,7},{4,0},{5,1},{6,2},{7,3},{8,12},{9,13},{10,... | collective-permute-start | bytes 589832 | tf_op jit(solution)/shard_map/ppermute | solution.py:457
  35.8 14.3 %collective-permute-start.2 = (bf16[256,768]{1,0:T(8,128)(2,1)S(1)}, bf16[256,768]{1,0:T(8,128)(2,1)S(1)}, u32[]{:S(2)}, u32[]{:S(2)}) collective-permute-start(bf16[256,768]{1,0:T(8,128)(2,1)S(1)} %collective-permute-done.1.refs_2_), channel_id=1, source_target_pairs={{0,1},{1,0},{2,3},{3,2},{4,5},{5,4},{6,7},{7,6},{8,9},{9,8},{10,11... | collective-permute-start | bytes 1179656 | tf_op jit(solution)/shard_map/ppermute | solution.py:457
  36.4 10.2 %copy-start.1 = (bf16[256,768]{1,0:T(8,128)(2,1)}, bf16[256,768]{1,0:T(8,128)(2,1)S(1)}, u32[]{:S(2)}) copy-start(bf16[256,768]{1,0:T(8,128)(2,1)S(1)} %collective-permute-done.3.refs_4_) | copy-start | bytes 1179652
  36.4 14.5 %collective-permute-start.4 = (bf16[256,768]{1,0:T(8,128)(2,1)S(1)}, bf16[256,768]{1,0:T(8,128)(2,1)}, u32[]{:S(2)}, u32[]{:S(2)}) collective-permute-start(bf16[256,768]{1,0:T(8,128)(2,1)S(1)} %collective-permute-done.3.refs_4_), channel_id=1, source_target_pairs={{0,1},{1,0},{2,3},{3,2},{4,5},{5,4},{6,7},{7,6},{8,9},{9,8},{10,11... | collective-permute-start | bytes 1179656 | tf_op jit(solution)/shard_map/ppermute | solution.py:457
  36.4 9.1 %collective-permute-start.6 = (bf16[128,768]{1,0:T(8,128)(2,1)S(1)}, bf16[128,768]{1,0:T(8,128)(2,1)}, u32[]{:S(2)}, u32[]{:S(2)}) collective-permute-start(bf16[128,768]{1,0:T(8,128)(2,1)S(1)} %slice.9), channel_id=1, source_target_pairs={{0,2},{1,3},{2,0},{3,1},{4,6},{5,7},{6,4},{7,5},{8,10},{9,11},{10,... | collective-permute-start | bytes 589832 | tf_op jit(solution)/shard_map/ppermute | solution.py:457
  42.9 8.0 %collective-permute-start.7 = (bf16[128,768]{1,0:T(8,128)(2,1)}, bf16[128,768]{1,0:T(8,128)(2,1)}, u32[]{:S(2)}, u32[]{:S(2)}) collective-permute-start(bf16[128,768]{1,0:T(8,128)(2,1)} %collective-permute-done.5.refs_6_), channel_id=1, source_target_pairs={{0,1},{1,0},{2,3},{3,2},{4,5},{5,4},{6,7},{7,6},{8,9},{9,8},{10,11... | collective-permute-start | bytes 589832 | tf_op jit(solution)/shard_map/ppermute | solution.py:457
  45.5 5.4 %collective-permute-start.8 = (bf16[128,768]{1,0:T(8,128)(2,1)}, bf16[128,768]{1,0:T(8,128)(2,1)}, u32[]{:S(2)}, u32[]{:S(2)}) collective-permute-start(bf16[128,768]{1,0:T(8,128)(2,1)} %collective-permute-done.6.refs_7_), channel_id=1, source_target_pairs={{0,1},{1,0},{2,3},{3,2},{4,5},{5,4},{6,7},{7,6},{8,9},{9,8},{10,11... | collective-permute-start | bytes 589832 | tf_op jit(solution)/shard_map/ppermute | solution.py:457
  46.5 16.4 %all-to-all-start.2 = ((bf16[16,96,128]{2,1,0:T(8,128)(2,1)}), bf16[16,96,128]{2,1,0:T(8,128)(2,1)S(1)}, u32[]{:S(2)}, u32[]{:S(2)}) async-start(bf16[16,96,128]{2,1,0:T(8,128)(2,1)} %shard_map.70), calls=%async_computation.2 | async-start | bytes 786432 | tf_op jit(solution)/shard_map/all_to_all | solution.py:418
  50.1 0.8 copy-start.3
  50.9 1.0 %copy-start.2 = (bf16[256,768]{1,0:T(8,128)(2,1)S(1)}, bf16[256,768]{1,0:T(8,128)(2,1)}, u32[]{:S(2)}) copy-start(bf16[256,768]{1,0:T(8,128)(2,1)} %copy-done.1) | copy-start | bytes 1179652
  51.9 1.0 %copy-start.4 = (bf16[256,768]{1,0:T(8,128)(2,1)S(1)}, bf16[256,768]{1,0:T(8,128)(2,1)}, u32[]{:S(2)}) copy-start(bf16[256,768]{1,0:T(8,128)(2,1)} %copy-done.3) | copy-start | bytes 1179652
  57.6 1.2 %copy-start = (bf16[1024,768]{1,0:T(8,128)(2,1)}, bf16[1024,768]{1,0:T(8,128)(2,1)S(1)}, u32[]{:S(2)}) copy-start(bf16[1024,768]{1,0:T(8,128)(2,1)S(1)} %get-tuple-element.24.left_far) | copy-start | bytes 4718596
  66.9 1.9 %collective-permute-start.10 = (bf16[384,384]{1,0:T(8,128)(2,1)S(1)}, bf16[384,384]{1,0:T(8,128)(2,1)S(1)}, u32[]{:S(2)}, u32[]{:S(2)}) collective-permute-start(bf16[384,384]{1,0:T(8,128)(2,1)S(1)} %get-tuple-element.29), channel_id=1, source_target_pairs={{0,1},{1,0},{2,3},{3,2},{4,5},{5,4},{6,7},{7,6},{8,9},{9,8},{10,11... | collective-permute-start | bytes 884744 | tf_op jit(solution)/shard_map/ppermute | solution.py:457
  67.0 1.9 %collective-permute-start.9 = (bf16[128,768]{1,0:T(8,128)(2,1)S(1)}, bf16[128,768]{1,0:T(8,128)(2,1)S(1)}, u32[]{:S(2)}, u32[]{:S(2)}) collective-permute-start(bf16[128,768]{1,0:T(8,128)(2,1)S(1)} %get-tuple-element.26), channel_id=1, source_target_pairs={{0,1},{1,0},{2,3},{3,2},{4,5},{5,4},{6,7},{7,6},{8,9},{9,8},{10,11... | collective-permute-start | bytes 589832 | tf_op jit(solution)/shard_map/ppermute | solution.py:457

commit v10 on v9

--- a/solution.py
+++ b/solution.py
@@ -182,6 +182,10 @@
             )
             spot = (2 * pair + odd) * 2 * part
             tied[:, spot : spot + 2 * part, :] = both
+
+
+def halve_kernel(rows, half, *, first):
+    half[...] = rows[first : first + half.shape[0]]
 
 
 def operand_kernel(weights, bounds, *refs, rows, col_dev):
@@ -491,9 +495,7 @@
 
     parts = exchange(tied.astype(F16), same_core)
     raw = {1: swap(own, CORES), 2: swap(own, 2 * CORES)}
-    parts = parts.astype(F32)
-    if pos_count > 1:
-        parts = lax.psum(jnp.sum(parts, 0, keepdims=True), "pos")
+    parts = lax.psum(jnp.sum(parts.astype(F32), 0, keepdims=True), "pos")
     copies = call(
         functools.partial(soften_kernel, scale=scale, part=part),
         (parts,),
@@ -502,7 +504,14 @@
     )
     held_bounds = bounds
     pairs = exchange(copies, same_core)
-    diagonal = [swap(raw[1][:reads], 2 * CORES), swap(raw[2][reads:], CORES)]
+    halves = call(
+        functools.partial(halve_kernel, first=0),
+        (raw[1],),
+        shape((reads, width), BF16),
+        4,
+        cost=pl.CostEstimate(flops=6 * 10**9, bytes_accessed=MIB, transcendentals=0),
+    )
+    diagonal = [swap(halves, 2 * CORES), swap(raw[2][reads:], CORES)]
 
     blocks = [own, other]
     for near in (raw[1], raw[2]):

time: 95 us -> 95 us (level)
    pallas_call x7 -> x8, Pallas kernels: 15.2 us -> 15.2 us  [call(): pl.pallas_call(kernel, in_specs=[away if at in far else near for at in ra...]
where the time goes in v10:
time: 95 us; the launch traced here: 94.5 us
  blocking collectives  43.9 us (46%)
  waiting for transfers between devices  17.7 us (19%)
  Pallas kernels  15.2 us (16%)
  starting transfers between devices  12.9 us (14%)
  local copies, waits for them, and re-layouts  3.1 us (3%)
    all_to_all x2, blocking collectives, exchange(): lax.all_to_all(array, 'read', split_axis=0, concat_axis=0, tiled=True, ax...  43.9 us
    pallas_call x8, Pallas kernels, call(): pl.pallas_call(kernel, in_specs=[away if at in far else near for at in ra...  15.2 us
    ppermute x11, waiting for transfers between devices, swap(): return lax.ppermute(array, 'read', [(i, i ^ bits) for i in range(count)])  12.8 us
    all_to_all x2, starting transfers between devices, exchange(): lax.all_to_all(array, 'read', split_axis=0, concat_axis=0, tiled=True, ax...  7.1 us
    ppermute x11, starting transfers between devices, swap(): return lax.ppermute(array, 'read', [(i, i ^ bits) for i in range(count)])  5.82 us
    all_to_all x2, waiting for transfers between devices, exchange(): lax.all_to_all(array, 'read', split_axis=0, concat_axis=0, tiled=True, ax...  4.93 us
    unnamed x10, local copies, waits for them, and re-layouts  3.09 us
  transfers between devices with their start and end apart: 13, of which 6 were waited for; matrix products, arithmetic and copies ran while one was open for 1% of the time, Pallas kernels for 8%

profile of v10, /device:TPU:0, one launch (start us, length us, event | category | flops | bytes accessed | tf_op | source)
XLA Modules:
  0.0 94.5 jit_solution(8510552649927415302)
XLA Ops:
  0.6 1.9 %shard_map.68 = (bf16[256,768]{1,0:T(8,128)(2,1)S(1)}, bf16[3,768,384]{2,1,0:T(8,128)(2,1)S(1)}, bf16[384,768]{1,0:T(8,128)(2,1)S(1)}, f32[128,128]{1,0:T(8,128)S(1)}) custom-call(bf16[4,32,768]{2,1,0:T(8,128)(2,1)} %features.1, bf16[4,32,768]{2,1,0:T(8,128)(2,1)} %grad_out.1, bf16[4,768,768]{2,1,0:T(8,128)(2,1)} %weights.5, s32[1,128]{1,0:T(1,128)} %bitcast.14, ...), custom_call_target="tpu_custom_call" | custom-call | tf_op jit(solution)/shard_map/pallas_call | solution.py:433
  2.5 20.3 %all_to_all.20 = bf16[32,8,768]{2,1,0:T(8,128)(2,1)S(1)} all-to-all(bf16[32,8,768]{2,1,0:T(8,128)(2,1)S(1)} %bitcast.12), channel_id=1, replica_groups=mesh['read'=32,'pos'=1] {'read'}, dimensions={0} | all-to-all | bytes 786432 | tf_op jit(solution)/shard_map/all_to_all | solution.py:422
  22.8 0.0 collective-permute-start
  22.8 1.0 %collective-permute-start.1 = (bf16[256,768]{1,0:T(8,128)(2,1)S(1)}, bf16[256,768]{1,0:T(8,128)(2,1)S(1)}, u32[]{:S(2)}, u32[]{:S(2)}) collective-permute-start(bf16[256,768]{1,0:T(8,128)(2,1)S(1)} %bitcast.8), channel_id=1, source_target_pairs={{0,2},{1,3},{2,0},{3,1},{4,6},{5,7},{6,4},{7,5},{8,10},{9,11},{10,... | collective-permute-start | bytes 1179656 | tf_op jit(solution)/shard_map/ppermute | solution.py:461
  23.8 1.0 %collective-permute-start.3 = (bf16[256,768]{1,0:T(8,128)(2,1)S(1)}, bf16[256,768]{1,0:T(8,128)(2,1)S(1)}, u32[]{:S(2)}, u32[]{:S(2)}) collective-permute-start(bf16[256,768]{1,0:T(8,128)(2,1)S(1)} %bitcast.9), channel_id=1, source_target_pairs={{0,4},{1,5},{2,6},{3,7},{4,0},{5,1},{6,2},{7,3},{8,12},{9,13},{10,... | collective-permute-start | bytes 1179656 | tf_op jit(solution)/shard_map/ppermute | solution.py:461
  24.8 0.0 collective-permute-done.other.refs_1_
  24.8 1.6 %shard_map.69 = (bf16[3,256,384]{2,1,0:T(8,128)(2,1)S(1)}, f32[16,96,128]{2,1,0:T(8,128)S(1)}, f32[128,768]{1,0:T(8,128)S(1)}, f32[128,128]{1,0:T(8,128)S(1)}) custom-call(bf16[256,768]{1,0:T(8,128)(2,1)S(1)} %bitcast.10, bf16[256,768]{1,0:T(8,128)(2,1)S(1)} %collective-permute-done.other.refs_1_, bf16[3,768,384]{2,1,0:T(8,128)(2,1)S(1)} %get-tuple-element.17.heads_in, ...), custom_call_target="tpu_custom_call" | custom-call | tf_op jit(solution)/shard_map/pallas_call | solution.py:433
  26.4 0.8 convert_element_type.6
  27.2 3.6 %all-to-all-start.1 = ((f16[16,96,128]{2,1,0:T(8,128)(2,1)}), f16[16,96,128]{2,1,0:T(8,128)(2,1)S(1)}, u32[]{:S(2)}, u32[]{:S(2)}) async-start(f16[16,96,128]{2,1,0:T(8,128)(2,1)} %convert_element_type.6), calls=%async_computation.1 | async-start | bytes 786432 | tf_op jit(solution)/shard_map/all_to_all | solution.py:422
  30.8 4.0 %collective-permute-done.1.rows.refs_2_ = bf16[256,768]{1,0:T(8,128)(2,1)S(1)} collective-permute-done((bf16[256,768]{1,0:T(8,128)(2,1)S(1)}, bf16[256,768]{1,0:T(8,128)(2,1)S(1)}, u32[]{:S(2)}, u32[]{:S(2)}) %collective-permute-start.1) | collective-permute-done | bytes 393248 | tf_op jit(solution)/shard_map/ppermute | solution.py:461
  34.7 0.0 copy-start.1
  34.7 1.1 %collective-permute-start.5 = (bf16[128,768]{1,0:T(8,128)(2,1)S(1)}, bf16[128,768]{1,0:T(8,128)(2,1)S(1)}, u32[]{:S(2)}, u32[]{:S(2)}) collective-permute-start(bf16[128,768]{1,0:T(8,128)(2,1)S(1)} %shard_map.71), channel_id=1, source_target_pairs={{0,4},{1,5},{2,6},{3,7},{4,0},{5,1},{6,2},{7,3},{8,12},{9,13},{10,... | collective-permute-start | bytes 589832 | tf_op jit(solution)/shard_map/ppermute | solution.py:461
  35.8 0.0 copy-done.1
  35.8 0.0 collective-permute-start.2
  35.8 0.6 collective-permute-done.3.refs_4_
  36.4 0.0 collective-permute-start.4
  36.4 2.2 %collective-permute-start.6 = (bf16[128,768]{1,0:T(8,128)(2,1)S(1)}, bf16[128,768]{1,0:T(8,128)(2,1)}, u32[]{:S(2)}, u32[]{:S(2)}) collective-permute-start(bf16[128,768]{1,0:T(8,128)(2,1)S(1)} %slice.4), channel_id=1, source_target_pairs={{0,2},{1,3},{2,0},{3,1},{4,6},{5,7},{6,4},{7,5},{8,10},{9,11},{10,... | collective-permute-start | bytes 589832 | tf_op jit(solution)/shard_map/ppermute | solution.py:461
  38.6 4.2 %collective-permute-done.5.refs_6_ = bf16[128,768]{1,0:T(8,128)(2,1)S(1)} collective-permute-done((bf16[128,768]{1,0:T(8,128)(2,1)S(1)}, bf16[128,768]{1,0:T(8,128)(2,1)S(1)}, u32[]{:S(2)}, u32[]{:S(2)}) %collective-permute-start.5) | collective-permute-done | bytes 196640 | tf_op jit(solution)/shard_map/ppermute | solution.py:461
  42.8 0.0 copy-start.3
  42.8 0.0 collective-permute-start.7
  42.8 2.7 %collective-permute-done.6.refs_7_ = bf16[128,768]{1,0:T(8,128)(2,1)} collective-permute-done((bf16[128,768]{1,0:T(8,128)(2,1)S(1)}, bf16[128,768]{1,0:T(8,128)(2,1)}, u32[]{:S(2)}, u32[]{:S(2)}) %collective-permute-start.6) | collective-permute-done | bytes 196640 | tf_op jit(solution)/shard_map/ppermute | solution.py:461
  45.5 0.0 collective-permute-start.8
  45.5 0.0 all-to-all-done.1
  45.5 0.1 convert_reduce_fusion
  45.6 0.9 %shard_map.70 = bf16[16,96,128]{2,1,0:T(8,128)(2,1)} custom-call(f32[1,96,128]{2,1,0:T(8,128)S(1)} %bitcast.13), custom_call_target="tpu_custom_call" | custom-call | tf_op jit(solution)/shard_map/pallas_call | solution.py:433
  46.5 3.6 %all-to-all-start.2 = ((bf16[16,96,128]{2,1,0:T(8,128)(2,1)}), bf16[16,96,128]{2,1,0:T(8,128)(2,1)S(1)}, u32[]{:S(2)}, u32[]{:S(2)}) async-start(bf16[16,96,128]{2,1,0:T(8,128)(2,1)} %shard_map.70), calls=%async_computation.2 | async-start | bytes 786432 | tf_op jit(solution)/shard_map/all_to_all | solution.py:422
  50.1 0.0 collective-permute-done.2.refs_3_
  50.1 0.0 collective-permute-done.4.refs_5_
  50.1 0.0 collective-permute-done.7.refs_8_
  50.1 0.0 collective-permute-done.8.refs_9_
  50.1 0.0 copy-done.3
  50.1 0.0 copy-start.2
  50.1 1.0 %copy-done.2 = bf16[256,768]{1,0:T(8,128)(2,1)S(1)} copy-done((bf16[256,768]{1,0:T(8,128)(2,1)S(1)}, bf16[256,768]{1,0:T(8,128)(2,1)}, u32[]{:S(2)}) %copy-start.2) | copy-done | bytes 393240
  51.1 0.0 copy-start.4
  51.1 0.9 copy-done.4
  52.0 4.7 %shard_map.72 = (bf16[1024,768]{1,0:T(8,128)(2,1)S(1)}, bf16[1024,384]{1,0:T(8,128)(2,1)S(1)}) custom-call(bf16[4,768,768]{2,1,0:T(8,128)(2,1)} %weights.5, f32[128,128]{1,0:T(8,128)S(1)} %get-tuple-element.22.bounds, bf16[256,768]{1,0:T(8,128)(2,1)S(1)} %bitcast.11, bf16[256,768]{1,0:T(8,128)(2,1)S(1)} %collective-permute-done.other.refs_1_, ...), custom_call_target="tpu_custom_call" | custom-call | flops 40000000000 | bytes 8388608 | tf_op jit(solution)/shard_map/pallas_call | solution.py:433
  56.8 0.0 copy-start
  56.8 1.2 %copy-done = bf16[1024,768]{1,0:T(8,128)(2,1)} copy-done((bf16[1024,768]{1,0:T(8,128)(2,1)}, bf16[1024,768]{1,0:T(8,128)(2,1)S(1)}, u32[]{:S(2)}) %copy-start) | copy-done | bytes 1572888
  57.9 4.9 %all-to-all-done.2.pairs = bf16[16,96,128]{2,1,0:T(8,128)(2,1)S(1)} async-done(((bf16[16,96,128]{2,1,0:T(8,128)(2,1)}), bf16[16,96,128]{2,1,0:T(8,128)(2,1)S(1)}, u32[]{:S(2)}, u32[]{:S(2)}) %all-to-all-start.2) | async-done | bytes 393248 | tf_op jit(solution)/shard_map/all_to_all | solution.py:422
  62.9 4.0 %shard_map.73 = (f32[128,768]{1,0:T(8,128)S(1)}, bf16[128,768]{1,0:T(8,128)(2,1)S(1)}, bf16[768,384]{1,0:T(8,128)(2,1)S(1)}, bf16[384,384]{1,0:T(8,128)(2,1)S(1)}) custom-call(bf16[16,96,128]{2,1,0:T(8,128)(2,1)S(1)} %all-to-all-done.2.pairs, bf16[3,256,384]{2,1,0:T(8,128)(2,1)S(1)} %get-tuple-element.21.proj, f32[128,128]{1,0:T(8,128)S(1)} %get-tuple-element.22.bounds, ...), custom_call_target="tpu_custom_call" | custom-call | tf_op jit(solution)/shard_map/pallas_call | solution.py:433
  66.9 0.1 collective-permute-start.10
  67.0 0.5 collective-permute-start.9
  67.5 1.4 %collective-permute-done.9.grad_recv = bf16[128,768]{1,0:T(8,128)(2,1)S(1)} collective-permute-done((bf16[128,768]{1,0:T(8,128)(2,1)S(1)}, bf16[128,768]{1,0:T(8,128)(2,1)S(1)}, u32[]{:S(2)}, u32[]{:S(2)}) %collective-permute-start.9) | collective-permute-done | bytes 196640 | tf_op jit(solution)/shard_map/ppermute | solution.py:461
  68.8 0.0 collective-permute-done.10.spare
  68.8 0.7 shard_map.74
  69.5 23.7 %all_to_all.21.arrived = bf16[32,24,512]{2,1,0:T(8,128)(2,1)S(1)} all-to-all(bf16[32,24,512]{2,1,0:T(8,128)(2,1)S(1)} %bitcast.6), channel_id=1, replica_groups=mesh['read'=32,'pos'=1] {'read'}, dimensions={0} | all-to-all | bytes 1572864 | tf_op jit(solution)/shard_map/all_to_all | solution.py:422
  93.2 1.3 %shard_map.75 = (bf16[4,32,768]{2,1,0:T(8,128)(2,1)}, f32[24,3072]{1,0:T(8,128)}) custom-call(bf16[32,24,512]{2,1,0:T(8,128)(2,1)S(1)} %all_to_all.21.arrived), custom_call_target="tpu_custom_call" | custom-call | tf_op jit(solution)/shard_map/pallas_call | solution.py:433
  (2 shorter events, 0.0 us)
Async XLA Ops:
  22.8 2.0 %collective-permute-start = (bf16[256,768]{1,0:T(8,128)(2,1)S(1)}, bf16[256,768]{1,0:T(8,128)(2,1)S(1)}, u32[]{:S(2)}, u32[]{:S(2)}) collective-permute-start(bf16[256,768]{1,0:T(8,128)(2,1)S(1)} %bitcast.7), channel_id=1, source_target_pairs={{0,1},{1,0},{2,3},{3,2},{4,5},{5,4},{6,7},{7,6},{8,9},{9,8},{10,11... | collective-permute-start | bytes 1179656 | tf_op jit(solution)/shard_map/ppermute | solution.py:461
  22.8 11.9 %collective-permute-start.1 = (bf16[256,768]{1,0:T(8,128)(2,1)S(1)}, bf16[256,768]{1,0:T(8,128)(2,1)S(1)}, u32[]{:S(2)}, u32[]{:S(2)}) collective-permute-start(bf16[256,768]{1,0:T(8,128)(2,1)S(1)} %bitcast.8), channel_id=1, source_target_pairs={{0,2},{1,3},{2,0},{3,1},{4,6},{5,7},{6,4},{7,5},{8,10},{9,11},{10,... | collective-permute-start | bytes 1179656 | tf_op jit(solution)/shard_map/ppermute | solution.py:461
  23.8 12.6 %collective-permute-start.3 = (bf16[256,768]{1,0:T(8,128)(2,1)S(1)}, bf16[256,768]{1,0:T(8,128)(2,1)S(1)}, u32[]{:S(2)}, u32[]{:S(2)}) collective-permute-start(bf16[256,768]{1,0:T(8,128)(2,1)S(1)} %bitcast.9), channel_id=1, source_target_pairs={{0,4},{1,5},{2,6},{3,7},{4,0},{5,1},{6,2},{7,3},{8,12},{9,13},{10,... | collective-permute-start | bytes 1179656 | tf_op jit(solution)/shard_map/ppermute | solution.py:461
  27.2 18.3 %all-to-all-start.1 = ((f16[16,96,128]{2,1,0:T(8,128)(2,1)}), f16[16,96,128]{2,1,0:T(8,128)(2,1)S(1)}, u32[]{:S(2)}, u32[]{:S(2)}) async-start(f16[16,96,128]{2,1,0:T(8,128)(2,1)} %convert_element_type.6), calls=%async_computation.1 | async-start | bytes 786432 | tf_op jit(solution)/shard_map/all_to_all | solution.py:422
  34.7 1.1 %copy-start.1 = (bf16[256,768]{1,0:T(8,128)(2,1)}, bf16[256,768]{1,0:T(8,128)(2,1)S(1)}, u32[]{:S(2)}) copy-start(bf16[256,768]{1,0:T(8,128)(2,1)S(1)} %collective-permute-done.1.rows.refs_2_) | copy-start | bytes 1179652
  34.7 8.1 %collective-permute-start.5 = (bf16[128,768]{1,0:T(8,128)(2,1)S(1)}, bf16[128,768]{1,0:T(8,128)(2,1)S(1)}, u32[]{:S(2)}, u32[]{:S(2)}) collective-permute-start(bf16[128,768]{1,0:T(8,128)(2,1)S(1)} %shard_map.71), channel_id=1, source_target_pairs={{0,4},{1,5},{2,6},{3,7},{4,0},{5,1},{6,2},{7,3},{8,12},{9,13},{10,... | collective-permute-start | bytes 589832 | tf_op jit(solution)/shard_map/ppermute | solution.py:461
  35.8 14.3 %collective-permute-start.2 = (bf16[256,768]{1,0:T(8,128)(2,1)S(1)}, bf16[256,768]{1,0:T(8,128)(2,1)}, u32[]{:S(2)}, u32[]{:S(2)}) collective-permute-start(bf16[256,768]{1,0:T(8,128)(2,1)S(1)} %collective-permute-done.1.rows.refs_2_), channel_id=1, source_target_pairs={{0,1},{1,0},{2,3},{3,2},{4,5},{5,4},{6,7},{7,6},{8,9},{9,8},{10,11... | collective-permute-start | bytes 1179656 | tf_op jit(solution)/shard_map/ppermute | solution.py:461
  36.4 13.7 %collective-permute-start.4 = (bf16[256,768]{1,0:T(8,128)(2,1)S(1)}, bf16[256,768]{1,0:T(8,128)(2,1)}, u32[]{:S(2)}, u32[]{:S(2)}) collective-permute-start(bf16[256,768]{1,0:T(8,128)(2,1)S(1)} %collective-permute-done.3.refs_4_), channel_id=1, source_target_pairs={{0,1},{1,0},{2,3},{3,2},{4,5},{5,4},{6,7},{7,6},{8,9},{9,8},{10,11... | collective-permute-start | bytes 1179656 | tf_op jit(solution)/shard_map/ppermute | solution.py:461
  36.4 9.1 %collective-permute-start.6 = (bf16[128,768]{1,0:T(8,128)(2,1)S(1)}, bf16[128,768]{1,0:T(8,128)(2,1)}, u32[]{:S(2)}, u32[]{:S(2)}) collective-permute-start(bf16[128,768]{1,0:T(8,128)(2,1)S(1)} %slice.4), channel_id=1, source_target_pairs={{0,2},{1,3},{2,0},{3,1},{4,6},{5,7},{6,4},{7,5},{8,10},{9,11},{10,... | collective-permute-start | bytes 589832 | tf_op jit(solution)/shard_map/ppermute | solution.py:461
  42.8 7.3 %copy-start.3 = (bf16[128,768]{1,0:T(8,128)(2,1)}, bf16[128,768]{1,0:T(8,128)(2,1)S(1)}, u32[]{:S(2)}) copy-start(bf16[128,768]{1,0:T(8,128)(2,1)S(1)} %collective-permute-done.5.refs_6_) | copy-start | bytes 589828
  42.8 7.3 %collective-permute-start.7 = (bf16[128,768]{1,0:T(8,128)(2,1)S(1)}, bf16[128,768]{1,0:T(8,128)(2,1)}, u32[]{:S(2)}, u32[]{:S(2)}) collective-permute-start(bf16[128,768]{1,0:T(8,128)(2,1)S(1)} %collective-permute-done.5.refs_6_), channel_id=1, source_target_pairs={{0,1},{1,0},{2,3},{3,2},{4,5},{5,4},{6,7},{7,6},{8,9},{9,8},{10,11... | collective-permute-start | bytes 589832 | tf_op jit(solution)/shard_map/ppermute | solution.py:461
  45.5 4.6 %collective-permute-start.8 = (bf16[128,768]{1,0:T(8,128)(2,1)}, bf16[128,768]{1,0:T(8,128)(2,1)}, u32[]{:S(2)}, u32[]{:S(2)}) collective-permute-start(bf16[128,768]{1,0:T(8,128)(2,1)} %collective-permute-done.6.refs_7_), channel_id=1, source_target_pairs={{0,1},{1,0},{2,3},{3,2},{4,5},{5,4},{6,7},{7,6},{8,9},{9,8},{10,11... | collective-permute-start | bytes 589832 | tf_op jit(solution)/shard_map/ppermute | solution.py:461
  46.5 16.4 %all-to-all-start.2 = ((bf16[16,96,128]{2,1,0:T(8,128)(2,1)}), bf16[16,96,128]{2,1,0:T(8,128)(2,1)S(1)}, u32[]{:S(2)}, u32[]{:S(2)}) async-start(bf16[16,96,128]{2,1,0:T(8,128)(2,1)} %shard_map.70), calls=%async_computation.2 | async-start | bytes 786432 | tf_op jit(solution)/shard_map/all_to_all | solution.py:422
  50.1 1.0 %copy-start.2 = (bf16[256,768]{1,0:T(8,128)(2,1)S(1)}, bf16[256,768]{1,0:T(8,128)(2,1)}, u32[]{:S(2)}) copy-start(bf16[256,768]{1,0:T(8,128)(2,1)} %copy-done.1) | copy-start | bytes 1179652
  51.1 0.9 copy-start.4
  56.8 1.2 %copy-start = (bf16[1024,768]{1,0:T(8,128)(2,1)}, bf16[1024,768]{1,0:T(8,128)(2,1)S(1)}, u32[]{:S(2)}) copy-start(bf16[1024,768]{1,0:T(8,128)(2,1)S(1)} %get-tuple-element.24.left_far) | copy-start | bytes 4718596
  66.9 1.9 %collective-permute-start.10 = (bf16[384,384]{1,0:T(8,128)(2,1)S(1)}, bf16[384,384]{1,0:T(8,128)(2,1)S(1)}, u32[]{:S(2)}, u32[]{:S(2)}) collective-permute-start(bf16[384,384]{1,0:T(8,128)(2,1)S(1)} %get-tuple-element.29), channel_id=1, source_target_pairs={{0,1},{1,0},{2,3},{3,2},{4,5},{5,4},{6,7},{7,6},{8,9},{9,8},{10,11... | collective-permute-start | bytes 884744 | tf_op jit(solution)/shard_map/ppermute | solution.py:461
  67.0 1.9 %collective-permute-start.9 = (bf16[128,768]{1,0:T(8,128)(2,1)S(1)}, bf16[128,768]{1,0:T(8,128)(2,1)S(1)}, u32[]{:S(2)}, u32[]{:S(2)}) collective-permute-start(bf16[128,768]{1,0:T(8,128)(2,1)S(1)} %get-tuple-element.26), channel_id=1, source_target_pairs={{0,1},{1,0},{2,3},{3,2},{4,5},{5,4},{6,7},{7,6},{8,9},{9,8},{10,11... | collective-permute-start | bytes 589832 | tf_op jit(solution)/shard_map/ppermute | solution.py:461

commit v11 on v9

--- a/solution.py
+++ b/solution.py
@@ -543,7 +543,8 @@
         ],
     )
     grad_recv = swap(grad_other, 1)
-    spare = swap(spare, 1)
+    last = [i for i in range(count) if i // CORES % KINDS == KINDS - 1]
+    spare = lax.ppermute(spare, "read", [(i, i ^ 1) for i in last])
     payload = call(
         functools.partial(pack_kernel, rows=rows),
         (grad_own, grad_recv, normed, bounds, product, spare),

time: 95 us -> 96.8 us (1.019)
  blocking collectives: 43.9 us -> 45.4 us
    all_to_all x2, blocking collectives: 43.9 us -> 45.4 us  [exchange(): lax.all_to_all(array, 'read', split_axis=0, concat_axis=0, tiled=True, ax...]
    ppermute x11 -> x10, starting transfers between devices: 5.78 us -> 5.29 us  [swap(): return lax.ppermute(array, 'read', [(i, i ^ bits) for i in range(count)])]
    ppermute x11 -> x10, waiting for transfers between devices: 12.8 us -> 12.8 us  [swap(): return lax.ppermute(array, 'read', [(i, i ^ bits) for i in range(count)])]
where the time goes in v11:
time: 96.8 us; the launch traced here: 96.2 us
  blocking collectives  45.4 us (47%)
  waiting for transfers between devices  17 us (18%)
  Pallas kernels  15.2 us (16%)
  starting transfers between devices  13.1 us (14%)
  local copies, waits for them, and re-layouts  3.94 us (4%)
    all_to_all x2, blocking collectives, exchange(): lax.all_to_all(array, 'read', split_axis=0, concat_axis=0, tiled=True, ax...  45.4 us
    pallas_call x7, Pallas kernels, call(): pl.pallas_call(kernel, in_specs=[away if at in far else near for at in ra...  15.2 us
    ppermute x10, waiting for transfers between devices, swap(): return lax.ppermute(array, 'read', [(i, i ^ bits) for i in range(count)])  12.8 us
    all_to_all x2, starting transfers between devices, exchange(): lax.all_to_all(array, 'read', split_axis=0, concat_axis=0, tiled=True, ax...  7.1 us
    ppermute x10, starting transfers between devices, swap(): return lax.ppermute(array, 'read', [(i, i ^ bits) for i in range(count)])  5.29 us
    all_to_all x2, waiting for transfers between devices, exchange(): lax.all_to_all(array, 'read', split_axis=0, concat_axis=0, tiled=True, ax...  4.13 us
    unnamed x10, local copies, waits for them, and re-layouts  3.91 us
  transfers between devices with their start and end apart: 13, of which 6 were waited for; matrix products, arithmetic and copies ran while one was open for 1% of the time, Pallas kernels for 8%

profile of v11, /device:TPU:0, one launch (start us, length us, event | category | flops | bytes accessed | tf_op | source)
XLA Modules:
  0.0 96.2 jit_solution(3030066088824089806)
XLA Ops:
  0.6 1.9 %shard_map.68 = (bf16[256,768]{1,0:T(8,128)(2,1)S(1)}, bf16[3,768,384]{2,1,0:T(8,128)(2,1)S(1)}, bf16[384,768]{1,0:T(8,128)(2,1)S(1)}, f32[128,128]{1,0:T(8,128)S(1)}) custom-call(bf16[4,32,768]{2,1,0:T(8,128)(2,1)} %features.1, bf16[4,32,768]{2,1,0:T(8,128)(2,1)} %grad_out.1, bf16[4,768,768]{2,1,0:T(8,128)(2,1)} %weights.5, s32[1,128]{1,0:T(1,128)} %bitcast.12, ...), custom_call_target="tpu_custom_call" | custom-call | tf_op jit(solution)/shard_map/pallas_call | solution.py:429
  2.5 20.3 %all_to_all.20 = bf16[32,8,768]{2,1,0:T(8,128)(2,1)S(1)} all-to-all(bf16[32,8,768]{2,1,0:T(8,128)(2,1)S(1)} %bitcast.11), channel_id=1, replica_groups=mesh['read'=32,'pos'=1] {'read'}, dimensions={0} | all-to-all | bytes 786432 | tf_op jit(solution)/shard_map/all_to_all | solution.py:418
  22.8 0.0 collective-permute-start
  22.8 1.0 %collective-permute-start.1 = (bf16[256,768]{1,0:T(8,128)(2,1)S(1)}, bf16[256,768]{1,0:T(8,128)(2,1)S(1)}, u32[]{:S(2)}, u32[]{:S(2)}) collective-permute-start(bf16[256,768]{1,0:T(8,128)(2,1)S(1)} %bitcast.7), channel_id=1, source_target_pairs={{0,2},{1,3},{2,0},{3,1},{4,6},{5,7},{6,4},{7,5},{8,10},{9,11},{10,... | collective-permute-start | bytes 1179656 | tf_op jit(solution)/shard_map/ppermute | solution.py:457
  23.8 1.0 %collective-permute-start.3 = (bf16[256,768]{1,0:T(8,128)(2,1)S(1)}, bf16[256,768]{1,0:T(8,128)(2,1)S(1)}, u32[]{:S(2)}, u32[]{:S(2)}) collective-permute-start(bf16[256,768]{1,0:T(8,128)(2,1)S(1)} %bitcast.8), channel_id=1, source_target_pairs={{0,4},{1,5},{2,6},{3,7},{4,0},{5,1},{6,2},{7,3},{8,12},{9,13},{10,... | collective-permute-start | bytes 1179656 | tf_op jit(solution)/shard_map/ppermute | solution.py:457
  24.8 0.0 collective-permute-done.other.refs_1_
  24.8 1.6 %shard_map.69 = (bf16[3,256,384]{2,1,0:T(8,128)(2,1)S(1)}, f32[16,96,128]{2,1,0:T(8,128)S(1)}, f32[128,768]{1,0:T(8,128)S(1)}, f32[128,128]{1,0:T(8,128)S(1)}) custom-call(bf16[256,768]{1,0:T(8,128)(2,1)S(1)} %bitcast.9, bf16[256,768]{1,0:T(8,128)(2,1)S(1)} %collective-permute-done.other.refs_1_, bf16[3,768,384]{2,1,0:T(8,128)(2,1)S(1)} %get-tuple-element.17.heads_in, ...), custom_call_target="tpu_custom_call" | custom-call | tf_op jit(solution)/shard_map/pallas_call | solution.py:429
  26.4 0.8 convert_element_type.6
  27.2 3.6 %all-to-all-start.1 = ((f16[16,96,128]{2,1,0:T(8,128)(2,1)}), f16[16,96,128]{2,1,0:T(8,128)(2,1)S(1)}, u32[]{:S(2)}, u32[]{:S(2)}) async-start(f16[16,96,128]{2,1,0:T(8,128)(2,1)} %convert_element_type.6), calls=%async_computation.1 | async-start | bytes 786432 | tf_op jit(solution)/shard_map/all_to_all | solution.py:418
  30.8 3.9 %collective-permute-done.1.refs_2_ = bf16[256,768]{1,0:T(8,128)(2,1)S(1)} collective-permute-done((bf16[256,768]{1,0:T(8,128)(2,1)S(1)}, bf16[256,768]{1,0:T(8,128)(2,1)S(1)}, u32[]{:S(2)}, u32[]{:S(2)}) %collective-permute-start.1) | collective-permute-done | bytes 393248 | tf_op jit(solution)/shard_map/ppermute | solution.py:457
  34.7 1.1 %collective-permute-start.5 = (bf16[128,768]{1,0:T(8,128)(2,1)S(1)}, bf16[128,768]{1,0:T(8,128)(2,1)}, u32[]{:S(2)}, u32[]{:S(2)}) collective-permute-start(bf16[128,768]{1,0:T(8,128)(2,1)S(1)} %slice.8), channel_id=1, source_target_pairs={{0,4},{1,5},{2,6},{3,7},{4,0},{5,1},{6,2},{7,3},{8,12},{9,13},{10,... | collective-permute-start | bytes 589832 | tf_op jit(solution)/shard_map/ppermute | solution.py:457
  35.8 0.0 collective-permute-start.2
  35.8 0.6 collective-permute-done.3.refs_4_
  36.4 0.0 copy-start.1
  36.4 0.0 collective-permute-start.4
  36.4 2.2 %collective-permute-start.6 = (bf16[128,768]{1,0:T(8,128)(2,1)S(1)}, bf16[128,768]{1,0:T(8,128)(2,1)}, u32[]{:S(2)}, u32[]{:S(2)}) collective-permute-start(bf16[128,768]{1,0:T(8,128)(2,1)S(1)} %slice.9), channel_id=1, source_target_pairs={{0,2},{1,3},{2,0},{3,1},{4,6},{5,7},{6,4},{7,5},{8,10},{9,11},{10,... | collective-permute-start | bytes 589832 | tf_op jit(solution)/shard_map/ppermute | solution.py:457
  38.6 4.3 %collective-permute-done.5.refs_6_ = bf16[128,768]{1,0:T(8,128)(2,1)} collective-permute-done((bf16[128,768]{1,0:T(8,128)(2,1)S(1)}, bf16[128,768]{1,0:T(8,128)(2,1)}, u32[]{:S(2)}, u32[]{:S(2)}) %collective-permute-start.5) | collective-permute-done | bytes 196640 | tf_op jit(solution)/shard_map/ppermute | solution.py:457
  42.9 0.0 collective-permute-start.7
  42.9 2.6 %collective-permute-done.6.refs_7_ = bf16[128,768]{1,0:T(8,128)(2,1)} collective-permute-done((bf16[128,768]{1,0:T(8,128)(2,1)S(1)}, bf16[128,768]{1,0:T(8,128)(2,1)}, u32[]{:S(2)}, u32[]{:S(2)}) %collective-permute-start.6) | collective-permute-done | bytes 196640 | tf_op jit(solution)/shard_map/ppermute | solution.py:457
  45.5 0.0 collective-permute-start.8
  45.5 0.0 all-to-all-done.1
  45.5 0.1 convert_element_type.7.parts
  45.6 1.0 %shard_map.70 = bf16[16,96,128]{2,1,0:T(8,128)(2,1)} custom-call(f32[16,96,128]{2,1,0:T(8,128)S(1)} %convert_element_type.7.parts), custom_call_target="tpu_custom_call" | custom-call | tf_op jit(solution)/shard_map/pallas_call | solution.py:429
  46.5 0.0 copy-done.1
  46.5 3.6 %all-to-all-start.2 = ((bf16[16,96,128]{2,1,0:T(8,128)(2,1)}), bf16[16,96,128]{2,1,0:T(8,128)(2,1)S(1)}, u32[]{:S(2)}, u32[]{:S(2)}) async-start(bf16[16,96,128]{2,1,0:T(8,128)(2,1)} %shard_map.70), calls=%async_computation.2 | async-start | bytes 786432 | tf_op jit(solution)/shard_map/all_to_all | solution.py:418
  50.1 0.0 collective-permute-done.2.refs_3_
  50.1 0.0 copy-start.3
  50.1 0.8 copy-done.3
  50.9 0.0 collective-permute-done.4.refs_5_
  50.9 0.0 collective-permute-done.7.refs_8_
  50.9 0.0 collective-permute-done.8.refs_9_
  50.9 0.0 copy-start.2
  50.9 1.0 %copy-done.2 = bf16[256,768]{1,0:T(8,128)(2,1)S(1)} copy-done((bf16[256,768]{1,0:T(8,128)(2,1)S(1)}, bf16[256,768]{1,0:T(8,128)(2,1)}, u32[]{:S(2)}) %copy-start.2) | copy-done | bytes 393240
  51.9 0.0 copy-start.4
  51.9 1.0 %copy-done.4 = bf16[256,768]{1,0:T(8,128)(2,1)S(1)} copy-done((bf16[256,768]{1,0:T(8,128)(2,1)S(1)}, bf16[256,768]{1,0:T(8,128)(2,1)}, u32[]{:S(2)}) %copy-start.4) | copy-done | bytes 393240
  52.9 4.7 %shard_map.71 = (bf16[1024,768]{1,0:T(8,128)(2,1)S(1)}, bf16[1024,384]{1,0:T(8,128)(2,1)S(1)}) custom-call(bf16[4,768,768]{2,1,0:T(8,128)(2,1)} %weights.5, f32[128,128]{1,0:T(8,128)S(1)} %get-tuple-element.22.bounds, bf16[256,768]{1,0:T(8,128)(2,1)S(1)} %bitcast.10, bf16[256,768]{1,0:T(8,128)(2,1)S(1)} %collective-permute-done.other.refs_1_, ...), custom_call_target="tpu_custom_call" | custom-call | flops 40000000000 | bytes 8388608 | tf_op jit(solution)/shard_map/pallas_call | solution.py:429
  57.6 0.0 copy-start
  57.6 1.2 %copy-done = bf16[1024,768]{1,0:T(8,128)(2,1)} copy-done((bf16[1024,768]{1,0:T(8,128)(2,1)}, bf16[1024,768]{1,0:T(8,128)(2,1)S(1)}, u32[]{:S(2)}) %copy-start) | copy-done | bytes 1572888
  58.8 4.1 %all-to-all-done.2.pairs = bf16[16,96,128]{2,1,0:T(8,128)(2,1)S(1)} async-done(((bf16[16,96,128]{2,1,0:T(8,128)(2,1)}), bf16[16,96,128]{2,1,0:T(8,128)(2,1)S(1)}, u32[]{:S(2)}, u32[]{:S(2)}) %all-to-all-start.2) | async-done | bytes 393248 | tf_op jit(solution)/shard_map/all_to_all | solution.py:418
  62.9 4.0 %shard_map.72 = (f32[128,768]{1,0:T(8,128)S(1)}, bf16[128,768]{1,0:T(8,128)(2,1)S(1)}, bf16[768,384]{1,0:T(8,128)(2,1)S(1)}, bf16[384,384]{1,0:T(8,128)(2,1)S(1)}) custom-call(bf16[16,96,128]{2,1,0:T(8,128)(2,1)S(1)} %all-to-all-done.2.pairs, bf16[3,256,384]{2,1,0:T(8,128)(2,1)S(1)} %get-tuple-element.21.proj, f32[128,128]{1,0:T(8,128)S(1)} %get-tuple-element.22.bounds, ...), custom_call_target="tpu_custom_call" | custom-call | tf_op jit(solution)/shard_map/pallas_call | solution.py:429
  66.9 0.7 collective-permute-start.10
  67.6 0.1 collective-permute-start.9
  67.7 1.4 %collective-permute-done.9.grad_recv = bf16[128,768]{1,0:T(8,128)(2,1)S(1)} collective-permute-done((bf16[128,768]{1,0:T(8,128)(2,1)S(1)}, bf16[128,768]{1,0:T(8,128)(2,1)S(1)}, u32[]{:S(2)}, u32[]{:S(2)}) %collective-permute-start.9) | collective-permute-done | bytes 196640 | tf_op jit(solution)/shard_map/ppermute | solution.py:457
  69.1 0.0 collective-permute-done.10.spare
  69.1 0.7 shard_map.73
  69.8 25.1 %all_to_all.21.arrived = bf16[32,24,512]{2,1,0:T(8,128)(2,1)S(1)} all-to-all(bf16[32,24,512]{2,1,0:T(8,128)(2,1)S(1)} %bitcast.5), channel_id=1, replica_groups=mesh['read'=32,'pos'=1] {'read'}, dimensions={0} | all-to-all | bytes 1572864 | tf_op jit(solution)/shard_map/all_to_all | solution.py:418
  94.9 1.3 %shard_map.74 = (bf16[4,32,768]{2,1,0:T(8,128)(2,1)}, f32[24,3072]{1,0:T(8,128)}) custom-call(bf16[32,24,512]{2,1,0:T(8,128)(2,1)S(1)} %all_to_all.21.arrived), custom_call_target="tpu_custom_call" | custom-call | tf_op jit(solution)/shard_map/pallas_call | solution.py:429
  (2 shorter events, 0.0 us)
Async XLA Ops:
  22.8 2.0 %collective-permute-start = (bf16[256,768]{1,0:T(8,128)(2,1)S(1)}, bf16[256,768]{1,0:T(8,128)(2,1)S(1)}, u32[]{:S(2)}, u32[]{:S(2)}) collective-permute-start(bf16[256,768]{1,0:T(8,128)(2,1)S(1)} %bitcast.6), channel_id=1, source_target_pairs={{0,1},{1,0},{2,3},{3,2},{4,5},{5,4},{6,7},{7,6},{8,9},{9,8},{10,11... | collective-permute-start | bytes 1179656 | tf_op jit(solution)/shard_map/ppermute | solution.py:457
  22.8 11.9 %collective-permute-start.1 = (bf16[256,768]{1,0:T(8,128)(2,1)S(1)}, bf16[256,768]{1,0:T(8,128)(2,1)S(1)}, u32[]{:S(2)}, u32[]{:S(2)}) collective-permute-start(bf16[256,768]{1,0:T(8,128)(2,1)S(1)} %bitcast.7), channel_id=1, source_target_pairs={{0,2},{1,3},{2,0},{3,1},{4,6},{5,7},{6,4},{7,5},{8,10},{9,11},{10,... | collective-permute-start | bytes 1179656 | tf_op jit(solution)/shard_map/ppermute | solution.py:457
  23.8 12.6 %collective-permute-start.3 = (bf16[256,768]{1,0:T(8,128)(2,1)S(1)}, bf16[256,768]{1,0:T(8,128)(2,1)S(1)}, u32[]{:S(2)}, u32[]{:S(2)}) collective-permute-start(bf16[256,768]{1,0:T(8,128)(2,1)S(1)} %bitcast.8), channel_id=1, source_target_pairs={{0,4},{1,5},{2,6},{3,7},{4,0},{5,1},{6,2},{7,3},{8,12},{9,13},{10,... | collective-permute-start | bytes 1179656 | tf_op jit(solution)/shard_map/ppermute | solution.py:457
  27.2 18.2 %all-to-all-start.1 = ((f16[16,96,128]{2,1,0:T(8,128)(2,1)}), f16[16,96,128]{2,1,0:T(8,128)(2,1)S(1)}, u32[]{:S(2)}, u32[]{:S(2)}) async-start(f16[16,96,128]{2,1,0:T(8,128)(2,1)} %convert_element_type.6), calls=%async_computation.1 | async-start | bytes 786432 | tf_op jit(solution)/shard_map/all_to_all | solution.py:418
  34.7 8.2 %collective-permute-start.5 = (bf16[128,768]{1,0:T(8,128)(2,1)S(1)}, bf16[128,768]{1,0:T(8,128)(2,1)}, u32[]{:S(2)}, u32[]{:S(2)}) collective-permute-start(bf16[128,768]{1,0:T(8,128)(2,1)S(1)} %slice.8), channel_id=1, source_target_pairs={{0,4},{1,5},{2,6},{3,7},{4,0},{5,1},{6,2},{7,3},{8,12},{9,13},{10,... | collective-permute-start | bytes 589832 | tf_op jit(solution)/shard_map/ppermute | solution.py:457
  35.8 14.3 %collective-permute-start.2 = (bf16[256,768]{1,0:T(8,128)(2,1)S(1)}, bf16[256,768]{1,0:T(8,128)(2,1)S(1)}, u32[]{:S(2)}, u32[]{:S(2)}) collective-permute-start(bf16[256,768]{1,0:T(8,128)(2,1)S(1)} %collective-permute-done.1.refs_2_), channel_id=1, source_target_pairs={{0,1},{1,0},{2,3},{3,2},{4,5},{5,4},{6,7},{7,6},{8,9},{9,8},{10,11... | collective-permute-start | bytes 1179656 | tf_op jit(solution)/shard_map/ppermute | solution.py:457
  36.4 10.2 %copy-start.1 = (bf16[256,768]{1,0:T(8,128)(2,1)}, bf16[256,768]{1,0:T(8,128)(2,1)S(1)}, u32[]{:S(2)}) copy-start(bf16[256,768]{1,0:T(8,128)(2,1)S(1)} %collective-permute-done.3.refs_4_) | copy-start | bytes 1179652
  36.4 14.5 %collective-permute-start.4 = (bf16[256,768]{1,0:T(8,128)(2,1)S(1)}, bf16[256,768]{1,0:T(8,128)(2,1)}, u32[]{:S(2)}, u32[]{:S(2)}) collective-permute-start(bf16[256,768]{1,0:T(8,128)(2,1)S(1)} %collective-permute-done.3.refs_4_), channel_id=1, source_target_pairs={{0,1},{1,0},{2,3},{3,2},{4,5},{5,4},{6,7},{7,6},{8,9},{9,8},{10,11... | collective-permute-start | bytes 1179656 | tf_op jit(solution)/shard_map/ppermute | solution.py:457
  36.4 9.1 %collective-permute-start.6 = (bf16[128,768]{1,0:T(8,128)(2,1)S(1)}, bf16[128,768]{1,0:T(8,128)(2,1)}, u32[]{:S(2)}, u32[]{:S(2)}) collective-permute-start(bf16[128,768]{1,0:T(8,128)(2,1)S(1)} %slice.9), channel_id=1, source_target_pairs={{0,2},{1,3},{2,0},{3,1},{4,6},{5,7},{6,4},{7,5},{8,10},{9,11},{10,... | collective-permute-start | bytes 589832 | tf_op jit(solution)/shard_map/ppermute | solution.py:457
  42.9 8.0 %collective-permute-start.7 = (bf16[128,768]{1,0:T(8,128)(2,1)}, bf16[128,768]{1,0:T(8,128)(2,1)}, u32[]{:S(2)}, u32[]{:S(2)}) collective-permute-start(bf16[128,768]{1,0:T(8,128)(2,1)} %collective-permute-done.5.refs_6_), channel_id=1, source_target_pairs={{0,1},{1,0},{2,3},{3,2},{4,5},{5,4},{6,7},{7,6},{8,9},{9,8},{10,11... | collective-permute-start | bytes 589832 | tf_op jit(solution)/shard_map/ppermute | solution.py:457
  45.5 5.4 %collective-permute-start.8 = (bf16[128,768]{1,0:T(8,128)(2,1)}, bf16[128,768]{1,0:T(8,128)(2,1)}, u32[]{:S(2)}, u32[]{:S(2)}) collective-permute-start(bf16[128,768]{1,0:T(8,128)(2,1)} %collective-permute-done.6.refs_7_), channel_id=1, source_target_pairs={{0,1},{1,0},{2,3},{3,2},{4,5},{5,4},{6,7},{7,6},{8,9},{9,8},{10,11... | collective-permute-start | bytes 589832 | tf_op jit(solution)/shard_map/ppermute | solution.py:457
  46.5 16.4 %all-to-all-start.2 = ((bf16[16,96,128]{2,1,0:T(8,128)(2,1)}), bf16[16,96,128]{2,1,0:T(8,128)(2,1)S(1)}, u32[]{:S(2)}, u32[]{:S(2)}) async-start(bf16[16,96,128]{2,1,0:T(8,128)(2,1)} %shard_map.70), calls=%async_computation.2 | async-start | bytes 786432 | tf_op jit(solution)/shard_map/all_to_all | solution.py:418
  50.1 0.8 copy-start.3
  50.9 1.0 %copy-start.2 = (bf16[256,768]{1,0:T(8,128)(2,1)S(1)}, bf16[256,768]{1,0:T(8,128)(2,1)}, u32[]{:S(2)}) copy-start(bf16[256,768]{1,0:T(8,128)(2,1)} %copy-done.1) | copy-start | bytes 1179652
  51.9 1.0 %copy-start.4 = (bf16[256,768]{1,0:T(8,128)(2,1)S(1)}, bf16[256,768]{1,0:T(8,128)(2,1)}, u32[]{:S(2)}) copy-start(bf16[256,768]{1,0:T(8,128)(2,1)} %copy-done.3) | copy-start | bytes 1179652
  57.6 1.2 %copy-start = (bf16[1024,768]{1,0:T(8,128)(2,1)}, bf16[1024,768]{1,0:T(8,128)(2,1)S(1)}, u32[]{:S(2)}) copy-start(bf16[1024,768]{1,0:T(8,128)(2,1)S(1)} %get-tuple-element.24.left_far) | copy-start | bytes 4718596
  66.9 2.2 %collective-permute-start.10 = (bf16[384,384]{1,0:T(8,128)(2,1)S(1)}, bf16[384,384]{1,0:T(8,128)(2,1)S(1)}, u32[]{:S(2)}, u32[]{:S(2)}) collective-permute-start(bf16[384,384]{1,0:T(8,128)(2,1)S(1)} %get-tuple-element.29), channel_id=1, source_target_pairs={{6,7},{7,6},{14,15},{15,14},{22,23},{23,22},{30,31},{31,30}} | collective-permute-start | bytes 884744 | tf_op jit(solution)/shard_map/ppermute | solution.py:547
  67.6 1.5 %collective-permute-start.9 = (bf16[128,768]{1,0:T(8,128)(2,1)S(1)}, bf16[128,768]{1,0:T(8,128)(2,1)S(1)}, u32[]{:S(2)}, u32[]{:S(2)}) collective-permute-start(bf16[128,768]{1,0:T(8,128)(2,1)S(1)} %get-tuple-element.26), channel_id=1, source_target_pairs={{0,1},{1,0},{2,3},{3,2},{4,5},{5,4},{6,7},{7,6},{8,9},{9,8},{10,11... | collective-permute-start | bytes 589832 | tf_op jit(solution)/shard_map/ppermute | solution.py:457
